TPU v7x, 32 devices: a whole 2x2x4 slice. The times are simulated.
32 devices in a mesh: group: 2 (over x), shard: 16 (over z, y, core).
Axes of the slice: x: 2, y: 2, z: 4, core: 2. Of those that a mesh axis runs over, the one named last changes fastest.
Arguments:
- replica_weights: bfloat16 [2, 16, 512, 2048], P('group', None, 'shard'), may hold values from -6 to 6
- anchor_slabs: float32 [16, 2, 512, 2048], P('shard', None, None, 'group'), may hold values from -6 to 6
- momentum_slabs: float32 [16, 2, 512, 2048], P('shard', None, None, 'group'), may hold values from -4 to 4
- slab_owner: int32 [16], replicated, may hold values from 0 to 15, as said below
- replica_embed: bfloat16 [2, 768, 512], P('group', 'shard'), may hold values from -6 to 6
- anchor_embed: float32 [768, 512], P('shard'), may hold values from -6 to 6
- momentum_embed: float32 [768, 512], P('shard'), may hold values from -4 to 4
- embed_basis: float32 [768, 64], P('shard'), may hold values from -0.21875 to 0.21875
Outputs:
- new_anchor_slabs: float32 [16, 2, 512, 2048], P('shard', None, None, 'group')
- new_momentum_slabs: float32 [16, 2, 512, 2048], P('shard', None, None, 'group')
- new_weights: bfloat16 [2, 16, 512, 2048], P('group', None, 'shard')
- new_anchor_embed: float32 [768, 512], P('shard')
- new_momentum_embed: float32 [768, 512], P('shard')
- new_embed_weights: bfloat16 [2, 768, 512], P('group', 'shard')
Inputs may be any that keep to these rules, and one draw needn't show every extreme that they name: `slab_owner`: of the devices of shard, a quarter own 2 matrices each, half own 1 each and a quarter own none.
All inputs are finite; a program needn't handle non-finite values.
Results may differ from a plain program's by a relative error of at most 0.008.
Values may be sent and summed in bfloat16 or wider, within the bound.
No kernel may reach another device: no remote copies, remote signals or barrier semaphores. Data moves between devices by JAX's collectives and lax.ppermute only.
A program may use at most 128 MiB of HBM per device.

v0:
```python
import jax
import jax.numpy as jnp
from jax import lax
from jax.sharding import PartitionSpec as P

OUTER_RATE = 0.7
MOMENTUM_COEF = 0.9


def slot_tables(slab_owner, devices, capacity):
    slab_count = slab_owner.shape[0]
    order_ids = jnp.arange(slab_count, dtype=jnp.int32)
    same_owner = slab_owner[:, None] == slab_owner[None, :]
    earlier = order_ids[None, :] < order_ids[:, None]
    slot_index = jnp.sum((same_owner & earlier).astype(jnp.int32), axis=1)
    matches = (slab_owner[:, None, None] == jnp.arange(devices, dtype=jnp.int32)[None, :, None]) & (
        slot_index[:, None, None] == jnp.arange(capacity, dtype=jnp.int32)[None, None, :]
    )
    slab_of = jnp.sum(jnp.where(matches, order_ids[:, None, None], 0), axis=0)
    slot_used = jnp.any(matches, axis=0)
    return (slot_index, slab_of, slot_used)


def nesterov(anchor_value, moment, mean_value):
    outer_grad = anchor_value - mean_value
    new_moment = MOMENTUM_COEF * moment + outer_grad
    new_anchor = anchor_value - OUTER_RATE * (outer_grad + MOMENTUM_COEF * new_moment)
    return (new_anchor, new_moment)


def on_device(
    replica_weights,
    anchor_slabs,
    momentum_slabs,
    slab_owner,
    replica_embed,
    anchor_embed,
    momentum_embed,
    embed_basis,
):
    local_rows = replica_weights[0]
    row_count = local_rows.shape[1]
    width = local_rows.shape[2]
    devices = lax.axis_size("shard")
    n_group = lax.axis_size("group")
    capacity = anchor_slabs.shape[1]
    slot_index, slab_of, slot_used = slot_tables(slab_owner, devices, capacity)
    send_ids = slab_of.T.reshape(-1)
    send_used = slot_used.T
    back_ids = slot_index * devices + slab_owner
    owner_here = lax.axis_index("shard")
    my_used = lax.dynamic_index_in_dim(slot_used, owner_here, 0, keepdims=False)
    anchor_here = anchor_slabs[0]
    moment_here = momentum_slabs[0]
    picked = jnp.take(local_rows, send_ids, axis=0)
    picked = picked.reshape(capacity, devices, local_rows.shape[1], local_rows.shape[2])
    received = lax.all_to_all(
        jnp.where(send_used[:, :, None, None], picked, jnp.zeros((), local_rows.dtype)),
        "shard",
        split_axis=1,
        concat_axis=1,
        tiled=True,
    )
    gathered = received.reshape(capacity, devices * received.shape[2], received.shape[3])
    summed = lax.psum_scatter(
        gathered.astype(jnp.float32).astype(jnp.bfloat16), "group", scatter_dimension=2, tiled=True
    ).astype(jnp.float32)
    new_anchor, new_moment = nesterov(anchor_here, moment_here, summed / n_group)
    keep = my_used[:, None, None]
    new_anchor = jnp.where(keep, new_anchor, anchor_here)
    new_moment = jnp.where(keep, new_moment, moment_here)
    new_half = new_anchor.astype(jnp.bfloat16)
    full_cols = lax.all_gather(new_half, "group", axis=2, tiled=True)
    split_rows = full_cols.reshape(capacity, devices, row_count, width)
    received = lax.all_to_all(split_rows, "shard", split_axis=1, concat_axis=1, tiled=True)
    flat_rows = received.reshape(capacity * devices, received.shape[2], received.shape[3])
    new_rows = jnp.take(flat_rows, back_ids, axis=0)
    embed_here = replica_embed[0].astype(jnp.float32)
    partial_factor = jnp.dot(
        embed_basis.T,
        anchor_embed / n_group - embed_here / n_group,
        precision=lax.Precision.HIGHEST,
    )
    embed_factor = lax.psum(partial_factor, ("group", "shard"))
    embed_grad = jnp.dot(embed_basis, embed_factor, precision=lax.Precision.HIGHEST)
    new_anchor_embed, new_momentum_embed = nesterov(
        anchor_embed, momentum_embed, anchor_embed - embed_grad
    )
    new_embed_rows = new_anchor_embed.astype(jnp.bfloat16)
    return (
        new_anchor[None],
        new_moment[None],
        new_rows[None],
        new_anchor_embed,
        new_momentum_embed,
        new_embed_rows[None],
    )


def solution(mesh):
    in_specs = (
        P("group", None, "shard", None),
        P("shard", None, None, "group"),
        P("shard", None, None, "group"),
        P(),
        P("group", "shard", None),
        P("shard", None),
        P("shard", None),
        P("shard", None),
    )
    out_specs = (
        P("shard", None, None, "group"),
        P("shard", None, None, "group"),
        P("group", None, "shard", None),
        P("shard", None),
        P("shard", None),
        P("group", "shard", None),
    )
    return jax.shard_map(
        on_device, mesh=mesh, in_specs=in_specs, out_specs=out_specs, check_vma=False
    )
```

profile of v0, /device:TPU:0, one launch (start us, length us, event | category | flops | bytes accessed | tf_op | source)
XLA Modules:
  0.0 449.0 jit_solution(755700197703524414)
XLA Ops:
  8.0 0.0 copy-start
  8.0 0.0 reduce-scatter.2.cloned.1.call-start
  8.1 1.0 convert_reduce_fusion
  9.1 0.7 iota_compare_fusion.1
  9.8 0.1 fusion.9
  9.9 0.1 and_reduce_fusion
  10.0 0.1 reshape.127
  10.1 0.0 copy-done
  10.1 2.8 gather_fusion
  12.9 2.7 select_select_fusion
  15.6 0.6 copy.21
  16.2 99.4 %all_to_all.10 = bf16[2,16,32,2048]{3,2,0,1:T(8,128)(2,1)S(1)} all-to-all(bf16[2,16,32,2048]{3,2,0,1:T(8,128)(2,1)S(1)} %copy.21), channel_id=1, replica_groups=mesh['group'=2,'shard'=16] {'shard'}, dimensions={1} | all-to-all | bytes 8388608 | tf_op jit(solution)/shard_map/all_to_all | solution.py:57
  115.7 2.3 copy.22
  118.0 0.0 reduce-scatter.2.cloned.1.call-update
  118.0 0.0 all-gather.2.cloned.1.call-start
  118.1 0.2 dynamic-slice_reduce_fusion
  118.3 54.8 %reduce-scatter.2.cloned.1.call-done = bf16[2,512,1024]{2,1,0:T(8,128)(2,1)} async-done(((bf16[2,512,2048]{2,1,0:T(8,128)(2,1)}), bf16[2,512,1024]{2,1,0:T(8,128)(2,1)}) %reduce-scatter.2.cloned.1.call-update) | async-done | bytes 2097168 | tf_op jit(solution)/shard_map/reduce_scatter | solution.py:65
  173.1 9.8 %fusion.13 = (bf16[2,512,1024]{2,1,0:T(8,128)(2,1)}, f32[1,2,512,1024]{3,2,1,0:T(8,128)}, f32[1,2,512,1024]{3,2,1,0:T(8,128)}) fusion(f32[1,2,512,1024]{3,2,1,0:T(8,128)} %param.10, bf16[2,512,1024]{2,1,0:T(8,128)(2,1)} %reduce-scatter.2.cloned.1.call-done, f32[1,2,512,1024]{3,2,1,0:T(8,128)} %param.9, pred[2]{0:T(512)(128)(4,1)S(1)} %dynamic-slice_reduce_fusion), kind=kLoop, calls=%fused_computation.41 | loop fusion | flops 12582912 | bytes 20971522 | tf_op jit(solution)/shard_map/convert_element_type | solution.py:72
  182.9 0.0 all-gather.2.cloned.1.call-update
  182.9 56.9 %all-gather.2.cloned.1.call-done = bf16[2,512,2048]{2,1,0:T(8,128)(2,1)} async-done(((bf16[2,512,1024]{2,1,0:T(8,128)(2,1)}), bf16[2,512,2048]{2,1,0:T(8,128)(2,1)}) %all-gather.2.cloned.1.call-update) | async-done | bytes 4194320 | tf_op jit(solution)/shard_map/all_gather | solution.py:73
  239.8 4.7 %copy.23 = bf16[2,16,32,2048]{3,2,0,1:T(8,128)(2,1)} copy(bf16[2,16,32,2048]{3,2,1,0:T(8,128)(2,1)} %bitcast.68) | data formatting | bytes 8388608 | tf_op jit(solution)/shard_map/reshape | solution.py:74
  244.6 0.0 copy-start.1
  244.6 0.0 copy-start.2
  244.6 0.0 copy-start.4
  244.6 0.0 copy-start.5
  244.6 0.0 copy-start.3
  244.6 5.8 %all-to-all-start.1 = ((bf16[2,16,32,2048]{3,2,0,1:T(8,128)(2,1)}), bf16[2,16,32,2048]{3,2,0,1:T(8,128)(2,1)}, u32[]{:S(2)}, u32[]{:S(2)}) async-start(bf16[2,16,32,2048]{3,2,0,1:T(8,128)(2,1)} %copy.23), calls=%async_computation.2 | async-start | bytes 8388608 | tf_op jit(solution)/shard_map/all_to_all | solution.py:75
  250.4 0.0 all-reduce.2.cloned.1.call-start
  250.5 0.0 copy-done.1
  250.5 0.0 copy-done.2
  250.5 0.0 copy-done.4
  250.5 1.0 convolution_bitcast_fusion
  251.4 0.0 all-reduce.2.cloned.1.call-update
  251.5 0.0 copy-done.5
  251.5 176.1 %all-reduce.2.cloned.1.call-done = f32[64,512]{1,0:T(8,128)} async-done(((f32[64,512]{1,0:T(8,128)}), f32[64,512]{1,0:T(8,128)}) %all-reduce.2.cloned.1.call-update) | async-done | bytes 131088 | tf_op jit(solution)/shard_map/psum | solution.py:84
  427.6 0.0 copy-done.3
  427.6 1.9 convert_bitcast_fusion
  429.5 0.0 all-to-all-done.1
  429.5 4.7 %copy.24 = bf16[2,16,32,2048]{3,2,1,0:T(8,128)(2,1)} copy(bf16[2,16,32,2048]{3,2,0,1:T(8,128)(2,1)} %all-to-all-done.1) | data formatting | bytes 8388608 | tf_op jit(solution)/shard_map/all_to_all | solution.py:75
  434.2 4.2 gather_fusion.1
  438.4 3.2 bitcast_select_fusion.1
  (6 shorter events, 0.0 us)
Async XLA Ops:
  8.0 2.1 copy-start
  8.0 165.1 %reduce-scatter.2.cloned.1.call-start = ((), (), s32[]{:S(2)}) async-start(), calls=%async_computation.3 | async-start | bytes 6291456 | tf_op jit(solution)/shard_map/reduce_scatter | solution.py:65
  118.0 121.8 %all-gather.2.cloned.1.call-start = ((), (), s32[]{:S(2)}) async-start(), calls=%async_computation.4 | async-start | bytes 6291456 | tf_op jit(solution)/shard_map/all_gather | solution.py:73
  244.6 5.9 %copy-start.1 = (f32[48,512]{1,0:T(8,128)S(1)}, f32[48,512]{1,0:T(8,128)}, u32[]{:S(2)}) copy-start(f32[48,512]{1,0:T(8,128)} %param.13) | copy-start | bytes 294916
  244.6 5.9 %copy-start.2 = (f32[48,64]{1,0:T(8,128)S(1)}, f32[48,64]{1,0:T(8,128)}, u32[]{:S(2)}) copy-start(f32[48,64]{1,0:T(8,128)} %param.15) | copy-start | bytes 36868
  244.6 5.9 %copy-start.4 = (bf16[1,48,512]{2,1,0:T(8,128)(2,1)S(1)}, bf16[1,48,512]{2,1,0:T(8,128)(2,1)}, u32[]{:S(2)}) copy-start(bf16[1,48,512]{2,1,0:T(8,128)(2,1)} %param.12) | copy-start | bytes 147460
  244.6 6.9 %copy-start.5 = (s32[16]{0:T(128)S(1)}, s32[16]{0:T(128)}, u32[]{:S(2)}) copy-start(s32[16]{0:T(128)} %param.11) | copy-start | bytes 196
  244.6 183.1 %copy-start.3 = (f32[48,512]{1,0:T(8,128)S(1)}, f32[48,512]{1,0:T(8,128)}, u32[]{:S(2)}) copy-start(f32[48,512]{1,0:T(8,128)} %param.14) | copy-start | bytes 294916
  244.6 184.9 %all-to-all-start.1 = ((bf16[2,16,32,2048]{3,2,0,1:T(8,128)(2,1)}), bf16[2,16,32,2048]{3,2,0,1:T(8,128)(2,1)}, u32[]{:S(2)}, u32[]{:S(2)}) async-start(bf16[2,16,32,2048]{3,2,0,1:T(8,128)(2,1)} %copy.23), calls=%async_computation.2 | async-start | bytes 8388608 | tf_op jit(solution)/shard_map/all_to_all | solution.py:75
  250.4 177.2 %all-reduce.2.cloned.1.call-start = ((), (), s32[]{:S(2)}) async-start(), calls=%async_computation.5 | async-start | bytes 262144 | tf_op jit(solution)/shard_map/psum | solution.py:84
Sparse Core Ops, SparseCore 0:
  118.1 54.8 reduce-scatter.1
  183.0 56.7 all-gather.1
Sparse Core Ops, SparseCore 1:
  257.9 169.7 all-reduce.1
where the time goes:
time: 449 us
  waiting for transfers between devices  288 us (64%)
  blocking collectives  99.4 us (22%)
  local copies, waits for them, and re-layouts  19.7 us (4%)
  other arithmetic  17.6 us (4%)
  between operations  15.6 us (3%)
  starting transfers between devices  5.94 us (1%)
    psum x1, waiting for transfers between devices, on_device(): embed_factor = lax.psum(partial_factor, ('group', 'shard'))  176 us
    all_to_all x1, blocking collectives, on_device(): lax.all_to_all(jnp.where(send_used[:, :, None, None], picked, jnp.zeros((...  99.4 us
    all_gather x1, waiting for transfers between devices, on_device(): full_cols = lax.all_gather(new_half, 'group', axis=2, tiled=True)  56.9 us
    reduce_scatter x1, waiting for transfers between devices, on_device(): lax.psum_scatter(gathered.astype(jnp.float32).astype(jnp.bfloat16), 'grou...  54.8 us
    convert_element_type x1, other arithmetic, on_device(): new_half = new_anchor.astype(jnp.bfloat16)  9.8 us
  transfers between devices with their start and end apart: 4, of which 3 were waited for; matrix products, arithmetic and copies ran while one was open for 1% of the time, Pallas kernels for 0%

commit v1 on v0

v1 whole, which is shorter than its diff:
```python
import jax
import jax.numpy as jnp
from jax import lax
from jax.experimental import pallas as pl
from jax.experimental.pallas import tpu as pltpu
from jax.sharding import PartitionSpec as P

OUTER_RATE = 0.7
MOMENTUM_COEF = 0.9
CHUNKS = 2
ROW_BLOCK = 128


def slot_tables(slab_owner, devices, capacity):
    slab_count = slab_owner.shape[0]
    order_ids = jnp.arange(slab_count, dtype=jnp.int32)
    same_owner = slab_owner[:, None] == slab_owner[None, :]
    earlier = order_ids[None, :] < order_ids[:, None]
    slot_index = jnp.sum((same_owner & earlier).astype(jnp.int32), axis=1)
    matches = (slab_owner[:, None, None] == jnp.arange(devices, dtype=jnp.int32)[None, :, None]) & (
        slot_index[:, None, None] == jnp.arange(capacity, dtype=jnp.int32)[None, None, :]
    )
    slab_of = jnp.sum(jnp.where(matches, order_ids[:, None, None], 0), axis=0)
    slot_used = jnp.any(matches, axis=0)
    return (slot_index, slab_of, slot_used)


def nesterov(anchor_value, moment, mean_value):
    outer_grad = anchor_value - mean_value
    new_moment = MOMENTUM_COEF * moment + outer_grad
    new_anchor = anchor_value - OUTER_RATE * (outer_grad + MOMENTUM_COEF * new_moment)
    return (new_anchor, new_moment)


def update_kernel(used_ref, got_ref, anchor_ref, moment_ref, *refs):
    new_anchor_ref, new_moment_ref, back_ref = refs[-3:]
    used = used_ref[pl.program_id(0)] > 0
    anchor = anchor_ref[0]
    moment = moment_ref[0]
    got = got_ref[...].astype(jnp.float32)
    mean = got.reshape(anchor.shape) * 0.5
    new_anchor, new_moment = nesterov(anchor, moment, mean)
    new_anchor = jnp.where(used, new_anchor, anchor)
    new_anchor_ref[0] = new_anchor
    new_moment_ref[0] = jnp.where(used, new_moment, moment)
    back_ref[...] = new_anchor.reshape(back_ref.shape).astype(back_ref.dtype)


def update_chunk(chunk, used, got, anchor, moment, earlier):
    devices, capacity, row_count, chunk_width = got.shape
    group_rows = ROW_BLOCK // row_count
    steps = devices // group_rows
    state = pl.BlockSpec((1, ROW_BLOCK, chunk_width), lambda c, i, *_: (c, i, chunk))
    parts = pl.BlockSpec((group_rows, None, row_count, chunk_width), lambda c, i, *_: (i, c, 0, 0))
    whole = pl.BlockSpec(memory_space=pl.ANY)
    aliases = {4: 0, 5: 1} if earlier else {}
    return pl.pallas_call(
        update_kernel,
        grid_spec=pltpu.PrefetchScalarGridSpec(
            num_scalar_prefetch=1,
            grid=(capacity, steps),
            in_specs=[parts, state, state] + [whole] * len(earlier),
            out_specs=[state, state, parts],
        ),
        out_shape=[
            jax.ShapeDtypeStruct(anchor.shape, anchor.dtype),
            jax.ShapeDtypeStruct(moment.shape, moment.dtype),
            jax.ShapeDtypeStruct(got.shape, got.dtype),
        ],
        input_output_aliases=aliases,
        compiler_params=pltpu.CompilerParams(vmem_limit_bytes=32 * 1024 * 1024),
    )(used, got, anchor, moment, *earlier)


def on_device(
    replica_weights,
    anchor_slabs,
    momentum_slabs,
    slab_owner,
    replica_embed,
    anchor_embed,
    momentum_embed,
    embed_basis,
):
    local_rows = replica_weights[0]
    slab_count, row_count, width = local_rows.shape
    devices = lax.axis_size("shard")
    n_group = lax.axis_size("group")
    capacity = anchor_slabs.shape[1]
    half = width // n_group
    chunk_width = half // CHUNKS
    group_here = lax.axis_index("group")
    swap = [(0, 1), (1, 0)]
    slot_index, slab_of, slot_used = slot_tables(slab_owner, devices, capacity)
    send_ids = slab_of.reshape(-1)
    back_ids = slab_owner * capacity + slot_index
    my_used = lax.dynamic_index_in_dim(
        slot_used, lax.axis_index("shard"), 0, keepdims=False
    ).astype(jnp.int32)

    def columns(column_group, chunk):
        start = column_group * half + chunk * chunk_width
        return lax.dynamic_slice_in_dim(local_rows, start, chunk_width, axis=2)

    peer_embed = lax.ppermute(replica_embed[0], "group", swap)
    peer_rows = [
        lax.ppermute(columns(1 - group_here, chunk), "group", swap) for chunk in range(CHUNKS)
    ]
    got = []
    for chunk in range(CHUNKS):
        mine = columns(group_here, chunk).astype(jnp.float32)
        summed = (mine + peer_rows[chunk].astype(jnp.float32)).astype(jnp.bfloat16)
        packed = jnp.take(summed, send_ids, axis=0)
        packed = packed.reshape(devices, capacity, row_count, chunk_width)
        got.append(lax.all_to_all(packed, "shard", split_axis=0, concat_axis=0, tiled=True))

    embed_sum = replica_embed[0].astype(jnp.float32) + peer_embed.astype(jnp.float32)
    partial_factor = jnp.dot(
        embed_basis.T, anchor_embed - embed_sum / n_group, precision=lax.Precision.HIGHEST
    )
    rank, embed_width = partial_factor.shape
    pieces = lax.all_to_all(
        partial_factor.reshape(devices, rank // devices, embed_width),
        "shard",
        split_axis=0,
        concat_axis=0,
        tiled=True,
    )
    piece = jnp.sum(pieces, axis=0, keepdims=True)
    embed_factor = lax.all_to_all(
        jnp.broadcast_to(piece, pieces.shape), "shard", split_axis=0, concat_axis=0, tiled=True
    ).reshape(rank, embed_width)

    state = ()
    received = []
    for chunk in range(CHUNKS):
        new_anchor, new_moment, back = update_chunk(
            chunk, my_used, got[chunk], anchor_slabs[0], momentum_slabs[0], state
        )
        state = (new_anchor, new_moment)
        received.append(lax.all_to_all(back, "shard", split_axis=0, concat_axis=0, tiled=True))
    new_rows = jnp.zeros((slab_count, row_count, width), jnp.bfloat16)
    for chunk in range(CHUNKS):
        flat = received[chunk].reshape(devices * capacity, row_count, chunk_width)
        own = jnp.take(flat, back_ids, axis=0)
        other = lax.ppermute(own, "group", swap)
        for column_group, value in ((group_here, own), (1 - group_here, other)):
            start = column_group * half + chunk * chunk_width
            new_rows = lax.dynamic_update_slice_in_dim(new_rows, value, start, axis=2)

    embed_grad = jnp.dot(embed_basis, embed_factor, precision=lax.Precision.HIGHEST)
    new_anchor_embed, new_momentum_embed = nesterov(
        anchor_embed, momentum_embed, anchor_embed - embed_grad
    )
    new_embed_rows = new_anchor_embed.astype(jnp.bfloat16)
    return (
        state[0][None],
        state[1][None],
        new_rows[None],
        new_anchor_embed,
        new_momentum_embed,
        new_embed_rows[None],
    )


def solution(mesh):
    in_specs = (
        P("group", None, "shard", None),
        P("shard", None, None, "group"),
        P("shard", None, None, "group"),
        P(),
        P("group", "shard", None),
        P("shard", None),
        P("shard", None),
        P("shard", None),
    )
    out_specs = (
        P("shard", None, None, "group"),
        P("shard", None, None, "group"),
        P("group", None, "shard", None),
        P("shard", None),
        P("shard", None),
        P("group", "shard", None),
    )
    return jax.shard_map(
        on_device, mesh=mesh, in_specs=in_specs, out_specs=out_specs, check_vma=False
    )
```

time: 449 us -> 182 us (0.41)
  waiting for transfers between devices: 288 us -> 67.9 us
  blocking collectives: 99.4 us -> 42.6 us
  starting transfers between devices: 5.94 us -> 32.1 us
  between operations: 15.6 us -> 0.86 us
  other arithmetic: 17.6 us -> 6.48 us
  Pallas kernels: 0 us -> 9.46 us
    psum x1 -> x0, waiting for transfers between devices: 176 us -> none  [on_device(): embed_factor = lax.psum(partial_factor, ('group', 'shard'))]
    all_gather x1 -> x0, waiting for transfers between devices: 56.9 us -> none  [on_device(): full_cols = lax.all_gather(new_half, 'group', axis=2, tiled=True)]
    all_to_all x1 -> x2, blocking collectives: 99.4 us -> 42.6 us  [the longest x1 30.8 us: on_device(): lax.all_to_all(packed, 'shard', split_axis=0, concat_axis=0, tiled=True)]
    reduce_scatter x1 -> x0, waiting for transfers between devices: 54.8 us -> none  [on_device(): lax.psum_scatter(gathered.astype(jnp.float32).astype(jnp.bfloat16), 'grou...]
    ppermute x0 -> x5, waiting for transfers between devices: none -> 35.6 us  [the longest x2 22.1 us: on_device(): lax.ppermute(columns(1 - group_here, chunk), 'group', swap)]
    all_to_all x1 -> x4, waiting for transfers between devices: 0.01 us -> 32.3 us  [the longest x2 16.9 us: on_device(): lax.all_to_all(back, 'shard', split_axis=0, concat_axis=0, tiled=True)]
    all_to_all x1 -> x4, starting transfers between devices: 5.81 us -> 25.6 us  [the longest x2 13.7 us: on_device(): lax.all_to_all(back, 'shard', split_axis=0, concat_axis=0, tiled=True)]
    unnamed x12 -> x26, local copies, waits for them, and re-layouts: 0.03 us -> 11.7 us
  transfers between devices with their start and end apart: 4 -> 9, of which waited for: 3 -> 7; matrix products, arithmetic and copies ran while one was open for 1% -> 5% of each run, Pallas kernels for 0% -> 5%
where the time goes in v1:
time: 182 us; the launch traced here: 181 us
  waiting for transfers between devices  67.9 us (37%)
  blocking collectives  42.6 us (23%)
  starting transfers between devices  32.1 us (18%)
  local copies, waits for them, and re-layouts  20.2 us (11%)
  Pallas kernels  9.46 us (5%)
  other arithmetic  6.48 us (4%)
    all_to_all x1, blocking collectives, on_device(): lax.all_to_all(packed, 'shard', split_axis=0, concat_axis=0, tiled=True)  30.8 us
    ppermute x2, waiting for transfers between devices, on_device(): lax.ppermute(columns(1 - group_here, chunk), 'group', swap)  22.1 us
    all_to_all x2, waiting for transfers between devices, on_device(): lax.all_to_all(back, 'shard', split_axis=0, concat_axis=0, tiled=True)  16.9 us
    all_to_all x2, starting transfers between devices, on_device(): lax.all_to_all(back, 'shard', split_axis=0, concat_axis=0, tiled=True)  13.7 us
    all_to_all x1, waiting for transfers between devices, on_device(): lax.all_to_all(packed, 'shard', split_axis=0, concat_axis=0, tiled=True)  13.5 us
    ppermute x1, waiting for transfers between devices, on_device(): peer_embed = lax.ppermute(replica_embed[0], 'group', swap)  13.5 us
    all_to_all x1, blocking collectives, on_device(): lax.all_to_all(jnp.broadcast_to(piece, pieces.shape), 'shard', split_axis...  11.8 us
    unnamed x26, local copies, waits for them, and re-layouts  11.7 us
  transfers between devices with their start and end apart: 9, of which 7 were waited for; matrix products, arithmetic and copies ran while one was open for 5% of the time, Pallas kernels for 5%

profile of v1, /device:TPU:0, one launch (start us, length us, event | category | flops | bytes accessed | tf_op | source)
XLA Modules:
  0.0 180.9 jit_solution(7649599986668767066)
XLA Ops:
  0.7 2.2 %dynamic-slice_bitcast_fusion = (bf16[16,32,512]{2,1,0:T(8,128)(2,1)}, bf16[16,32,512]{2,1,0:T(8,128)(2,1)S(1)}) fusion(bf16[1,16,32,2048]{3,2,1,0:T(8,128)(2,1)} %param.12, s32[]{:T(128)S(6)} %select_n.43, s32[]{:T(128)S(6)} %select_n.40), kind=kLoop, calls=%fused_computation.18 | loop fusion | bytes 2097160 | tf_op jit(solution)/shard_map/dynamic_slice | solution.py:103
  2.9 2.9 %collective-permute-start.1 = (bf16[16,32,512]{2,1,0:T(8,128)(2,1)}, bf16[16,32,512]{2,1,0:T(8,128)(2,1)S(1)}, u32[]{:S(2)}, u32[]{:S(2)}) collective-permute-start(bf16[16,32,512]{2,1,0:T(8,128)(2,1)} %get-tuple-element.31), channel_id=1, source_target_pairs={{0,16},{16,0},{1,17},{17,1},{2,18},{18,2},{3,19},{19,3},{4,20},{20... | collective-permute-start | bytes 1572872 | tf_op jit(solution)/shard_map/ppermute | solution.py:107
  5.9 0.2 convert_reduce_fusion
  6.1 0.1 iota_compare_fusion.1
  6.2 0.1 fusion.10
  6.3 0.1 copy.17
  6.3 0.1 reshape.110
  6.5 12.3 %collective-permute-done.1 = bf16[16,32,512]{2,1,0:T(8,128)(2,1)S(1)} collective-permute-done((bf16[16,32,512]{2,1,0:T(8,128)(2,1)}, bf16[16,32,512]{2,1,0:T(8,128)(2,1)S(1)}, u32[]{:S(2)}, u32[]{:S(2)}) %collective-permute-start.1) | collective-permute-done | bytes 524320 | tf_op jit(solution)/shard_map/ppermute | solution.py:107
  18.8 0.8 copy-done.8
  19.6 9.7 %collective-permute-done = bf16[16,32,512]{2,1,0:T(8,128)(2,1)} collective-permute-done((bf16[16,32,512]{2,1,0:T(8,128)(2,1)S(1)}, bf16[16,32,512]{2,1,0:T(8,128)(2,1)}, u32[]{:S(2)}, u32[]{:S(2)}) %collective-permute-start) | collective-permute-done | bytes 524320 | tf_op jit(solution)/shard_map/ppermute | solution.py:107
  29.3 1.6 fusion.2
  30.9 0.6 gather_fusion.1
  31.6 0.6 gather_fusion
  32.2 1.2 broadcast_select_fusion
  33.4 30.8 %all_to_all.30.got_ref = bf16[16,2,32,512]{3,2,1,0:T(8,128)(2,1)S(1)} all-to-all(bf16[16,2,32,512]{3,2,1,0:T(8,128)(2,1)S(1)} %bitcast.52), channel_id=1, replica_groups=mesh['group'=2,'shard'=16] {'shard'}, dimensions={0} | all-to-all | bytes 2097152 | tf_op jit(solution)/shard_map/all_to_all | solution.py:115
  64.2 5.0 %all-to-all-start = ((bf16[16,2,32,512]{3,2,1,0:T(8,128)(2,1)}), bf16[16,2,32,512]{3,2,1,0:T(8,128)(2,1)S(1)}, u32[]{:S(2)}, u32[]{:S(2)}) async-start(bf16[16,2,32,512]{3,2,1,0:T(8,128)(2,1)} %bitcast.2), calls=%async_computation | async-start | bytes 2097152 | tf_op jit(solution)/shard_map/all_to_all | solution.py:115
  69.2 0.1 and_reduce_fusion
  69.3 0.2 fusion.13.used_ref
  69.5 2.2 %copy-done.1 = f32[1,2,512,1024]{3,2,1,0:T(8,128)S(1)} copy-done((f32[1,2,512,1024]{3,2,1,0:T(8,128)S(1)}, f32[1,2,512,1024]{3,2,1,0:T(8,128)}, u32[]{:S(2)}) %copy-start.1) | copy-done | bytes 4194328
  71.7 2.2 %copy-done.3 = f32[1,2,512,1024]{3,2,1,0:T(8,128)S(1)} copy-done((f32[1,2,512,1024]{3,2,1,0:T(8,128)S(1)}, f32[1,2,512,1024]{3,2,1,0:T(8,128)}, u32[]{:S(2)}) %copy-start.3) | copy-done | bytes 4194328
  73.9 4.8 %shard_map.127 = (f32[2,512,1024]{2,1,0:T(8,128)}, f32[2,512,1024]{2,1,0:T(8,128)}, bf16[16,2,32,512]{3,2,1,0:T(8,128)(2,1)}) custom-call(s32[2]{0:T(128)S(1)} %fusion.13.used_ref, bf16[16,2,32,512]{3,2,1,0:T(8,128)(2,1)S(1)} %all_to_all.30.got_ref, f32[2,512,1024]{2,1,0:T(8,128)S(1)} %bitcast.46, f32[2,512,1024]{2,1,0:T(8,128)S(1)} %bitcast.48), custom_call_target="tpu_custom_call" | custom-call | tf_op jit(solution)/shard_map/pallas_call | solution.py:57
  78.7 13.5 %all-to-all-done.got_ref = bf16[16,2,32,512]{3,2,1,0:T(8,128)(2,1)S(1)} async-done(((bf16[16,2,32,512]{3,2,1,0:T(8,128)(2,1)}), bf16[16,2,32,512]{3,2,1,0:T(8,128)(2,1)S(1)}, u32[]{:S(2)}, u32[]{:S(2)}) %all-to-all-start) | async-done | bytes 1048608 | tf_op jit(solution)/shard_map/all_to_all | solution.py:115
  92.2 6.9 %all-to-all-start.2 = ((bf16[16,2,32,512]{3,2,1,0:T(8,128)(2,1)}), bf16[16,2,32,512]{3,2,1,0:T(8,128)(2,1)S(1)}, u32[]{:S(2)}, u32[]{:S(2)}) async-start(bf16[16,2,32,512]{3,2,1,0:T(8,128)(2,1)} %get-tuple-element.18), calls=%async_computation.2 | async-start | bytes 2097152 | tf_op jit(solution)/shard_map/all_to_all | solution.py:141
  99.1 2.2 %copy-done.2 = f32[1,2,512,1024]{3,2,1,0:T(8,128)S(1)} copy-done((f32[1,2,512,1024]{3,2,1,0:T(8,128)S(1)}, f32[1,2,512,1024]{3,2,1,0:T(8,128)}, u32[]{:S(2)}) %copy-start.2) | copy-done | bytes 4194328
  101.2 2.2 %copy-done.4 = f32[1,2,512,1024]{3,2,1,0:T(8,128)S(1)} copy-done((f32[1,2,512,1024]{3,2,1,0:T(8,128)S(1)}, f32[1,2,512,1024]{3,2,1,0:T(8,128)}, u32[]{:S(2)}) %copy-start.4) | copy-done | bytes 4194328
  103.4 4.7 %shard_map.128 = (f32[2,512,1024]{2,1,0:T(8,128)}, f32[2,512,1024]{2,1,0:T(8,128)}, bf16[16,2,32,512]{3,2,1,0:T(8,128)(2,1)}) custom-call(s32[2]{0:T(128)S(1)} %fusion.13.used_ref, bf16[16,2,32,512]{3,2,1,0:T(8,128)(2,1)S(1)} %all-to-all-done.got_ref, f32[2,512,1024]{2,1,0:T(8,128)S(1)} %bitcast.47, ...), custom_call_target="tpu_custom_call", output_to_operand_aliasing={{0}: (4, {}), {1}: (5, {})} | custom-call | tf_op jit(solution)/shard_map/pallas_call | solution.py:57
  108.1 13.9 %all-to-all-done.2 = bf16[16,2,32,512]{3,2,1,0:T(8,128)(2,1)S(1)} async-done(((bf16[16,2,32,512]{3,2,1,0:T(8,128)(2,1)}), bf16[16,2,32,512]{3,2,1,0:T(8,128)(2,1)S(1)}, u32[]{:S(2)}, u32[]{:S(2)}) %all-to-all-start.2) | async-done | bytes 1048608 | tf_op jit(solution)/shard_map/all_to_all | solution.py:141
  122.0 6.9 %all-to-all-start.3 = ((bf16[16,2,32,512]{3,2,1,0:T(8,128)(2,1)}), bf16[16,2,32,512]{3,2,1,0:T(8,128)(2,1)S(1)}, u32[]{:S(2)}, u32[]{:S(2)}) async-start(bf16[16,2,32,512]{3,2,1,0:T(8,128)(2,1)} %get-tuple-element.19), calls=%async_computation.3 | async-start | bytes 2097152 | tf_op jit(solution)/shard_map/all_to_all | solution.py:141
  128.9 1.4 gather_fusion.2
  130.3 0.2 broadcast_in_dim.70
  130.5 0.8 copy-done.7
  131.3 0.9 bitcast_dynamic-update-slice_fusion.3
  132.3 1.5 collective-permute-start.2
  133.7 0.5 collective-permute-start.4
  134.3 13.5 %collective-permute-done.4 = bf16[48,512]{1,0:T(8,128)(2,1)S(1)} collective-permute-done((bf16[48,512]{1,0:T(8,128)(2,1)S(1)}, bf16[48,512]{1,0:T(8,128)(2,1)S(1)}, u32[]{:S(2)}, u32[]{:S(2)}) %collective-permute-start.4) | collective-permute-done | bytes 49184 | tf_op jit(solution)/shard_map/ppermute | solution.py:105
  147.8 0.3 convolution_bitcast_fusion
  148.1 0.7 reshape.115
  148.8 3.0 %all-to-all-done.3 = bf16[16,2,32,512]{3,2,1,0:T(8,128)(2,1)S(1)} async-done(((bf16[16,2,32,512]{3,2,1,0:T(8,128)(2,1)}), bf16[16,2,32,512]{3,2,1,0:T(8,128)(2,1)S(1)}, u32[]{:S(2)}, u32[]{:S(2)}) %all-to-all-start.3) | async-done | bytes 1048608 | tf_op jit(solution)/shard_map/all_to_all | solution.py:141
  151.8 6.9 %all-to-all-start.4 = ((f32[16,4,512]{2,1,0:T(4,128)}), f32[16,4,512]{2,1,0:T(4,128)S(1)}, u32[]{:S(2)}, u32[]{:S(2)}) async-start(f32[16,4,512]{2,1,0:T(4,128)} %reshape.115), calls=%async_computation.4 | async-start | bytes 262144 | tf_op jit(solution)/shard_map/all_to_all | solution.py:122
  158.7 1.4 gather_fusion.3
  160.1 1.1 bitcast_dynamic-update-slice_fusion.2
  161.2 2.0 %bitcast_dynamic-update-slice_fusion.1 = (bf16[1,16,32,2048]{3,2,1,0:T(8,128)(2,1)S(1)}, bf16[16,32,512]{2,1,0:T(8,128)(2,1)}) fusion(bf16[1,16,32,2048]{3,2,1,0:T(8,128)(2,1)S(1)} %bitcast_dynamic-update-slice_fusion.2, s32[]{:T(128)S(6)} %select_n.39, bf16[16,32,512]{2,1,0:T(8,128)(2,1)} %gather_fusion.3, pred[16]{0:T(512)(128)(4,1)S(1)} %get-tuple-element.27), kind=kLoop, calls=%fused_computation.15 | loop fusion | flops 262144 | bytes 1573380 | tf_op jit(solution)/shard_map/dynamic_update_slice | solution.py:149
  163.2 1.5 collective-permute-start.3
  164.7 1.9 %all-to-all-done.4 = f32[16,4,512]{2,1,0:T(4,128)S(1)} async-done(((f32[16,4,512]{2,1,0:T(4,128)}), f32[16,4,512]{2,1,0:T(4,128)S(1)}, u32[]{:S(2)}, u32[]{:S(2)}) %all-to-all-start.4) | async-done | bytes 131104 | tf_op jit(solution)/shard_map/all_to_all | solution.py:122
  166.7 11.8 %all_to_all.31 = f32[16,4,512]{2,1,0:T(4,128)S(1)} all-to-all(f32[16,4,512]{2,1,0:T(4,128)S(1)} %broadcast_in_dim.75), channel_id=1, replica_groups=mesh['group'=2,'shard'=16] {'shard'}, dimensions={0} | all-to-all | bytes 262144 | tf_op jit(solution)/shard_map/all_to_all | solution.py:130
  178.5 0.9 convert_bitcast_fusion
  179.5 0.1 bitcast_dynamic-update-slice_fusion
  179.6 1.3 copy-done.5
  (31 shorter events, 0.2 us)
Async XLA Ops:
  0.6 147.1 %copy-start = (f32[48,64]{1,0:T(8,128)S(1)}, f32[48,64]{1,0:T(8,128)}, u32[]{:S(2)}) copy-start(f32[48,64]{1,0:T(8,128)} %param.19) | copy-start | bytes 36868
  0.6 28.7 %copy-start.6 = (bf16[1,16,32,2048]{3,2,1,0:T(8,128)(2,1)S(1)}, bf16[1,16,32,2048]{3,2,1,0:T(8,128)(2,1)}, u32[]{:S(2)}) copy-start(bf16[1,16,32,2048]{3,2,1,0:T(8,128)(2,1)} %param.12) | copy-start | bytes 6291460
  0.7 5.2 %copy-start.12 = (s32[16]{0:T(128)S(1)}, s32[16]{0:T(128)}, u32[]{:S(2)}) copy-start(s32[16]{0:T(128)} %param.15) | copy-start | bytes 196
  2.9 15.9 %collective-permute-start.1 = (bf16[16,32,512]{2,1,0:T(8,128)(2,1)}, bf16[16,32,512]{2,1,0:T(8,128)(2,1)S(1)}, u32[]{:S(2)}, u32[]{:S(2)}) collective-permute-start(bf16[16,32,512]{2,1,0:T(8,128)(2,1)} %get-tuple-element.31), channel_id=1, source_target_pairs={{0,16},{16,0},{1,17},{17,1},{2,18},{18,2},{3,19},{19,3},{4,20},{20... | collective-permute-start | bytes 1572872 | tf_op jit(solution)/shard_map/ppermute | solution.py:107
  5.9 23.5 %collective-permute-start = (bf16[16,32,512]{2,1,0:T(8,128)(2,1)S(1)}, bf16[16,32,512]{2,1,0:T(8,128)(2,1)}, u32[]{:S(2)}, u32[]{:S(2)}) collective-permute-start(bf16[16,32,512]{2,1,0:T(8,128)(2,1)S(1)} %get-tuple-element.32), channel_id=1, source_target_pairs={{0,16},{16,0},{1,17},{17,1},{2,18},{18,2},{3,19},{19,3},{4,20},{20... | collective-permute-start | bytes 1572872 | tf_op jit(solution)/shard_map/ppermute | solution.py:107
  18.8 0.8 copy-start.8
  64.2 27.9 %all-to-all-start = ((bf16[16,2,32,512]{3,2,1,0:T(8,128)(2,1)}), bf16[16,2,32,512]{3,2,1,0:T(8,128)(2,1)S(1)}, u32[]{:S(2)}, u32[]{:S(2)}) async-start(bf16[16,2,32,512]{3,2,1,0:T(8,128)(2,1)} %bitcast.2), calls=%async_computation | async-start | bytes 2097152 | tf_op jit(solution)/shard_map/all_to_all | solution.py:115
  69.5 2.2 %copy-start.1 = (f32[1,2,512,1024]{3,2,1,0:T(8,128)S(1)}, f32[1,2,512,1024]{3,2,1,0:T(8,128)}, u32[]{:S(2)}) copy-start(f32[1,2,512,1024]{3,2,1,0:T(8,128)} %param.13) | copy-start | bytes 12582916
  71.7 2.2 %copy-start.3 = (f32[1,2,512,1024]{3,2,1,0:T(8,128)S(1)}, f32[1,2,512,1024]{3,2,1,0:T(8,128)}, u32[]{:S(2)}) copy-start(f32[1,2,512,1024]{3,2,1,0:T(8,128)} %param.14) | copy-start | bytes 12582916
  92.2 29.8 %all-to-all-start.2 = ((bf16[16,2,32,512]{3,2,1,0:T(8,128)(2,1)}), bf16[16,2,32,512]{3,2,1,0:T(8,128)(2,1)S(1)}, u32[]{:S(2)}, u32[]{:S(2)}) async-start(bf16[16,2,32,512]{3,2,1,0:T(8,128)(2,1)} %get-tuple-element.18), calls=%async_computation.2 | async-start | bytes 2097152 | tf_op jit(solution)/shard_map/all_to_all | solution.py:141
  99.1 2.2 %copy-start.2 = (f32[1,2,512,1024]{3,2,1,0:T(8,128)S(1)}, f32[1,2,512,1024]{3,2,1,0:T(8,128)}, u32[]{:S(2)}) copy-start(f32[1,2,512,1024]{3,2,1,0:T(8,128)} %param.13) | copy-start | bytes 12582916
  101.2 2.2 %copy-start.4 = (f32[1,2,512,1024]{3,2,1,0:T(8,128)S(1)}, f32[1,2,512,1024]{3,2,1,0:T(8,128)}, u32[]{:S(2)}) copy-start(f32[1,2,512,1024]{3,2,1,0:T(8,128)} %param.14) | copy-start | bytes 12582916
  122.0 29.8 %all-to-all-start.3 = ((bf16[16,2,32,512]{3,2,1,0:T(8,128)(2,1)}), bf16[16,2,32,512]{3,2,1,0:T(8,128)(2,1)S(1)}, u32[]{:S(2)}, u32[]{:S(2)}) async-start(bf16[16,2,32,512]{3,2,1,0:T(8,128)(2,1)} %get-tuple-element.19), calls=%async_computation.3 | async-start | bytes 2097152 | tf_op jit(solution)/shard_map/all_to_all | solution.py:141
  130.3 1.0 copy-start.7
  130.3 3.5 %copy-start.11 = (bf16[1,48,512]{2,1,0:T(8,128)(2,1)S(1)}, bf16[1,48,512]{2,1,0:T(8,128)(2,1)}, u32[]{:S(2)}) copy-start(bf16[1,48,512]{2,1,0:T(8,128)(2,1)} %param.16) | copy-start | bytes 147460
  130.3 17.5 %copy-start.9 = (f32[48,512]{1,0:T(8,128)S(1)}, f32[48,512]{1,0:T(8,128)}, u32[]{:S(2)}) copy-start(f32[48,512]{1,0:T(8,128)} %param.17) | copy-start | bytes 294916
  132.3 27.8 %collective-permute-start.2 = (bf16[16,32,512]{2,1,0:T(8,128)(2,1)}, bf16[16,32,512]{2,1,0:T(8,128)(2,1)}, u32[]{:S(2)}, u32[]{:S(2)}) collective-permute-start(bf16[16,32,512]{2,1,0:T(8,128)(2,1)} %get-tuple-element.26), channel_id=1, source_target_pairs={{0,16},{16,0},{1,17},{17,1},{2,18},{18,2},{3,19},{19,3},{4,20},{20... | collective-permute-start | bytes 1572872 | tf_op jit(solution)/shard_map/ppermute | solution.py:146
  133.7 14.0 %collective-permute-start.4 = (bf16[48,512]{1,0:T(8,128)(2,1)S(1)}, bf16[48,512]{1,0:T(8,128)(2,1)S(1)}, u32[]{:S(2)}, u32[]{:S(2)}) collective-permute-start(bf16[48,512]{1,0:T(8,128)(2,1)S(1)} %bitcast.55), channel_id=1, source_target_pairs={{0,16},{16,0},{1,17},{17,1},{2,18},{18,2},{3,19},{19,3},{4,20},{20... | collective-permute-start | bytes 147464 | tf_op jit(solution)/shard_map/ppermute | solution.py:105
  151.8 14.8 %all-to-all-start.4 = ((f32[16,4,512]{2,1,0:T(4,128)}), f32[16,4,512]{2,1,0:T(4,128)S(1)}, u32[]{:S(2)}, u32[]{:S(2)}) async-start(f32[16,4,512]{2,1,0:T(4,128)} %reshape.115), calls=%async_computation.4 | async-start | bytes 262144 | tf_op jit(solution)/shard_map/all_to_all | solution.py:122
  158.7 19.8 %copy-start.10 = (f32[48,512]{1,0:T(8,128)S(1)}, f32[48,512]{1,0:T(8,128)}, u32[]{:S(2)}) copy-start(f32[48,512]{1,0:T(8,128)} %param.18) | copy-start | bytes 294916
  163.2 16.3 %collective-permute-start.3 = (bf16[16,32,512]{2,1,0:T(8,128)(2,1)}, bf16[16,32,512]{2,1,0:T(8,128)(2,1)S(1)}, u32[]{:S(2)}, u32[]{:S(2)}) collective-permute-start(bf16[16,32,512]{2,1,0:T(8,128)(2,1)} %get-tuple-element.24), channel_id=1, source_target_pairs={{0,16},{16,0},{1,17},{17,1},{2,18},{18,2},{3,19},{19,3},{4,20},{20... | collective-permute-start | bytes 1572872 | tf_op jit(solution)/shard_map/ppermute | solution.py:146
  179.6 1.3 copy-start.5

commit v2 on v0

v2 whole, which is shorter than its diff:
```python
import jax
import jax.numpy as jnp
from jax import lax
from jax.experimental import pallas as pl
from jax.experimental.pallas import tpu as pltpu
from jax.sharding import PartitionSpec as P

OUTER_RATE = 0.7
MOMENTUM_COEF = 0.9
PLANES = 4
CHUNKS = ((4, 2, False), (0, 4, False), (6, 2, False))
EMBED = None
ORDER = (
    (0, 0), (EMBED, 0), (1, 0), (2, 0), (EMBED, 0), (0, 1), (EMBED, 0), (1, 1, 0), (0, 2), (EMBED, 0),
    (0, 3), (2, 1, 1), (1, 2), (0, 4, 2), (2, 2), (1, 3), (EMBED, 0), (2, 3), (0, 5), (1, 4), (EMBED, 0),
    (2, 4, 1), (1, 5), (EMBED, 0), (0, 6), (2, 5), (1, 6), (2, 6),
)
VMEM_LIMIT = 48 * 1024 * 1024


def nesterov(anchor_value, moment, mean_value):
    outer_grad = anchor_value - mean_value
    new_moment = MOMENTUM_COEF * moment + outer_grad
    new_anchor = anchor_value - OUTER_RATE * (outer_grad + MOMENTUM_COEF * new_moment)
    return (new_anchor, new_moment)


def call(
    kernel, scalars, operands, in_specs, out_shape, out_specs, grid=(1,), aliases=None, after=(), name=None,
    scratch=()
):
    first, last = len(scalars), len(scalars) + len(after)

    def body(*refs):
        kernel(*refs[:first], *refs[last:])

    return pl.pallas_call(
        body,
        grid_spec=pltpu.PrefetchScalarGridSpec(
            num_scalar_prefetch=first,
            grid=grid,
            in_specs=[pl.BlockSpec(memory_space=pl.ANY)] * len(after) + in_specs,
            out_specs=out_specs,
            scratch_shapes=scratch,
        ),
        out_shape=out_shape,
        input_output_aliases={first + len(after) + i: o for i, o in (aliases or {}).items()},
        compiler_params=pltpu.CompilerParams(vmem_limit_bytes=VMEM_LIMIT),
        name=name,
        cost_estimate=pl.CostEstimate(flops=1, bytes_accessed=1, transcendentals=0),
    )(*scalars, *after, *operands)


def full(shape):
    return pl.BlockSpec(memory_space=pltpu.VMEM)


def like(shape, dtype=jnp.bfloat16):
    return jax.ShapeDtypeStruct(shape, dtype)


WHOLE = pl.BlockSpec(memory_space=pl.ANY)


def columns(group, rows, start, width):
    first = group * (rows.shape[2] // 2) + start
    return pl.ds(pl.multiple_of(first, width), width)


def take_columns(here, local_rows, start, width, after):
    block = local_rows.shape[:2] + (width,)

    def kernel(here_ref, rows_ref, *refs):
        done = refs[-1]
        copies = []
        for i, group in enumerate((1 - here_ref[0], here_ref[0])):
            chosen = columns(group, rows_ref, start, width)
            copies.append(pltpu.make_async_copy(rows_ref.at[:, :, chosen], refs[i], done.at[i]))
        for copy in copies:
            copy.start()
        for copy in copies:
            copy.wait()

    return call(
        kernel,
        (here,),
        (local_rows,),
        [WHOLE],
        [like(block)] * 2,
        [full(block)] * 2,
        after=after,
        scratch=[pltpu.SemaphoreType.DMA((2,))],
        name="take_columns",
    )


def sum_and_pack(plane_ids, mine, peer, slots, after):
    def kernel(ids_ref, mine_ref, peer_ref, *outs):
        for k, out in enumerate(outs):

            @pl.loop(0, slots)
            def _(j, k=k, out=out):
                i = ids_ref[k, j]
                out[j] = mine_ref[i] + peer_ref[i]

    packed = (slots,) + mine.shape[1:]
    return call(
        kernel,
        (plane_ids,),
        (mine, peer),
        [full(mine.shape)] * 2,
        [like(packed)] * PLANES,
        [full(packed)] * PLANES,
        after=after,
        name="sum_and_pack",
    )


def sum_for_owners(slab_of, mine, peer, after):
    devices, capacity = slab_of.shape

    def kernel(ids_ref, mine_ref, peer_ref, out):
        @pl.loop(0, devices)
        def _(d):
            for c in range(capacity):
                i = ids_ref[d, c]
                out[d, c] = mine_ref[i] + peer_ref[i]

    packed = (devices, capacity) + mine.shape[1:]
    return call(
        kernel,
        (slab_of,),
        (mine, peer),
        [full(mine.shape)] * 2,
        like(packed),
        full(packed),
        after=after,
        name="sum_for_owners",
    )


def pack_for_owners(here, owner_pos, parts, inside, capacity, after):
    slots, row_count, width = parts[0].shape

    def kernel(here_ref, pos_ref, *refs):
        ins, outs = refs[:PLANES], refs[PLANES:]
        for k, part in enumerate(ins):
            z = lax.rem(here_ref[1] + PLANES - k, PLANES)
            for m, out in enumerate(outs):
                for c in range(capacity):
                    out[c, z] = part[pos_ref[m, c]]

    packed = (capacity, PLANES, row_count, width)
    return call(
        kernel,
        (here, owner_pos),
        parts,
        [full(parts[0].shape)] * PLANES,
        [like(packed)] * inside,
        [full(packed)] * inside,
        after=after,
        name="pack_for_owners",
    )


def update_chunk(here, used, got, anchor, moment, start, earlier, after):
    capacity, planes, row_count, width = got[0].shape
    inside = len(got)

    def kernel(here_ref, used_ref, *refs):
        ins, anchor_ref, moment_ref = refs[:inside], refs[inside], refs[inside + 1]
        new_anchor_ref, new_moment_ref = refs[-inside - 2], refs[-inside - 1]
        outs = refs[-inside:]
        c = pl.program_id(0)
        used_here = used_ref[c] > 0

        @pl.loop(0, planes)
        def _(z):
            for m in range(inside):
                first = (z * inside + (here_ref[2] ^ m)) * row_count
                rows = pl.ds(pl.multiple_of(first, row_count), row_count)
                anchor_value = anchor_ref[rows, :]
                moment_value = moment_ref[rows, :]
                mean = ins[m][c, z].astype(jnp.float32) * 0.5
                new_anchor, new_moment = nesterov(anchor_value, moment_value, mean)
                new_anchor = jnp.where(used_here, new_anchor, anchor_value)
                new_anchor_ref[rows, :] = new_anchor
                new_moment_ref[rows, :] = jnp.where(used_here, new_moment, moment_value)
                outs[m][c, z] = new_anchor.astype(outs[m].dtype)

    state = pl.BlockSpec((None, anchor.shape[1], width), lambda c, *_: (c, 0, start // width))
    part = full(got[0].shape)
    return call(
        kernel,
        (here, used),
        (*got, anchor, moment, *earlier),
        [part] * inside + [state, state] + [WHOLE] * len(earlier),
        [like(anchor.shape, anchor.dtype)] * 2 + [like(got[0].shape)] * inside,
        [state, state] + [part] * inside,
        grid=(capacity,),
        aliases={inside + 2: 0, inside + 3: 1} if earlier else {},
        after=after,
        name="update_chunk",
    )


def update_owned(here, used, got, anchor, moment, start, earlier, after):
    devices, capacity, row_count, width = got.shape

    def kernel(here_ref, used_ref, got_ref, anchor_ref, moment_ref, *refs):
        new_anchor_ref, new_moment_ref, out_ref = refs[-3:]
        c = pl.program_id(0)
        used_here = used_ref[c] > 0

        @pl.loop(0, devices)
        def _(d):
            rows = pl.ds(pl.multiple_of(d * row_count, row_count), row_count)
            anchor_value = anchor_ref[rows, :]
            moment_value = moment_ref[rows, :]
            mean = got_ref[d, c].astype(jnp.float32) * 0.5
            new_anchor, new_moment = nesterov(anchor_value, moment_value, mean)
            new_anchor = jnp.where(used_here, new_anchor, anchor_value)
            new_anchor_ref[rows, :] = new_anchor
            new_moment_ref[rows, :] = jnp.where(used_here, new_moment, moment_value)
            out_ref[d, c] = new_anchor.astype(out_ref.dtype)

    state = pl.BlockSpec((None, anchor.shape[1], width), lambda c, *_: (c, 0, start // width))
    part = full(got.shape)
    return call(
        kernel,
        (here, used),
        (got, anchor, moment, *earlier),
        [part, state, state] + [WHOLE] * len(earlier),
        [like(anchor.shape, anchor.dtype)] * 2 + [like(got.shape)],
        [state, state, part],
        grid=(capacity,),
        aliases={3: 0, 4: 1} if earlier else {},
        after=after,
        name="update_owned",
    )


def pack_for_planes(here, owner_pos, owner_used, backs, slots, after):
    capacity, _, row_count, width = backs[0].shape
    inside = len(backs)

    def kernel(here_ref, pos_ref, used_ref, *refs):
        ins, outs = refs[:inside], refs[inside:]
        for m in range(inside):
            for c in range(capacity):

                @pl.when(used_ref[m, c] > 0)
                def _(m=m, c=c):
                    for k, out in enumerate(outs):
                        out[pos_ref[m, c]] = ins[m][c, lax.rem(here_ref[1] + k, PLANES)]

    packed = (slots, row_count, width)
    return call(
        kernel,
        (here, owner_pos, owner_used),
        backs,
        [full(backs[0].shape)] * inside,
        [like(packed)] * PLANES,
        [full(packed)] * PLANES,
        after=after,
        name="pack_for_planes",
    )


def unpack(in_ids, in_counts, parts, slab_count, after):
    _, row_count, width = parts[0].shape

    def kernel(ids_ref, counts_ref, *refs):
        for k in range(PLANES):

            @pl.loop(0, counts_ref[k])
            def _(j, k=k):
                refs[-1][ids_ref[k, j]] = refs[k][j]

    block = (slab_count, row_count, width)
    return call(
        kernel,
        (in_ids, in_counts),
        parts,
        [full(parts[0].shape)] * PLANES,
        like(block),
        full(block),
        after=after,
        name="unpack",
    )


def unpack_owned(slab_owner, slot_index, got, after):
    slab_count = slab_owner.shape[0]

    def kernel(owner_ref, slot_ref, got_ref, out_ref):
        @pl.loop(0, slab_count)
        def _(s):
            out_ref[s] = got_ref[owner_ref[s], slot_ref[s]]

    block = (slab_count,) + got.shape[2:]
    return call(
        kernel,
        (slab_owner, slot_index),
        (got,),
        [full(got.shape)],
        like(block),
        full(block),
        after=after,
        name="unpack_owned",
    )


def place(here, own, other, start, whole_shape, earlier, after):
    width = own.shape[2]

    def kernel(here_ref, own_ref, other_ref, *refs):
        out_ref, done = refs[-2:]
        copies = []
        for i, (group, value) in enumerate(((here_ref[0], own_ref), (1 - here_ref[0], other_ref))):
            chosen = columns(group, out_ref, start, width)
            copies.append(pltpu.make_async_copy(value, out_ref.at[:, :, chosen], done.at[i]))
        for copy in copies:
            copy.start()
        for copy in copies:
            copy.wait()

    return call(
        kernel,
        (here,),
        (own, other, *earlier),
        [full(own.shape)] * 2 + [WHOLE] * len(earlier),
        like(whole_shape),
        WHOLE,
        aliases={2: 0} if earlier else {},
        after=after,
        scratch=[pltpu.SemaphoreType.DMA((2,))],
        name="place",
    )


def project_embed(embed_basis, anchor_embed, embed_rows, peer_rows, after):
    def kernel(basis_ref, anchor_ref, mine_ref, peer_ref, out_ref):
        total = mine_ref[...].astype(jnp.float32) + peer_ref[...].astype(jnp.float32)
        out_ref[...] = lax.dot_general(
            basis_ref[...],
            anchor_ref[...] - total * 0.5,
            (((0,), (0,)), ((), ())),
            precision=lax.Precision.HIGHEST,
            preferred_element_type=jnp.float32,
        )

    operands = (embed_basis, anchor_embed, embed_rows, peer_rows)
    shape = (embed_basis.shape[1], anchor_embed.shape[1])
    return call(
        kernel,
        (),
        operands,
        [full(value.shape) for value in operands],
        like(shape, jnp.float32),
        full(shape),
        after=after,
        name="project_embed",
    )


def add(first, second, after):
    def kernel(first_ref, second_ref, out_ref):
        out_ref[...] = first_ref[...] + second_ref[...]

    return call(
        kernel,
        (),
        (first, second),
        [full(first.shape)] * 2,
        like(first.shape, first.dtype),
        full(first.shape),
        after=after,
        name="add",
    )


def update_embed(embed_basis, embed_factor, anchor_embed, momentum_embed, after):
    def kernel(basis_ref, factor_ref, anchor_ref, moment_ref, *outs):
        embed_grad = jnp.dot(
            basis_ref[...],
            factor_ref[...],
            precision=lax.Precision.HIGHEST,
            preferred_element_type=jnp.float32,
        )
        anchor = anchor_ref[...]
        new_anchor, new_moment = nesterov(anchor, moment_ref[...], anchor - embed_grad)
        for out, value in zip(outs, (new_anchor, new_moment, new_anchor)):
            out[...] = value.astype(out.dtype)

    operands = (embed_basis, embed_factor, anchor_embed, momentum_embed)
    shape = anchor_embed.shape
    return call(
        kernel,
        (),
        operands,
        [full(value.shape) for value in operands],
        [like(shape, jnp.float32), like(shape, jnp.float32), like(shape)],
        [full(shape)] * 3,
        after=after,
        name="update_embed",
    )


def moved(
    slots,
    tables,
    local_rows,
    anchor,
    moment,
    embed_rows,
    anchor_embed,
    momentum_embed,
    embed_basis,
):
    (here, to_ids, from_ids, from_counts, owner_pos, owner_used, my_used, slab_of, slab_owner,
        slot_index) = tables
    devices = lax.axis_size("shard")
    inside = devices // PLANES
    capacity = anchor.shape[0]
    eighth = local_rows.shape[2] // 16
    swap = [(0, 1), (1, 0)]
    def over_planes(parts):
        return [parts[0]] + [
            lax.ppermute(
                parts[k], "shard", [(i, (i + k * inside) % devices) for i in range(devices)]
            )
            for k in range(1, PLANES)
        ]

    def over_devices(value):
        return lax.all_to_all(value, "shard", split_axis=0, concat_axis=0, tiled=True)

    def in_plane(parts):
        return [parts[0]] + [
            lax.ppermute(parts[m], "shard", [(i, i ^ m) for i in range(devices)])
            for m in range(1, inside)
        ]

    def embed_steps():
        after = yield None
        rows = lax.optimization_barrier((embed_rows, *after))[0]
        peer = lax.ppermute(rows, "group", swap)
        after = yield after[0]
        factor = project_embed(embed_basis, anchor_embed, embed_rows, peer, after)
        step = 1
        while step < devices:
            pairs = [(i, i ^ step) for i in range(devices)]
            other = lax.ppermute(factor, "shard", pairs)
            after = yield factor
            factor = add(factor, other, after)
            step *= 2
        after = yield factor
        yield update_embed(embed_basis, factor, anchor_embed, momentum_embed, after)

    embed = embed_steps()
    next(embed)
    new_embed = None
    held = [None] * len(CHUNKS)
    state, new_rows, after = (), (), ()
    for chunk, step, *waits in ORDER:
        for wait in waits:
            after += tuple(held[wait])
        if chunk == EMBED:
            new_embed = embed.send(after)
            if isinstance(new_embed, jax.Array):
                after = (new_embed,)
            continue
        start, width, direct = CHUNKS[chunk]
        start, width = start * eighth, width * eighth
        value = held[chunk]
        if step == 0:
            if not after:
                first = (1 - here[0]) * (local_rows.shape[2] // 2) + start
                after = (lax.dynamic_slice_in_dim(local_rows, first, width, axis=2),)
                value = lax.ppermute(after[0], "group", swap)
                token, mine = take_columns(here, local_rows, start, width, after)
                value = (mine, value)
            else:
                token, mine = take_columns(here, local_rows, start, width, after)
                value = (mine, lax.ppermute(token, "group", swap))
        elif step == 1 and direct:
            token = sum_for_owners(slab_of, *value, after)
            value = over_devices(token)
        elif step == 1:
            parts = sum_and_pack(to_ids, *value, slots, after)
            token, value = parts[0], over_planes(parts)
        elif step == 2:
            parts = pack_for_owners(here, owner_pos, value, inside, capacity, after)
            token = parts[0]
            value = in_plane(parts)
        elif step == 3 and direct:
            *state, token = update_owned(here, my_used, value, anchor, moment, start, state, after)
            value = over_devices(token)
        elif step == 3:
            first, second, *parts = update_chunk(
                here, my_used, value, anchor, moment, start, state, after
            )
            state, token, value = (first, second), parts[0], in_plane(parts)
        elif step == 4:
            parts = pack_for_planes(here, owner_pos, owner_used, value, slots, after)
            token, value = parts[0], over_planes(parts)
        elif step == 5:
            if direct:
                token = unpack_owned(slab_owner, slot_index, value, after)
            else:
                token = unpack(from_ids, from_counts, value, slab_owner.shape[0], after)
            value = (token, lax.ppermute(token, "group", swap))
        else:
            new_rows = (place(here, *value, start, local_rows.shape, new_rows, after),)
        held[chunk] = value
        after = (token,)
    while isinstance(new_embed, jax.Array):
        new_embed = embed.send(after)
    return (*state, *new_rows, *new_embed)


def on_device(
    replica_weights,
    anchor_slabs,
    momentum_slabs,
    slab_owner,
    replica_embed,
    anchor_embed,
    momentum_embed,
    embed_basis,
):
    slab_count = slab_owner.shape[0]
    devices = lax.axis_size("shard")
    capacity = anchor_slabs.shape[1]
    inside = devices // PLANES
    device_here = lax.axis_index("shard")
    plane, place_here = device_here // inside, device_here % inside
    here = jnp.stack([lax.axis_index("group"), plane, place_here]).astype(jnp.int32)

    order = jnp.arange(slab_count, dtype=jnp.int32)
    earlier = order[None, :] < order[:, None]
    same_owner = slab_owner[:, None] == slab_owner[None, :]
    slab_plane = slab_owner // inside
    same_plane = slab_plane[:, None] == slab_plane[None, :]
    slot_index = jnp.sum((same_owner & earlier).astype(jnp.int32), axis=1)
    position = jnp.sum((same_plane & earlier).astype(jnp.int32), axis=1)
    offsets = jnp.arange(PLANES, dtype=jnp.int32)
    places = jnp.arange(capacity * inside, dtype=jnp.int32)

    def slots_of(planes):
        held = slab_plane[None, :] == planes[:, None]
        at_place = held[:, None, :] & (position[None, None, :] == places[None, :, None])
        return (
            jnp.sum(jnp.where(at_place, order, 0), axis=2),
            jnp.sum(held.astype(jnp.int32), axis=1),
        )

    to_ids, _ = slots_of((plane + offsets) % PLANES)
    from_ids, from_counts = slots_of((plane - offsets) % PLANES)
    owners = plane * inside + (place_here ^ jnp.arange(inside, dtype=jnp.int32))
    at_owner = (slab_owner[None, None, :] == owners[:, None, None]) & (
        slot_index[None, None, :] == jnp.arange(capacity, dtype=jnp.int32)[None, :, None]
    )
    owner_pos = jnp.sum(jnp.where(at_owner, position, 0), axis=2)
    owner_used = jnp.any(at_owner, axis=2).astype(jnp.int32)
    matches = (slab_owner[None, None, :] == jnp.arange(devices, dtype=jnp.int32)[:, None, None]) & (
        slot_index[None, None, :] == jnp.arange(capacity, dtype=jnp.int32)[None, :, None]
    )
    slab_of = jnp.sum(jnp.where(matches, order, 0), axis=2)
    tables = (
        here, to_ids, from_ids, from_counts, owner_pos, owner_used, owner_used[0], slab_of, slab_owner, slot_index
    )

    most = capacity * inside
    fewer = most * 3 // 4
    operands = (
        tables,
        replica_weights[0],
        anchor_slabs[0],
        momentum_slabs[0],
        replica_embed[0],
        anchor_embed,
        momentum_embed,
        embed_basis,
    )
    results = lax.cond(
        jnp.max(from_counts) <= fewer,
        lambda *values: moved(fewer, *values),
        lambda *values: moved(most, *values),
        *operands,
    )
    return tuple(
        value[None] if index not in (3, 4) else value for index, value in enumerate(results)
    )


def solution(mesh):
    in_specs = (
        P("group", None, "shard", None),
        P("shard", None, None, "group"),
        P("shard", None, None, "group"),
        P(),
        P("group", "shard", None),
        P("shard", None),
        P("shard", None),
        P("shard", None),
    )
    out_specs = (
        P("shard", None, None, "group"),
        P("shard", None, None, "group"),
        P("group", None, "shard", None),
        P("shard", None),
        P("shard", None),
        P("group", "shard", None),
    )
    return jax.shard_map(
        on_device, mesh=mesh, in_specs=in_specs, out_specs=out_specs, check_vma=False
    )
```

time: 449 us -> 142 us (0.32)
  waiting for transfers between devices: 288 us -> 43.1 us
  blocking collectives: 99.4 us -> 0 us
  starting transfers between devices: 5.94 us -> 60.7 us
  Pallas kernels: 0 us -> 27.4 us
  local copies, waits for them, and re-layouts: 19.7 us -> 1.42 us
  between operations: 15.6 us -> 1.32 us
  other arithmetic: 17.6 us -> 7.27 us
    psum x1 -> x0, waiting for transfers between devices: 176 us -> none  [on_device(): embed_factor = lax.psum(partial_factor, ('group', 'shard'))]
    all_to_all x1 -> x0, blocking collectives: 99.4 us -> none  [on_device(): lax.all_to_all(jnp.where(send_used[:, :, None, None], picked, jnp.zeros((...]
    ppermute x0 -> x47, starting transfers between devices: none -> 60.7 us  [the longest x18 35.8 us: over_planes(): lax.ppermute(parts[k], 'shard', [(i, (i + k * inside) % devices) for i in...]
    all_gather x1 -> x0, waiting for transfers between devices: 56.9 us -> none  [on_device(): full_cols = lax.all_gather(new_half, 'group', axis=2, tiled=True)]
    reduce_scatter x1 -> x0, waiting for transfers between devices: 54.8 us -> none  [on_device(): lax.psum_scatter(gathered.astype(jnp.float32).astype(jnp.bfloat16), 'grou...]
    ppermute x0 -> x47, waiting for transfers between devices: none -> 43.1 us  [the longest x18 20.9 us: over_planes(): lax.ppermute(parts[k], 'shard', [(i, (i + k * inside) % devices) for i in...]
    pallas_call x0 -> x27, Pallas kernels: none -> 27.4 us  [call(): pl.pallas_call(body, grid_spec=pltpu.PrefetchScalarGridSpec(num_scalar_pr...]
    convert_element_type x1 -> x2, other arithmetic: 9.8 us -> 0.6 us  [the longest x1 0.53 us: on_device(): owner_used = jnp.any(at_owner, axis=2).astype(jnp.int32)]
  transfers between devices with their start and end apart: 4 -> 47, of which waited for: 3 -> 14; matrix products, arithmetic and copies ran while one was open for 1% -> 2% of each run, Pallas kernels for 0% -> 17%
where the time goes in v2:
time: 142 us
  starting transfers between devices  60.7 us (43%)
  waiting for transfers between devices  43.1 us (30%)
  Pallas kernels  27.4 us (19%)
  other arithmetic  7.27 us (5%)
  local copies, waits for them, and re-layouts  1.42 us (1%)
    ppermute x18, starting transfers between devices, over_planes(): lax.ppermute(parts[k], 'shard', [(i, (i + k * inside) % devices) for i in...  35.8 us
    pallas_call x27, Pallas kernels, call(): pl.pallas_call(body, grid_spec=pltpu.PrefetchScalarGridSpec(num_scalar_pr...  27.4 us
    ppermute x18, waiting for transfers between devices, over_planes(): lax.ppermute(parts[k], 'shard', [(i, (i + k * inside) % devices) for i in...  20.9 us
    ppermute x18, starting transfers between devices, in_plane(): lax.ppermute(parts[m], 'shard', [(i, i ^ m) for i in range(devices)])  11.1 us
    ppermute x4, waiting for transfers between devices, embed_steps(): other = lax.ppermute(factor, 'shard', pairs)  8.35 us
    ppermute x3, waiting for transfers between devices, moved(): value = (token, lax.ppermute(token, 'group', swap))  7.52 us
    ppermute x18, waiting for transfers between devices, in_plane(): lax.ppermute(parts[m], 'shard', [(i, i ^ m) for i in range(devices)])  6.28 us
    ppermute x3, starting transfers between devices, moved(): value = (token, lax.ppermute(token, 'group', swap))  3.65 us
  transfers between devices with their start and end apart: 47, of which 14 were waited for; matrix products, arithmetic and copies ran while one was open for 2% of the time, Pallas kernels for 17%

profile of v2, /device:TPU:0, one launch (start us, length us, event | category | flops | bytes accessed | tf_op | source)
XLA Modules:
  0.0 141.8 jit_solution(10212528552224640428)
XLA Ops:
  5.3 136.5 %conditional.1 = (f32[2,512,1024]{2,1,0:T(8,128)}, f32[2,512,1024]{2,1,0:T(8,128)}, f32[48,512]{1,0:T(8,128)}, f32[48,512]{1,0:T(8,128)}, bf16[48,512]{1,0:T(8,128)(2,1)}, /*index=5*/bf16[1,16,32,2048]{3,2,1,0:T(8,128)(2,1)}) conditional(s32[]{:T(128)} %convert_element_type.16, (s32[4,2]{0,1:T(2,128)}, s32[16,16]{1,0:T(8,128)S(1)}, ...), branch_computations={%region_4.9_spmd, %region_9.14_spmd} | conditional | flops 3829 | bytes 79799848 | solution.py:587
  6.6 3.0 %collective-permute-start.48 = (bf16[16,32,256]{2,1,0:T(8,128)(2,1)S(1)}, bf16[16,32,256]{2,1,0:T(8,128)(2,1)S(1)}, u32[]{:S(2)}, u32[]{:S(2)}) collective-permute-start(bf16[16,32,256]{2,1,0:T(8,128)(2,1)S(1)} %dynamic-slice_bitcast_fusion.1.refs_1_), channel_id=1, source_target_pairs={{0,16},{16,0},{1,17},{17,1},{2,18},{18,2},{3,19},{19,3},{4,20},{20... | collective-permute-start | bytes 786440 | tf_op jit(solution)/shard_map/cond/branch_1_fun/ppermute | solution.py:481
  9.6 1.6 %take_columns.9 = (bf16[16,32,256]{2,1,0:T(8,128)(2,1)S(1)}, bf16[16,32,256]{2,1,0:T(8,128)(2,1)S(1)}) custom-call(s32[3]{0:T(128)S(1)} %get-tuple-element.298.refs_0_, bf16[16,32,256]{2,1,0:T(8,128)(2,1)S(1)} %dynamic-slice_bitcast_fusion.1.refs_1_, bf16[16,32,2048]{2,1,0:T(8,128)(2,1)} %bitcast.43), custom_call_target="tpu_custom_call" | custom-call | flops 1 | bytes 1 | tf_op jit(solution)/shard_map/cond/branch_1_fun/take_columns/pallas_call | solution.py:37
  12.0 2.1 %collective-permute-start.53 = (bf16[16,32,512]{2,1,0:T(8,128)(2,1)S(1)}, bf16[16,32,512]{2,1,0:T(8,128)(2,1)S(1)}, u32[]{:S(2)}, u32[]{:S(2)}) collective-permute-start(bf16[16,32,512]{2,1,0:T(8,128)(2,1)S(1)} %get-tuple-element.309.refs_1_), channel_id=1, source_target_pairs={{0,16},{16,0},{1,17},{17,1},{2,18},{18,2},{3,19},{19,3},{4,20},{20... | collective-permute-start | bytes 1572872 | tf_op jit(solution)/shard_map/cond/branch_1_fun/ppermute | solution.py:486
  16.4 1.6 %take_columns.11 = (bf16[16,32,256]{2,1,0:T(8,128)(2,1)S(1)}, bf16[16,32,256]{2,1,0:T(8,128)(2,1)S(1)}) custom-call(s32[3]{0:T(128)S(1)} %get-tuple-element.298.refs_0_, bf16[16,32,512]{2,1,0:T(8,128)(2,1)S(1)} %get-tuple-element.309.refs_1_, bf16[16,32,2048]{2,1,0:T(8,128)(2,1)} %bitcast.44), custom_call_target="tpu_custom_call" | custom-call | flops 1 | bytes 1 | tf_op jit(solution)/shard_map/cond/branch_1_fun/take_columns/pallas_call | solution.py:37
  19.5 2.0 %collective-permute-start.50 = (bf16[6,32,256]{2,1,0:T(8,128)(2,1)S(1)}, bf16[6,32,256]{2,1,0:T(8,128)(2,1)S(1)}, u32[]{:S(2)}, u32[]{:S(2)}) collective-permute-start(bf16[6,32,256]{2,1,0:T(8,128)(2,1)S(1)} %get-tuple-element.317), channel_id=1, source_target_pairs={{0,4},{1,5},{2,6},{3,7},{4,8},{5,9},{6,10},{7,11},{8,12},{9,13},{1... | collective-permute-start | bytes 294920 | tf_op jit(solution)/shard_map/cond/branch_1_fun/ppermute | solution.py:430
  21.4 2.6 %collective-permute-start.51 = (bf16[6,32,256]{2,1,0:T(8,128)(2,1)S(1)}, bf16[6,32,256]{2,1,0:T(8,128)(2,1)S(1)}, u32[]{:S(2)}, u32[]{:S(2)}) collective-permute-start(bf16[6,32,256]{2,1,0:T(8,128)(2,1)S(1)} %get-tuple-element.318), channel_id=1, source_target_pairs={{0,8},{1,9},{2,10},{3,11},{4,12},{5,13},{6,14},{7,15},{8,0},{9,1},... | collective-permute-start | bytes 294920 | tf_op jit(solution)/shard_map/cond/branch_1_fun/ppermute | solution.py:430
  24.0 1.3 collective-permute-start.52
  26.3 1.6 %collective-permute-start.54 = (f32[64,512]{1,0:T(8,128)S(1)}, f32[64,512]{1,0:T(8,128)S(1)}, u32[]{:S(2)}, u32[]{:S(2)}) collective-permute-start(f32[64,512]{1,0:T(8,128)S(1)} %add.95.refs_1_), channel_id=1, source_target_pairs={{0,2},{1,3},{2,0},{3,1},{4,6},{5,7},{6,4},{7,5},{8,10},{9,11},{10,... | collective-permute-start | bytes 393224 | tf_op jit(solution)/shard_map/cond/branch_1_fun/ppermute | solution.py:454
  27.9 3.3 %collective-permute-done.51.refs_4_.refs_5_ = bf16[6,32,256]{2,1,0:T(8,128)(2,1)S(1)} collective-permute-done((bf16[6,32,256]{2,1,0:T(8,128)(2,1)S(1)}, bf16[6,32,256]{2,1,0:T(8,128)(2,1)S(1)}, u32[]{:S(2)}, u32[]{:S(2)}) %collective-permute-start.51) | collective-permute-done | bytes 98336 | tf_op jit(solution)/shard_map/cond/branch_1_fun/ppermute | solution.py:430
  32.7 1.6 %collective-permute-start.56 = (bf16[2,4,32,256]{3,2,1,0:T(8,128)(2,1)S(1)}, bf16[2,4,32,256]{3,2,1,0:T(8,128)(2,1)S(1)}, u32[]{:S(2)}, u32[]{:S(2)}) collective-permute-start(bf16[2,4,32,256]{3,2,1,0:T(8,128)(2,1)S(1)} %get-tuple-element.324), channel_id=1, source_target_pairs={{0,2},{1,3},{2,0},{3,1},{4,6},{5,7},{6,4},{7,5},{8,10},{9,11},{10,... | collective-permute-start | bytes 393224 | tf_op jit(solution)/shard_map/cond/branch_1_fun/ppermute | solution.py:441
  34.3 1.5 %collective-permute-start.61 = (bf16[16,32,256]{2,1,0:T(8,128)(2,1)S(1)}, bf16[16,32,256]{2,1,0:T(8,128)(2,1)S(1)}, u32[]{:S(2)}, u32[]{:S(2)}) collective-permute-start(bf16[16,32,256]{2,1,0:T(8,128)(2,1)S(1)} %get-tuple-element.310.refs_0_), channel_id=1, source_target_pairs={{0,16},{16,0},{1,17},{17,1},{2,18},{18,2},{3,19},{19,3},{4,20},{20... | collective-permute-start | bytes 786440 | tf_op jit(solution)/shard_map/cond/branch_1_fun/ppermute | solution.py:486
  35.9 2.7 %collective-permute-start.58 = (bf16[6,32,512]{2,1,0:T(8,128)(2,1)S(1)}, bf16[6,32,512]{2,1,0:T(8,128)(2,1)S(1)}, u32[]{:S(2)}, u32[]{:S(2)}) collective-permute-start(bf16[6,32,512]{2,1,0:T(8,128)(2,1)S(1)} %get-tuple-element.329), channel_id=1, source_target_pairs={{0,4},{1,5},{2,6},{3,7},{4,8},{5,9},{6,10},{7,11},{8,12},{9,13},{1... | collective-permute-start | bytes 589832 | tf_op jit(solution)/shard_map/cond/branch_1_fun/ppermute | solution.py:430
  38.5 1.6 %collective-permute-start.59 = (bf16[6,32,512]{2,1,0:T(8,128)(2,1)S(1)}, bf16[6,32,512]{2,1,0:T(8,128)(2,1)S(1)}, u32[]{:S(2)}, u32[]{:S(2)}) collective-permute-start(bf16[6,32,512]{2,1,0:T(8,128)(2,1)S(1)} %get-tuple-element.330), channel_id=1, source_target_pairs={{0,8},{1,9},{2,10},{3,11},{4,12},{5,13},{6,14},{7,15},{8,0},{9,1},... | collective-permute-start | bytes 589832 | tf_op jit(solution)/shard_map/cond/branch_1_fun/ppermute | solution.py:430
  40.2 2.1 %collective-permute-start.60 = (bf16[6,32,512]{2,1,0:T(8,128)(2,1)S(1)}, bf16[6,32,512]{2,1,0:T(8,128)(2,1)S(1)}, u32[]{:S(2)}, u32[]{:S(2)}) collective-permute-start(bf16[6,32,512]{2,1,0:T(8,128)(2,1)S(1)} %get-tuple-element.331), channel_id=1, source_target_pairs={{0,12},{1,13},{2,14},{3,15},{4,0},{5,1},{6,2},{7,3},{8,4},{9,5},{1... | collective-permute-start | bytes 589832 | tf_op jit(solution)/shard_map/cond/branch_1_fun/ppermute | solution.py:430
  42.3 3.6 %update_chunk.9 = (f32[2,512,1024]{2,1,0:T(8,128)}, f32[2,512,1024]{2,1,0:T(8,128)}, bf16[2,4,32,256]{3,2,1,0:T(8,128)(2,1)S(1)}, bf16[2,4,32,256]{3,2,1,0:T(8,1...) custom-call(s32[3]{0:T(128)S(1)} %get-tuple-element.298.refs_0_, ...), custom_call_target="tpu_custom_call" | custom-call | flops 1 | bytes 1 | tf_op jit(solution)/shard_map/cond/branch_1_fun/update_chunk/pallas_call | solution.py:37
  46.0 2.0 %collective-permute-start.66 = (bf16[2,4,32,256]{3,2,1,0:T(8,128)(2,1)S(1)}, bf16[2,4,32,256]{3,2,1,0:T(8,128)(2,1)S(1)}, u32[]{:S(2)}, u32[]{:S(2)}) collective-permute-start(bf16[2,4,32,256]{3,2,1,0:T(8,128)(2,1)S(1)} %get-tuple-element.339), channel_id=1, source_target_pairs={{0,2},{1,3},{2,0},{3,1},{4,6},{5,7},{6,4},{7,5},{8,10},{9,11},{10,... | collective-permute-start | bytes 393224 | tf_op jit(solution)/shard_map/cond/branch_1_fun/ppermute | solution.py:441
  48.1 5.6 %collective-permute-done.59.refs_4_.refs_5_ = bf16[6,32,512]{2,1,0:T(8,128)(2,1)S(1)} collective-permute-done((bf16[6,32,512]{2,1,0:T(8,128)(2,1)S(1)}, bf16[6,32,512]{2,1,0:T(8,128)(2,1)S(1)}, u32[]{:S(2)}, u32[]{:S(2)}) %collective-permute-start.59) | collective-permute-done | bytes 196640 | tf_op jit(solution)/shard_map/cond/branch_1_fun/ppermute | solution.py:430
  55.3 4.8 %collective-permute-start.62 = (bf16[6,32,256]{2,1,0:T(8,128)(2,1)S(1)}, bf16[6,32,256]{2,1,0:T(8,128)(2,1)S(1)}, u32[]{:S(2)}, u32[]{:S(2)}) collective-permute-start(bf16[6,32,256]{2,1,0:T(8,128)(2,1)S(1)} %get-tuple-element.335), channel_id=1, source_target_pairs={{0,4},{1,5},{2,6},{3,7},{4,8},{5,9},{6,10},{7,11},{8,12},{9,13},{1... | collective-permute-start | bytes 294920 | tf_op jit(solution)/shard_map/cond/branch_1_fun/ppermute | solution.py:430
  60.1 1.6 %collective-permute-start.69 = (bf16[2,4,32,512]{3,2,1,0:T(8,128)(2,1)S(1)}, bf16[2,4,32,512]{3,2,1,0:T(8,128)(2,1)S(1)}, u32[]{:S(2)}, u32[]{:S(2)}) collective-permute-start(bf16[2,4,32,512]{3,2,1,0:T(8,128)(2,1)S(1)} %get-tuple-element.344), channel_id=1, source_target_pairs={{0,2},{1,3},{2,0},{3,1},{4,6},{5,7},{6,4},{7,5},{8,10},{9,11},{10,... | collective-permute-start | bytes 786440 | tf_op jit(solution)/shard_map/cond/branch_1_fun/ppermute | solution.py:441
  61.6 1.3 collective-permute-start.63
  63.0 1.2 collective-permute-done.62.refs_5_.refs_4_
  64.2 1.7 %collective-permute-start.64 = (bf16[6,32,256]{2,1,0:T(8,128)(2,1)S(1)}, bf16[6,32,256]{2,1,0:T(8,128)(2,1)S(1)}, u32[]{:S(2)}, u32[]{:S(2)}) collective-permute-start(bf16[6,32,256]{2,1,0:T(8,128)(2,1)S(1)} %get-tuple-element.337), channel_id=1, source_target_pairs={{0,12},{1,13},{2,14},{3,15},{4,0},{5,1},{6,2},{7,3},{8,4},{9,5},{1... | collective-permute-start | bytes 294920 | tf_op jit(solution)/shard_map/cond/branch_1_fun/ppermute | solution.py:430
  65.9 3.7 %collective-permute-done.63.refs_6_.refs_5_ = bf16[6,32,256]{2,1,0:T(8,128)(2,1)S(1)} collective-permute-done((bf16[6,32,256]{2,1,0:T(8,128)(2,1)S(1)}, bf16[6,32,256]{2,1,0:T(8,128)(2,1)S(1)}, u32[]{:S(2)}, u32[]{:S(2)}) %collective-permute-start.63) | collective-permute-done | bytes 98336 | tf_op jit(solution)/shard_map/cond/branch_1_fun/ppermute | solution.py:430
  72.2 1.5 %collective-permute-start.75 = (bf16[6,32,256]{2,1,0:T(8,128)(2,1)S(1)}, bf16[6,32,256]{2,1,0:T(8,128)(2,1)S(1)}, u32[]{:S(2)}, u32[]{:S(2)}) collective-permute-start(bf16[6,32,256]{2,1,0:T(8,128)(2,1)S(1)} %get-tuple-element.360), channel_id=1, source_target_pairs={{0,4},{1,5},{2,6},{3,7},{4,8},{5,9},{6,10},{7,11},{8,12},{9,13},{1... | collective-permute-start | bytes 294920 | tf_op jit(solution)/shard_map/cond/branch_1_fun/ppermute | solution.py:430
  73.7 1.5 %collective-permute-start.73 = (bf16[2,4,32,256]{3,2,1,0:T(8,128)(2,1)S(1)}, bf16[2,4,32,256]{3,2,1,0:T(8,128)(2,1)S(1)}, u32[]{:S(2)}, u32[]{:S(2)}) collective-permute-start(bf16[2,4,32,256]{3,2,1,0:T(8,128)(2,1)S(1)} %get-tuple-element.350), channel_id=1, source_target_pairs={{0,2},{1,3},{2,0},{3,1},{4,6},{5,7},{6,4},{7,5},{8,10},{9,11},{10,... | collective-permute-start | bytes 393224 | tf_op jit(solution)/shard_map/cond/branch_1_fun/ppermute | solution.py:441
  75.3 3.4 %update_chunk.10 = (f32[2,512,1024]{2,1,0:T(8,128)}, f32[2,512,1024]{2,1,0:T(8,128)}, bf16[2,4,32,512]{3,2,1,0:T(8,128)(2,1)S(1)}, bf16[2,4,32,512]{3,2,1,0:T(8,...) custom-call(s32[3]{0:T(128)S(1)} %get-tuple-element.298.refs_0_, ...), custom_call_target="tpu_custom_call", output_to_operand_aliasing={{0}: (9, {}), {1}: (10, {})} | custom-call | flops 1 | bytes 1 | tf_op jit(solution)/shard_map/cond/branch_1_fun/update_chunk/pallas_call | solution.py:37
  79.3 1.5 %collective-permute-start.79 = (bf16[2,4,32,512]{3,2,1,0:T(8,128)(2,1)S(1)}, bf16[2,4,32,512]{3,2,1,0:T(8,128)(2,1)S(1)}, u32[]{:S(2)}, u32[]{:S(2)}) collective-permute-start(bf16[2,4,32,512]{3,2,1,0:T(8,128)(2,1)S(1)} %get-tuple-element.364), channel_id=1, source_target_pairs={{0,2},{1,3},{2,0},{3,1},{4,6},{5,7},{6,4},{7,5},{8,10},{9,11},{10,... | collective-permute-start | bytes 786440 | tf_op jit(solution)/shard_map/cond/branch_1_fun/ppermute | solution.py:441
  80.8 1.4 collective-permute-start.76
  82.2 2.8 %collective-permute-start.77 = (bf16[6,32,256]{2,1,0:T(8,128)(2,1)S(1)}, bf16[6,32,256]{2,1,0:T(8,128)(2,1)S(1)}, u32[]{:S(2)}, u32[]{:S(2)}) collective-permute-start(bf16[6,32,256]{2,1,0:T(8,128)(2,1)S(1)} %get-tuple-element.362), channel_id=1, source_target_pairs={{0,12},{1,13},{2,14},{3,15},{4,0},{5,1},{6,2},{7,3},{8,4},{9,5},{1... | collective-permute-start | bytes 294920 | tf_op jit(solution)/shard_map/cond/branch_1_fun/ppermute | solution.py:430
  85.1 2.3 %update_chunk.11 = (f32[2,512,1024]{2,1,0:T(8,128)}, f32[2,512,1024]{2,1,0:T(8,128)}, bf16[2,4,32,256]{3,2,1,0:T(8,128)(2,1)S(1)}, bf16[2,4,32,256]{3,2,1,0:T(8,...) custom-call(s32[3]{0:T(128)S(1)} %get-tuple-element.298.refs_0_, ...), custom_call_target="tpu_custom_call", output_to_operand_aliasing={{0}: (9, {}), {1}: (10, {})} | custom-call | flops 1 | bytes 1 | tf_op jit(solution)/shard_map/cond/branch_1_fun/update_chunk/pallas_call | solution.py:37
  87.4 2.1 %collective-permute-done.76.refs_5_ = bf16[6,32,256]{2,1,0:T(8,128)(2,1)S(1)} collective-permute-done((bf16[6,32,256]{2,1,0:T(8,128)(2,1)S(1)}, bf16[6,32,256]{2,1,0:T(8,128)(2,1)S(1)}, u32[]{:S(2)}, u32[]{:S(2)}) %collective-permute-start.76) | collective-permute-done | bytes 98336 | tf_op jit(solution)/shard_map/cond/branch_1_fun/ppermute | solution.py:430
  89.5 1.5 %collective-permute-start.81 = (f32[64,512]{1,0:T(8,128)S(1)}, f32[64,512]{1,0:T(8,128)S(1)}, u32[]{:S(2)}, u32[]{:S(2)}) collective-permute-start(f32[64,512]{1,0:T(8,128)S(1)} %add.97.refs_2_.refs_1_), channel_id=1, source_target_pairs={{0,8},{1,9},{2,10},{3,11},{4,12},{5,13},{6,14},{7,15},{8,0},{9,1},... | collective-permute-start | bytes 393224 | tf_op jit(solution)/shard_map/cond/branch_1_fun/ppermute | solution.py:454
  93.2 2.3 %collective-permute-start.82 = (bf16[6,32,512]{2,1,0:T(8,128)(2,1)S(1)}, bf16[6,32,512]{2,1,0:T(8,128)(2,1)S(1)}, u32[]{:S(2)}, u32[]{:S(2)}) collective-permute-start(bf16[6,32,512]{2,1,0:T(8,128)(2,1)S(1)} %get-tuple-element.367), channel_id=1, source_target_pairs={{0,4},{1,5},{2,6},{3,7},{4,8},{5,9},{6,10},{7,11},{8,12},{9,13},{1... | collective-permute-start | bytes 589832 | tf_op jit(solution)/shard_map/cond/branch_1_fun/ppermute | solution.py:430
  96.2 1.8 %collective-permute-start.84 = (bf16[6,32,512]{2,1,0:T(8,128)(2,1)S(1)}, bf16[6,32,512]{2,1,0:T(8,128)(2,1)S(1)}, u32[]{:S(2)}, u32[]{:S(2)}) collective-permute-start(bf16[6,32,512]{2,1,0:T(8,128)(2,1)S(1)} %get-tuple-element.369), channel_id=1, source_target_pairs={{0,12},{1,13},{2,14},{3,15},{4,0},{5,1},{6,2},{7,3},{8,4},{9,5},{1... | collective-permute-start | bytes 589832 | tf_op jit(solution)/shard_map/cond/branch_1_fun/ppermute | solution.py:430
  98.1 1.5 %collective-permute-start.86 = (bf16[2,4,32,256]{3,2,1,0:T(8,128)(2,1)S(1)}, bf16[2,4,32,256]{3,2,1,0:T(8,128)(2,1)S(1)}, u32[]{:S(2)}, u32[]{:S(2)}) collective-permute-start(bf16[2,4,32,256]{3,2,1,0:T(8,128)(2,1)S(1)} %get-tuple-element.371), channel_id=1, source_target_pairs={{0,2},{1,3},{2,0},{3,1},{4,6},{5,7},{6,4},{7,5},{8,10},{9,11},{10,... | collective-permute-start | bytes 393224 | tf_op jit(solution)/shard_map/cond/branch_1_fun/ppermute | solution.py:441
  99.6 8.3 %collective-permute-done.81.refs_2_ = f32[64,512]{1,0:T(8,128)S(1)} collective-permute-done((f32[64,512]{1,0:T(8,128)S(1)}, f32[64,512]{1,0:T(8,128)S(1)}, u32[]{:S(2)}, u32[]{:S(2)}) %collective-permute-start.81) | collective-permute-done | bytes 131104 | tf_op jit(solution)/shard_map/cond/branch_1_fun/ppermute | solution.py:454
  108.3 5.4 %collective-permute-done.87.refs_11_ = bf16[2,4,32,256]{3,2,1,0:T(8,128)(2,1)S(1)} collective-permute-done((bf16[2,4,32,256]{3,2,1,0:T(8,128)(2,1)S(1)}, bf16[2,4,32,256]{3,2,1,0:T(8,128)(2,1)S(1)}, u32[]{:S(2)}, u32[]{:S(2)}) %collective-permute-start.87) | collective-permute-done | bytes 131104 | tf_op jit(solution)/shard_map/cond/branch_1_fun/ppermute | solution.py:441
  115.8 2.8 %collective-permute-start.88 = (bf16[6,32,256]{2,1,0:T(8,128)(2,1)S(1)}, bf16[6,32,256]{2,1,0:T(8,128)(2,1)S(1)}, u32[]{:S(2)}, u32[]{:S(2)}) collective-permute-start(bf16[6,32,256]{2,1,0:T(8,128)(2,1)S(1)} %get-tuple-element.378), channel_id=1, source_target_pairs={{0,4},{1,5},{2,6},{3,7},{4,8},{5,9},{6,10},{7,11},{8,12},{9,13},{1... | collective-permute-start | bytes 294920 | tf_op jit(solution)/shard_map/cond/branch_1_fun/ppermute | solution.py:430
  118.6 1.6 %collective-permute-start.89 = (bf16[6,32,256]{2,1,0:T(8,128)(2,1)S(1)}, bf16[6,32,256]{2,1,0:T(8,128)(2,1)S(1)}, u32[]{:S(2)}, u32[]{:S(2)}) collective-permute-start(bf16[6,32,256]{2,1,0:T(8,128)(2,1)S(1)} %get-tuple-element.379), channel_id=1, source_target_pairs={{0,8},{1,9},{2,10},{3,11},{4,12},{5,13},{6,14},{7,15},{8,0},{9,1},... | collective-permute-start | bytes 294920 | tf_op jit(solution)/shard_map/cond/branch_1_fun/ppermute | solution.py:430
  121.0 1.5 %collective-permute-start.93 = (bf16[16,32,256]{2,1,0:T(8,128)(2,1)S(1)}, bf16[16,32,256]{2,1,0:T(8,128)(2,1)S(1)}, u32[]{:S(2)}, u32[]{:S(2)}) collective-permute-start(bf16[16,32,256]{2,1,0:T(8,128)(2,1)S(1)} %unpack.9.refs_3_.refs_2_), channel_id=1, source_target_pairs={{0,16},{16,0},{1,17},{17,1},{2,18},{18,2},{3,19},{19,3},{4,20},{20... | collective-permute-start | bytes 786440 | tf_op jit(solution)/shard_map/cond/branch_1_fun/ppermute | solution.py:513
  123.4 3.3 %collective-permute-done.89.refs_5_ = bf16[6,32,256]{2,1,0:T(8,128)(2,1)S(1)} collective-permute-done((bf16[6,32,256]{2,1,0:T(8,128)(2,1)S(1)}, bf16[6,32,256]{2,1,0:T(8,128)(2,1)S(1)}, u32[]{:S(2)}, u32[]{:S(2)}) %collective-permute-start.89) | collective-permute-done | bytes 98336 | tf_op jit(solution)/shard_map/cond/branch_1_fun/ppermute | solution.py:430
  127.5 1.6 %collective-permute-start.91 = (bf16[16,32,256]{2,1,0:T(8,128)(2,1)S(1)}, bf16[16,32,256]{2,1,0:T(8,128)(2,1)S(1)}, u32[]{:S(2)}, u32[]{:S(2)}) collective-permute-start(bf16[16,32,256]{2,1,0:T(8,128)(2,1)S(1)} %unpack.11.refs_1_.refs_2_), channel_id=1, source_target_pairs={{0,16},{16,0},{1,17},{17,1},{2,18},{18,2},{3,19},{19,3},{4,20},{20... | collective-permute-start | bytes 786440 | tf_op jit(solution)/shard_map/cond/branch_1_fun/ppermute | solution.py:513
  130.0 5.7 %collective-permute-done.93.refs_3_ = bf16[16,32,256]{2,1,0:T(8,128)(2,1)S(1)} collective-permute-done((bf16[16,32,256]{2,1,0:T(8,128)(2,1)S(1)}, bf16[16,32,256]{2,1,0:T(8,128)(2,1)S(1)}, u32[]{:S(2)}, u32[]{:S(2)}) %collective-permute-start.93) | collective-permute-done | bytes 262176 | tf_op jit(solution)/shard_map/cond/branch_1_fun/ppermute | solution.py:513
  135.7 1.3 place.9.refs_4_
  137.0 1.5 %place.10.refs_4_ = bf16[16,32,2048]{2,1,0:T(8,128)(2,1)} custom-call(s32[3]{0:T(128)S(1)} %get-tuple-element.298.refs_0_, bf16[16,32,256]{2,1,0:T(8,128)(2,1)S(1)} %unpack.11.refs_1_.refs_2_, bf16[16,32,512]{2,1,0:T(8,128)(2,1)S(1)} %unpack.10.refs_0_.refs_2_.refs_1_, ...), custom_call_target="tpu_custom_call", output_to_operand_aliasing={{}: (4, {})} | custom-call | flops 1 | bytes 1 | tf_op jit(solution)/shard_map/cond/branch_1_fun/place/pallas_call | solution.py:37
  138.6 1.9 %collective-permute-done.91.refs_3_ = bf16[16,32,256]{2,1,0:T(8,128)(2,1)S(1)} collective-permute-done((bf16[16,32,256]{2,1,0:T(8,128)(2,1)S(1)}, bf16[16,32,256]{2,1,0:T(8,128)(2,1)S(1)}, u32[]{:S(2)}, u32[]{:S(2)}) %collective-permute-start.91) | collective-permute-done | bytes 262176 | tf_op jit(solution)/shard_map/cond/branch_1_fun/ppermute | solution.py:513
  140.4 1.3 place.11
  (135 shorter events, 25.9 us)
Async XLA Ops:
  6.6 12.1 %collective-permute-start.48 = (bf16[16,32,256]{2,1,0:T(8,128)(2,1)S(1)}, bf16[16,32,256]{2,1,0:T(8,128)(2,1)S(1)}, u32[]{:S(2)}, u32[]{:S(2)}) collective-permute-start(bf16[16,32,256]{2,1,0:T(8,128)(2,1)S(1)} %dynamic-slice_bitcast_fusion.1.refs_1_), channel_id=1, source_target_pairs={{0,16},{16,0},{1,17},{17,1},{2,18},{18,2},{3,19},{19,3},{4,20},{20... | collective-permute-start | bytes 786440 | tf_op jit(solution)/shard_map/cond/branch_1_fun/ppermute | solution.py:481
  11.2 6.7 %collective-permute-start.47 = (bf16[48,512]{1,0:T(8,128)(2,1)}, bf16[48,512]{1,0:T(8,128)(2,1)S(1)}, u32[]{:S(2)}, u32[]{:S(2)}) collective-permute-start(bf16[48,512]{1,0:T(8,128)(2,1)} %bitcast.49), channel_id=1, source_target_pairs={{0,16},{16,0},{1,17},{17,1},{2,18},{18,2},{3,19},{19,3},{4,20},{20... | collective-permute-start | bytes 147464 | tf_op jit(solution)/shard_map/cond/branch_1_fun/ppermute | solution.py:448
  12.0 19.1 %collective-permute-start.53 = (bf16[16,32,512]{2,1,0:T(8,128)(2,1)S(1)}, bf16[16,32,512]{2,1,0:T(8,128)(2,1)S(1)}, u32[]{:S(2)}, u32[]{:S(2)}) collective-permute-start(bf16[16,32,512]{2,1,0:T(8,128)(2,1)S(1)} %get-tuple-element.309.refs_1_), channel_id=1, source_target_pairs={{0,16},{16,0},{1,17},{17,1},{2,18},{18,2},{3,19},{19,3},{4,20},{20... | collective-permute-start | bytes 1572872 | tf_op jit(solution)/shard_map/cond/branch_1_fun/ppermute | solution.py:486
  18.3 7.9 %collective-permute-start.49 = (f32[64,512]{1,0:T(8,128)S(1)}, f32[64,512]{1,0:T(8,128)S(1)}, u32[]{:S(2)}, u32[]{:S(2)}) collective-permute-start(f32[64,512]{1,0:T(8,128)S(1)} %project_embed.3.refs_1_), channel_id=1, source_target_pairs={{0,1},{1,0},{2,3},{3,2},{4,5},{5,4},{6,7},{7,6},{8,9},{9,8},{10,11... | collective-permute-start | bytes 393224 | tf_op jit(solution)/shard_map/cond/branch_1_fun/ppermute | solution.py:454
  19.5 8.4 %collective-permute-start.50 = (bf16[6,32,256]{2,1,0:T(8,128)(2,1)S(1)}, bf16[6,32,256]{2,1,0:T(8,128)(2,1)S(1)}, u32[]{:S(2)}, u32[]{:S(2)}) collective-permute-start(bf16[6,32,256]{2,1,0:T(8,128)(2,1)S(1)} %get-tuple-element.317), channel_id=1, source_target_pairs={{0,4},{1,5},{2,6},{3,7},{4,8},{5,9},{6,10},{7,11},{8,12},{9,13},{1... | collective-permute-start | bytes 294920 | tf_op jit(solution)/shard_map/cond/branch_1_fun/ppermute | solution.py:430
  21.4 9.8 %collective-permute-start.51 = (bf16[6,32,256]{2,1,0:T(8,128)(2,1)S(1)}, bf16[6,32,256]{2,1,0:T(8,128)(2,1)S(1)}, u32[]{:S(2)}, u32[]{:S(2)}) collective-permute-start(bf16[6,32,256]{2,1,0:T(8,128)(2,1)S(1)} %get-tuple-element.318), channel_id=1, source_target_pairs={{0,8},{1,9},{2,10},{3,11},{4,12},{5,13},{6,14},{7,15},{8,0},{9,1},... | collective-permute-start | bytes 294920 | tf_op jit(solution)/shard_map/cond/branch_1_fun/ppermute | solution.py:430
  24.0 7.2 %collective-permute-start.52 = (bf16[6,32,256]{2,1,0:T(8,128)(2,1)S(1)}, bf16[6,32,256]{2,1,0:T(8,128)(2,1)S(1)}, u32[]{:S(2)}, u32[]{:S(2)}) collective-permute-start(bf16[6,32,256]{2,1,0:T(8,128)(2,1)S(1)} %get-tuple-element.319), channel_id=1, source_target_pairs={{0,12},{1,13},{2,14},{3,15},{4,0},{5,1},{6,2},{7,3},{8,4},{9,5},{1... | collective-permute-start | bytes 294920 | tf_op jit(solution)/shard_map/cond/branch_1_fun/ppermute | solution.py:430
  26.3 9.6 %collective-permute-start.54 = (f32[64,512]{1,0:T(8,128)S(1)}, f32[64,512]{1,0:T(8,128)S(1)}, u32[]{:S(2)}, u32[]{:S(2)}) collective-permute-start(f32[64,512]{1,0:T(8,128)S(1)} %add.95.refs_1_), channel_id=1, source_target_pairs={{0,2},{1,3},{2,0},{3,1},{4,6},{5,7},{6,4},{7,5},{8,10},{9,11},{10,... | collective-permute-start | bytes 393224 | tf_op jit(solution)/shard_map/cond/branch_1_fun/ppermute | solution.py:454
  32.6 5.9 %collective-permute-start.55 = (bf16[2,4,32,256]{3,2,1,0:T(8,128)(2,1)S(1)}, bf16[2,4,32,256]{3,2,1,0:T(8,128)(2,1)S(1)}, u32[]{:S(2)}, u32[]{:S(2)}) collective-permute-start(bf16[2,4,32,256]{3,2,1,0:T(8,128)(2,1)S(1)} %get-tuple-element.323), channel_id=1, source_target_pairs={{0,1},{1,0},{2,3},{3,2},{4,5},{5,4},{6,7},{7,6},{8,9},{9,8},{10,11... | collective-permute-start | bytes 393224 | tf_op jit(solution)/shard_map/cond/branch_1_fun/ppermute | solution.py:441
  32.7 7.5 %collective-permute-start.56 = (bf16[2,4,32,256]{3,2,1,0:T(8,128)(2,1)S(1)}, bf16[2,4,32,256]{3,2,1,0:T(8,128)(2,1)S(1)}, u32[]{:S(2)}, u32[]{:S(2)}) collective-permute-start(bf16[2,4,32,256]{3,2,1,0:T(8,128)(2,1)S(1)} %get-tuple-element.324), channel_id=1, source_target_pairs={{0,2},{1,3},{2,0},{3,1},{4,6},{5,7},{6,4},{7,5},{8,10},{9,11},{10,... | collective-permute-start | bytes 393224 | tf_op jit(solution)/shard_map/cond/branch_1_fun/ppermute | solution.py:441
  34.3 11.7 %collective-permute-start.61 = (bf16[16,32,256]{2,1,0:T(8,128)(2,1)S(1)}, bf16[16,32,256]{2,1,0:T(8,128)(2,1)S(1)}, u32[]{:S(2)}, u32[]{:S(2)}) collective-permute-start(bf16[16,32,256]{2,1,0:T(8,128)(2,1)S(1)} %get-tuple-element.310.refs_0_), channel_id=1, source_target_pairs={{0,16},{16,0},{1,17},{17,1},{2,18},{18,2},{3,19},{19,3},{4,20},{20... | collective-permute-start | bytes 786440 | tf_op jit(solution)/shard_map/cond/branch_1_fun/ppermute | solution.py:486
  35.9 6.4 %collective-permute-start.57 = (bf16[2,4,32,256]{3,2,1,0:T(8,128)(2,1)S(1)}, bf16[2,4,32,256]{3,2,1,0:T(8,128)(2,1)S(1)}, u32[]{:S(2)}, u32[]{:S(2)}) collective-permute-start(bf16[2,4,32,256]{3,2,1,0:T(8,128)(2,1)S(1)} %get-tuple-element.325), channel_id=1, source_target_pairs={{0,3},{1,2},{2,1},{3,0},{4,7},{5,6},{6,5},{7,4},{8,11},{9,10},{10,... | collective-permute-start | bytes 393224 | tf_op jit(solution)/shard_map/cond/branch_1_fun/ppermute | solution.py:441
  35.9 12.1 %collective-permute-start.58 = (bf16[6,32,512]{2,1,0:T(8,128)(2,1)S(1)}, bf16[6,32,512]{2,1,0:T(8,128)(2,1)S(1)}, u32[]{:S(2)}, u32[]{:S(2)}) collective-permute-start(bf16[6,32,512]{2,1,0:T(8,128)(2,1)S(1)} %get-tuple-element.329), channel_id=1, source_target_pairs={{0,4},{1,5},{2,6},{3,7},{4,8},{5,9},{6,10},{7,11},{8,12},{9,13},{1... | collective-permute-start | bytes 589832 | tf_op jit(solution)/shard_map/cond/branch_1_fun/ppermute | solution.py:430
  38.5 15.2 %collective-permute-start.59 = (bf16[6,32,512]{2,1,0:T(8,128)(2,1)S(1)}, bf16[6,32,512]{2,1,0:T(8,128)(2,1)S(1)}, u32[]{:S(2)}, u32[]{:S(2)}) collective-permute-start(bf16[6,32,512]{2,1,0:T(8,128)(2,1)S(1)} %get-tuple-element.330), channel_id=1, source_target_pairs={{0,8},{1,9},{2,10},{3,11},{4,12},{5,13},{6,14},{7,15},{8,0},{9,1},... | collective-permute-start | bytes 589832 | tf_op jit(solution)/shard_map/cond/branch_1_fun/ppermute | solution.py:430
  40.2 13.6 %collective-permute-start.60 = (bf16[6,32,512]{2,1,0:T(8,128)(2,1)S(1)}, bf16[6,32,512]{2,1,0:T(8,128)(2,1)S(1)}, u32[]{:S(2)}, u32[]{:S(2)}) collective-permute-start(bf16[6,32,512]{2,1,0:T(8,128)(2,1)S(1)} %get-tuple-element.331), channel_id=1, source_target_pairs={{0,12},{1,13},{2,14},{3,15},{4,0},{5,1},{6,2},{7,3},{8,4},{9,5},{1... | collective-permute-start | bytes 589832 | tf_op jit(solution)/shard_map/cond/branch_1_fun/ppermute | solution.py:430
  46.0 14.1 %collective-permute-start.65 = (bf16[2,4,32,256]{3,2,1,0:T(8,128)(2,1)S(1)}, bf16[2,4,32,256]{3,2,1,0:T(8,128)(2,1)S(1)}, u32[]{:S(2)}, u32[]{:S(2)}) collective-permute-start(bf16[2,4,32,256]{3,2,1,0:T(8,128)(2,1)S(1)} %get-tuple-element.338), channel_id=1, source_target_pairs={{0,1},{1,0},{2,3},{3,2},{4,5},{5,4},{6,7},{7,6},{8,9},{9,8},{10,11... | collective-permute-start | bytes 393224 | tf_op jit(solution)/shard_map/cond/branch_1_fun/ppermute | solution.py:441
  46.0 15.7 %collective-permute-start.66 = (bf16[2,4,32,256]{3,2,1,0:T(8,128)(2,1)S(1)}, bf16[2,4,32,256]{3,2,1,0:T(8,128)(2,1)S(1)}, u32[]{:S(2)}, u32[]{:S(2)}) collective-permute-start(bf16[2,4,32,256]{3,2,1,0:T(8,128)(2,1)S(1)} %get-tuple-element.339), channel_id=1, source_target_pairs={{0,2},{1,3},{2,0},{3,1},{4,6},{5,7},{6,4},{7,5},{8,10},{9,11},{10,... | collective-permute-start | bytes 393224 | tf_op jit(solution)/shard_map/cond/branch_1_fun/ppermute | solution.py:441
  48.0 13.6 %collective-permute-start.67 = (bf16[2,4,32,256]{3,2,1,0:T(8,128)(2,1)S(1)}, bf16[2,4,32,256]{3,2,1,0:T(8,128)(2,1)S(1)}, u32[]{:S(2)}, u32[]{:S(2)}) collective-permute-start(bf16[2,4,32,256]{3,2,1,0:T(8,128)(2,1)S(1)} %get-tuple-element.340), channel_id=1, source_target_pairs={{0,3},{1,2},{2,1},{3,0},{4,7},{5,6},{6,5},{7,4},{8,11},{9,10},{10,... | collective-permute-start | bytes 393224 | tf_op jit(solution)/shard_map/cond/branch_1_fun/ppermute | solution.py:441
  55.2 17.0 %collective-permute-start.68 = (bf16[2,4,32,512]{3,2,1,0:T(8,128)(2,1)S(1)}, bf16[2,4,32,512]{3,2,1,0:T(8,128)(2,1)S(1)}, u32[]{:S(2)}, u32[]{:S(2)}) collective-permute-start(bf16[2,4,32,512]{3,2,1,0:T(8,128)(2,1)S(1)} %get-tuple-element.343), channel_id=1, source_target_pairs={{0,1},{1,0},{2,3},{3,2},{4,5},{5,4},{6,7},{7,6},{8,9},{9,8},{10,11... | collective-permute-start | bytes 786440 | tf_op jit(solution)/shard_map/cond/branch_1_fun/ppermute | solution.py:441
  55.3 8.9 %collective-permute-start.62 = (bf16[6,32,256]{2,1,0:T(8,128)(2,1)S(1)}, bf16[6,32,256]{2,1,0:T(8,128)(2,1)S(1)}, u32[]{:S(2)}, u32[]{:S(2)}) collective-permute-start(bf16[6,32,256]{2,1,0:T(8,128)(2,1)S(1)} %get-tuple-element.335), channel_id=1, source_target_pairs={{0,4},{1,5},{2,6},{3,7},{4,8},{5,9},{6,10},{7,11},{8,12},{9,13},{1... | collective-permute-start | bytes 294920 | tf_op jit(solution)/shard_map/cond/branch_1_fun/ppermute | solution.py:430
  60.1 13.6 %collective-permute-start.69 = (bf16[2,4,32,512]{3,2,1,0:T(8,128)(2,1)S(1)}, bf16[2,4,32,512]{3,2,1,0:T(8,128)(2,1)S(1)}, u32[]{:S(2)}, u32[]{:S(2)}) collective-permute-start(bf16[2,4,32,512]{3,2,1,0:T(8,128)(2,1)S(1)} %get-tuple-element.344), channel_id=1, source_target_pairs={{0,2},{1,3},{2,0},{3,1},{4,6},{5,7},{6,4},{7,5},{8,10},{9,11},{10,... | collective-permute-start | bytes 786440 | tf_op jit(solution)/shard_map/cond/branch_1_fun/ppermute | solution.py:441
  61.6 13.6 %collective-permute-start.70 = (bf16[2,4,32,512]{3,2,1,0:T(8,128)(2,1)S(1)}, bf16[2,4,32,512]{3,2,1,0:T(8,128)(2,1)S(1)}, u32[]{:S(2)}, u32[]{:S(2)}) collective-permute-start(bf16[2,4,32,512]{3,2,1,0:T(8,128)(2,1)S(1)} %get-tuple-element.345), channel_id=1, source_target_pairs={{0,3},{1,2},{2,1},{3,0},{4,7},{5,6},{6,5},{7,4},{8,11},{9,10},{10,... | collective-permute-start | bytes 786440 | tf_op jit(solution)/shard_map/cond/branch_1_fun/ppermute | solution.py:441
  61.6 7.9 %collective-permute-start.63 = (bf16[6,32,256]{2,1,0:T(8,128)(2,1)S(1)}, bf16[6,32,256]{2,1,0:T(8,128)(2,1)S(1)}, u32[]{:S(2)}, u32[]{:S(2)}) collective-permute-start(bf16[6,32,256]{2,1,0:T(8,128)(2,1)S(1)} %get-tuple-element.336), channel_id=1, source_target_pairs={{0,8},{1,9},{2,10},{3,11},{4,12},{5,13},{6,14},{7,15},{8,0},{9,1},... | collective-permute-start | bytes 294920 | tf_op jit(solution)/shard_map/cond/branch_1_fun/ppermute | solution.py:430
  64.2 6.6 %collective-permute-start.64 = (bf16[6,32,256]{2,1,0:T(8,128)(2,1)S(1)}, bf16[6,32,256]{2,1,0:T(8,128)(2,1)S(1)}, u32[]{:S(2)}, u32[]{:S(2)}) collective-permute-start(bf16[6,32,256]{2,1,0:T(8,128)(2,1)S(1)} %get-tuple-element.337), channel_id=1, source_target_pairs={{0,12},{1,13},{2,14},{3,15},{4,0},{5,1},{6,2},{7,3},{8,4},{9,5},{1... | collective-permute-start | bytes 294920 | tf_op jit(solution)/shard_map/cond/branch_1_fun/ppermute | solution.py:430
  69.6 9.2 %collective-permute-start.71 = (f32[64,512]{1,0:T(8,128)S(1)}, f32[64,512]{1,0:T(8,128)S(1)}, u32[]{:S(2)}, u32[]{:S(2)}) collective-permute-start(f32[64,512]{1,0:T(8,128)S(1)} %add.96.refs_2_.refs_1_), channel_id=1, source_target_pairs={{0,4},{1,5},{2,6},{3,7},{4,0},{5,1},{6,2},{7,3},{8,12},{9,13},{10,... | collective-permute-start | bytes 393224 | tf_op jit(solution)/shard_map/cond/branch_1_fun/ppermute | solution.py:454
  72.1 8.7 %collective-permute-start.72 = (bf16[2,4,32,256]{3,2,1,0:T(8,128)(2,1)S(1)}, bf16[2,4,32,256]{3,2,1,0:T(8,128)(2,1)S(1)}, u32[]{:S(2)}, u32[]{:S(2)}) collective-permute-start(bf16[2,4,32,256]{3,2,1,0:T(8,128)(2,1)S(1)} %get-tuple-element.349), channel_id=1, source_target_pairs={{0,1},{1,0},{2,3},{3,2},{4,5},{5,4},{6,7},{7,6},{8,9},{9,8},{10,11... | collective-permute-start | bytes 393224 | tf_op jit(solution)/shard_map/cond/branch_1_fun/ppermute | solution.py:441
  72.2 7.1 %collective-permute-start.75 = (bf16[6,32,256]{2,1,0:T(8,128)(2,1)S(1)}, bf16[6,32,256]{2,1,0:T(8,128)(2,1)S(1)}, u32[]{:S(2)}, u32[]{:S(2)}) collective-permute-start(bf16[6,32,256]{2,1,0:T(8,128)(2,1)S(1)} %get-tuple-element.360), channel_id=1, source_target_pairs={{0,4},{1,5},{2,6},{3,7},{4,8},{5,9},{6,10},{7,11},{8,12},{9,13},{1... | collective-permute-start | bytes 294920 | tf_op jit(solution)/shard_map/cond/branch_1_fun/ppermute | solution.py:430
  73.7 7.1 %collective-permute-start.73 = (bf16[2,4,32,256]{3,2,1,0:T(8,128)(2,1)S(1)}, bf16[2,4,32,256]{3,2,1,0:T(8,128)(2,1)S(1)}, u32[]{:S(2)}, u32[]{:S(2)}) collective-permute-start(bf16[2,4,32,256]{3,2,1,0:T(8,128)(2,1)S(1)} %get-tuple-element.350), channel_id=1, source_target_pairs={{0,2},{1,3},{2,0},{3,1},{4,6},{5,7},{6,4},{7,5},{8,10},{9,11},{10,... | collective-permute-start | bytes 393224 | tf_op jit(solution)/shard_map/cond/branch_1_fun/ppermute | solution.py:441
  75.2 7.0 %collective-permute-start.74 = (bf16[2,4,32,256]{3,2,1,0:T(8,128)(2,1)S(1)}, bf16[2,4,32,256]{3,2,1,0:T(8,128)(2,1)S(1)}, u32[]{:S(2)}, u32[]{:S(2)}) collective-permute-start(bf16[2,4,32,256]{3,2,1,0:T(8,128)(2,1)S(1)} %get-tuple-element.351), channel_id=1, source_target_pairs={{0,3},{1,2},{2,1},{3,0},{4,7},{5,6},{6,5},{7,4},{8,11},{9,10},{10,... | collective-permute-start | bytes 393224 | tf_op jit(solution)/shard_map/cond/branch_1_fun/ppermute | solution.py:441
  78.7 12.9 %collective-permute-start.78 = (bf16[2,4,32,512]{3,2,1,0:T(8,128)(2,1)S(1)}, bf16[2,4,32,512]{3,2,1,0:T(8,128)(2,1)S(1)}, u32[]{:S(2)}, u32[]{:S(2)}) collective-permute-start(bf16[2,4,32,512]{3,2,1,0:T(8,128)(2,1)S(1)} %get-tuple-element.363), channel_id=1, source_target_pairs={{0,1},{1,0},{2,3},{3,2},{4,5},{5,4},{6,7},{7,6},{8,9},{9,8},{10,11... | collective-permute-start | bytes 786440 | tf_op jit(solution)/shard_map/cond/branch_1_fun/ppermute | solution.py:441
  79.3 12.4 %collective-permute-start.79 = (bf16[2,4,32,512]{3,2,1,0:T(8,128)(2,1)S(1)}, bf16[2,4,32,512]{3,2,1,0:T(8,128)(2,1)S(1)}, u32[]{:S(2)}, u32[]{:S(2)}) collective-permute-start(bf16[2,4,32,512]{3,2,1,0:T(8,128)(2,1)S(1)} %get-tuple-element.364), channel_id=1, source_target_pairs={{0,2},{1,3},{2,0},{3,1},{4,6},{5,7},{6,4},{7,5},{8,10},{9,11},{10,... | collective-permute-start | bytes 786440 | tf_op jit(solution)/shard_map/cond/branch_1_fun/ppermute | solution.py:441
  80.8 11.7 %collective-permute-start.80 = (bf16[2,4,32,512]{3,2,1,0:T(8,128)(2,1)S(1)}, bf16[2,4,32,512]{3,2,1,0:T(8,128)(2,1)S(1)}, u32[]{:S(2)}, u32[]{:S(2)}) collective-permute-start(bf16[2,4,32,512]{3,2,1,0:T(8,128)(2,1)S(1)} %get-tuple-element.365), channel_id=1, source_target_pairs={{0,3},{1,2},{2,1},{3,0},{4,7},{5,6},{6,5},{7,4},{8,11},{9,10},{10,... | collective-permute-start | bytes 786440 | tf_op jit(solution)/shard_map/cond/branch_1_fun/ppermute | solution.py:441
  80.8 8.7 %collective-permute-start.76 = (bf16[6,32,256]{2,1,0:T(8,128)(2,1)S(1)}, bf16[6,32,256]{2,1,0:T(8,128)(2,1)S(1)}, u32[]{:S(2)}, u32[]{:S(2)}) collective-permute-start(bf16[6,32,256]{2,1,0:T(8,128)(2,1)S(1)} %get-tuple-element.361), channel_id=1, source_target_pairs={{0,8},{1,9},{2,10},{3,11},{4,12},{5,13},{6,14},{7,15},{8,0},{9,1},... | collective-permute-start | bytes 294920 | tf_op jit(solution)/shard_map/cond/branch_1_fun/ppermute | solution.py:430
  82.2 7.3 %collective-permute-start.77 = (bf16[6,32,256]{2,1,0:T(8,128)(2,1)S(1)}, bf16[6,32,256]{2,1,0:T(8,128)(2,1)S(1)}, u32[]{:S(2)}, u32[]{:S(2)}) collective-permute-start(bf16[6,32,256]{2,1,0:T(8,128)(2,1)S(1)} %get-tuple-element.362), channel_id=1, source_target_pairs={{0,12},{1,13},{2,14},{3,15},{4,0},{5,1},{6,2},{7,3},{8,4},{9,5},{1... | collective-permute-start | bytes 294920 | tf_op jit(solution)/shard_map/cond/branch_1_fun/ppermute | solution.py:430
  87.4 41.7 %copy-start.17 = (f32[48,512]{1,0:T(8,128)S(1)}, f32[48,512]{1,0:T(8,128)}, u32[]{:S(2)}) copy-start(f32[48,512]{1,0:T(8,128)} %get-tuple-element.374.refs_4_) | copy-start | bytes 294916 | tf_op jit(solution)/shard_map/cond
  89.5 8.6 %collective-permute-start.85 = (bf16[2,4,32,256]{3,2,1,0:T(8,128)(2,1)S(1)}, bf16[2,4,32,256]{3,2,1,0:T(8,128)(2,1)S(1)}, u32[]{:S(2)}, u32[]{:S(2)}) collective-permute-start(bf16[2,4,32,256]{3,2,1,0:T(8,128)(2,1)S(1)} %get-tuple-element.370), channel_id=1, source_target_pairs={{0,1},{1,0},{2,3},{3,2},{4,5},{5,4},{6,7},{7,6},{8,9},{9,8},{10,11... | collective-permute-start | bytes 393224 | tf_op jit(solution)/shard_map/cond/branch_1_fun/ppermute | solution.py:441
  89.5 18.5 %collective-permute-start.81 = (f32[64,512]{1,0:T(8,128)S(1)}, f32[64,512]{1,0:T(8,128)S(1)}, u32[]{:S(2)}, u32[]{:S(2)}) collective-permute-start(f32[64,512]{1,0:T(8,128)S(1)} %add.97.refs_2_.refs_1_), channel_id=1, source_target_pairs={{0,8},{1,9},{2,10},{3,11},{4,12},{5,13},{6,14},{7,15},{8,0},{9,1},... | collective-permute-start | bytes 393224 | tf_op jit(solution)/shard_map/cond/branch_1_fun/ppermute | solution.py:454
  93.2 20.5 %collective-permute-start.82 = (bf16[6,32,512]{2,1,0:T(8,128)(2,1)S(1)}, bf16[6,32,512]{2,1,0:T(8,128)(2,1)S(1)}, u32[]{:S(2)}, u32[]{:S(2)}) collective-permute-start(bf16[6,32,512]{2,1,0:T(8,128)(2,1)S(1)} %get-tuple-element.367), channel_id=1, source_target_pairs={{0,4},{1,5},{2,6},{3,7},{4,8},{5,9},{6,10},{7,11},{8,12},{9,13},{1... | collective-permute-start | bytes 589832 | tf_op jit(solution)/shard_map/cond/branch_1_fun/ppermute | solution.py:430
  95.6 18.1 %collective-permute-start.83 = (bf16[6,32,512]{2,1,0:T(8,128)(2,1)S(1)}, bf16[6,32,512]{2,1,0:T(8,128)(2,1)S(1)}, u32[]{:S(2)}, u32[]{:S(2)}) collective-permute-start(bf16[6,32,512]{2,1,0:T(8,128)(2,1)S(1)} %get-tuple-element.368), channel_id=1, source_target_pairs={{0,8},{1,9},{2,10},{3,11},{4,12},{5,13},{6,14},{7,15},{8,0},{9,1},... | collective-permute-start | bytes 589832 | tf_op jit(solution)/shard_map/cond/branch_1_fun/ppermute | solution.py:430
  96.2 17.5 %collective-permute-start.84 = (bf16[6,32,512]{2,1,0:T(8,128)(2,1)S(1)}, bf16[6,32,512]{2,1,0:T(8,128)(2,1)S(1)}, u32[]{:S(2)}, u32[]{:S(2)}) collective-permute-start(bf16[6,32,512]{2,1,0:T(8,128)(2,1)S(1)} %get-tuple-element.369), channel_id=1, source_target_pairs={{0,12},{1,13},{2,14},{3,15},{4,0},{5,1},{6,2},{7,3},{8,4},{9,5},{1... | collective-permute-start | bytes 589832 | tf_op jit(solution)/shard_map/cond/branch_1_fun/ppermute | solution.py:430
  98.1 10.2 %collective-permute-start.86 = (bf16[2,4,32,256]{3,2,1,0:T(8,128)(2,1)S(1)}, bf16[2,4,32,256]{3,2,1,0:T(8,128)(2,1)S(1)}, u32[]{:S(2)}, u32[]{:S(2)}) collective-permute-start(bf16[2,4,32,256]{3,2,1,0:T(8,128)(2,1)S(1)} %get-tuple-element.371), channel_id=1, source_target_pairs={{0,2},{1,3},{2,0},{3,1},{4,6},{5,7},{6,4},{7,5},{8,10},{9,11},{10,... | collective-permute-start | bytes 393224 | tf_op jit(solution)/shard_map/cond/branch_1_fun/ppermute | solution.py:441
  107.9 5.8 %collective-permute-start.87 = (bf16[2,4,32,256]{3,2,1,0:T(8,128)(2,1)S(1)}, bf16[2,4,32,256]{3,2,1,0:T(8,128)(2,1)S(1)}, u32[]{:S(2)}, u32[]{:S(2)}) collective-permute-start(bf16[2,4,32,256]{3,2,1,0:T(8,128)(2,1)S(1)} %get-tuple-element.372), channel_id=1, source_target_pairs={{0,3},{1,2},{2,1},{3,0},{4,7},{5,6},{6,5},{7,4},{8,11},{9,10},{10,... | collective-permute-start | bytes 393224 | tf_op jit(solution)/shard_map/cond/branch_1_fun/ppermute | solution.py:441
  115.2 21.8 %collective-permute-start.92 = (bf16[16,32,512]{2,1,0:T(8,128)(2,1)S(1)}, bf16[16,32,512]{2,1,0:T(8,128)(2,1)S(1)}, u32[]{:S(2)}, u32[]{:S(2)}) collective-permute-start(bf16[16,32,512]{2,1,0:T(8,128)(2,1)S(1)} %unpack.10.refs_0_.refs_2_.refs_1_), channel_id=1, source_target_pairs={{0,16},{16,0},{1,17},{17,1},{2,18},{18,2},{3,19},{19,3},{4,20},{20... | collective-permute-start | bytes 1572872 | tf_op jit(solution)/shard_map/cond/branch_1_fun/ppermute | solution.py:513
  115.8 7.6 %collective-permute-start.88 = (bf16[6,32,256]{2,1,0:T(8,128)(2,1)S(1)}, bf16[6,32,256]{2,1,0:T(8,128)(2,1)S(1)}, u32[]{:S(2)}, u32[]{:S(2)}) collective-permute-start(bf16[6,32,256]{2,1,0:T(8,128)(2,1)S(1)} %get-tuple-element.378), channel_id=1, source_target_pairs={{0,4},{1,5},{2,6},{3,7},{4,8},{5,9},{6,10},{7,11},{8,12},{9,13},{1... | collective-permute-start | bytes 294920 | tf_op jit(solution)/shard_map/cond/branch_1_fun/ppermute | solution.py:430
  118.6 8.1 %collective-permute-start.89 = (bf16[6,32,256]{2,1,0:T(8,128)(2,1)S(1)}, bf16[6,32,256]{2,1,0:T(8,128)(2,1)S(1)}, u32[]{:S(2)}, u32[]{:S(2)}) collective-permute-start(bf16[6,32,256]{2,1,0:T(8,128)(2,1)S(1)} %get-tuple-element.379), channel_id=1, source_target_pairs={{0,8},{1,9},{2,10},{3,11},{4,12},{5,13},{6,14},{7,15},{8,0},{9,1},... | collective-permute-start | bytes 294920 | tf_op jit(solution)/shard_map/cond/branch_1_fun/ppermute | solution.py:430
  120.2 6.6 %collective-permute-start.90 = (bf16[6,32,256]{2,1,0:T(8,128)(2,1)S(1)}, bf16[6,32,256]{2,1,0:T(8,128)(2,1)S(1)}, u32[]{:S(2)}, u32[]{:S(2)}) collective-permute-start(bf16[6,32,256]{2,1,0:T(8,128)(2,1)S(1)} %get-tuple-element.380), channel_id=1, source_target_pairs={{0,12},{1,13},{2,14},{3,15},{4,0},{5,1},{6,2},{7,3},{8,4},{9,5},{1... | collective-permute-start | bytes 294920 | tf_op jit(solution)/shard_map/cond/branch_1_fun/ppermute | solution.py:430
  121.0 14.7 %collective-permute-start.93 = (bf16[16,32,256]{2,1,0:T(8,128)(2,1)S(1)}, bf16[16,32,256]{2,1,0:T(8,128)(2,1)S(1)}, u32[]{:S(2)}, u32[]{:S(2)}) collective-permute-start(bf16[16,32,256]{2,1,0:T(8,128)(2,1)S(1)} %unpack.9.refs_3_.refs_2_), channel_id=1, source_target_pairs={{0,16},{16,0},{1,17},{17,1},{2,18},{18,2},{3,19},{19,3},{4,20},{20... | collective-permute-start | bytes 786440 | tf_op jit(solution)/shard_map/cond/branch_1_fun/ppermute | solution.py:513
  127.5 12.9 %collective-permute-start.91 = (bf16[16,32,256]{2,1,0:T(8,128)(2,1)S(1)}, bf16[16,32,256]{2,1,0:T(8,128)(2,1)S(1)}, u32[]{:S(2)}, u32[]{:S(2)}) collective-permute-start(bf16[16,32,256]{2,1,0:T(8,128)(2,1)S(1)} %unpack.11.refs_1_.refs_2_), channel_id=1, source_target_pairs={{0,16},{16,0},{1,17},{17,1},{2,18},{18,2},{3,19},{19,3},{4,20},{20... | collective-permute-start | bytes 786440 | tf_op jit(solution)/shard_map/cond/branch_1_fun/ppermute | solution.py:513
  (17 other events, 279.6 us)

commit v3 on v2

--- a/solution.py
+++ b/solution.py
@@ -8,12 +8,13 @@
 OUTER_RATE = 0.7
 MOMENTUM_COEF = 0.9
 PLANES = 4
-CHUNKS = ((4, 2, False), (0, 4, False), (6, 2, False))
+CHUNKS = ((4, 2), (0, 4), (6, 2))
 EMBED = None
+FIRST = 0
 ORDER = (
-    (0, 0), (EMBED, 0), (1, 0), (2, 0), (EMBED, 0), (0, 1), (EMBED, 0), (1, 1, 0), (0, 2), (EMBED, 0),
-    (0, 3), (2, 1, 1), (1, 2), (0, 4, 2), (2, 2), (1, 3), (EMBED, 0), (2, 3), (0, 5), (1, 4), (EMBED, 0),
-    (2, 4, 1), (1, 5), (EMBED, 0), (0, 6), (2, 5), (1, 6), (2, 6),
+    (0, 1), (1, 1, 0), (0, 2), (EMBED, 0), (0, 3), (EMBED, 0), (2, 1, 1), (1, 2), (EMBED, 0),
+    (0, 4, 2), (2, 2), (1, 3), (2, 3), (0, 5), (1, 4), (2, 4, 1), (EMBED, 0), (1, 5), (0, 6), (2, 5), (EMBED, 0),
+    (1, 6), (EMBED, 0), (2, 6),
 )
 VMEM_LIMIT = 48 * 1024 * 1024
 
@@ -67,30 +68,67 @@
     return pl.ds(pl.multiple_of(first, width), width)
 
 
-def take_columns(here, local_rows, start, width, after):
-    block = local_rows.shape[:2] + (width,)
-
-    def kernel(here_ref, rows_ref, *refs):
-        done = refs[-1]
-        copies = []
-        for i, group in enumerate((1 - here_ref[0], here_ref[0])):
-            chosen = columns(group, rows_ref, start, width)
-            copies.append(pltpu.make_async_copy(rows_ref.at[:, :, chosen], refs[i], done.at[i]))
-        for copy in copies:
-            copy.start()
-        for copy in copies:
-            copy.wait()
-
-    return call(
-        kernel,
-        (here,),
-        (local_rows,),
-        [WHOLE],
-        [like(block)] * 2,
-        [full(block)] * 2,
-        after=after,
-        scratch=[pltpu.SemaphoreType.DMA((2,))],
-        name="take_columns",
+def slot_tables(here, slab_owner, devices, capacity):
+    inside = devices // PLANES
+    slab_count = slab_owner.shape[0]
+    plane_slots = capacity * inside
+    shift = inside.bit_length() - 1
+
+    def kernel(
+        here_ref, owner_ref, to_ref, from_ref, count_ref, pos_ref, used_ref, most_ref, planes, owners
+    ):
+        plane, place_here = here_ref[1], here_ref[2]
+        for k in range(PLANES):
+            planes[k] = 0
+
+            @pl.loop(0, plane_slots)
+            def _(j, k=k):
+                to_ref[k, j] = 0
+                from_ref[k, j] = 0
+
+        @pl.loop(0, devices)
+        def _(o):
+            owners[o] = 0
+
+        @pl.loop(0, inside)
+        def _(m):
+            for c in range(capacity):
+                pos_ref[m, c] = 0
+                used_ref[m, c] = 0
+
+        @pl.loop(0, slab_count)
+        def _(s):
+            owner = owner_ref[s]
+            its_plane = owner >> shift
+            j, c = planes[its_plane], owners[owner]
+            planes[its_plane] = j + 1
+            owners[owner] = c + 1
+            to_ref[(its_plane - plane) & (PLANES - 1), j] = s
+            from_ref[(plane - its_plane) & (PLANES - 1), j] = s
+
+            @pl.when(its_plane == plane)
+            def _():
+                m = (owner & (inside - 1)) ^ place_here
+                pos_ref[m, c] = j
+                used_ref[m, c] = 1
+
+        most = planes[0]
+        for k in range(PLANES):
+            count_ref[k] = planes[(plane - k) & (PLANES - 1)]
+            most = jnp.maximum(most, planes[k])
+        most_ref[0] = most
+
+    shapes = [(PLANES, plane_slots)] * 2 + [(PLANES,)] + [(inside, capacity)] * 2 + [(1,)]
+    scalars = pl.BlockSpec(memory_space=pltpu.SMEM)
+    return call(
+        kernel,
+        (here, slab_owner),
+        (),
+        [],
+        [like(shape, jnp.int32) for shape in shapes],
+        [scalars] * len(shapes),
+        scratch=[pltpu.SMEM((PLANES,), jnp.int32), pltpu.SMEM((devices,), jnp.int32)],
+        name="slot_tables",
     )
 
 
@@ -113,29 +151,6 @@
         [full(packed)] * PLANES,
         after=after,
         name="sum_and_pack",
-    )
-
-
-def sum_for_owners(slab_of, mine, peer, after):
-    devices, capacity = slab_of.shape
-
-    def kernel(ids_ref, mine_ref, peer_ref, out):
-        @pl.loop(0, devices)
-        def _(d):
-            for c in range(capacity):
-                i = ids_ref[d, c]
-                out[d, c] = mine_ref[i] + peer_ref[i]
-
-    packed = (devices, capacity) + mine.shape[1:]
-    return call(
-        kernel,
-        (slab_of,),
-        (mine, peer),
-        [full(mine.shape)] * 2,
-        like(packed),
-        full(packed),
-        after=after,
-        name="sum_for_owners",
     )
 
 
@@ -172,7 +187,7 @@
         new_anchor_ref, new_moment_ref = refs[-inside - 2], refs[-inside - 1]
         outs = refs[-inside:]
         c = pl.program_id(0)
-        used_here = used_ref[c] > 0
+        used_here = used_ref[0, c] > 0
 
         @pl.loop(0, planes)
         def _(z):
@@ -204,42 +219,6 @@
     )
 
 
-def update_owned(here, used, got, anchor, moment, start, earlier, after):
-    devices, capacity, row_count, width = got.shape
-
-    def kernel(here_ref, used_ref, got_ref, anchor_ref, moment_ref, *refs):
-        new_anchor_ref, new_moment_ref, out_ref = refs[-3:]
-        c = pl.program_id(0)
-        used_here = used_ref[c] > 0
-
-        @pl.loop(0, devices)
-        def _(d):
-            rows = pl.ds(pl.multiple_of(d * row_count, row_count), row_count)
-            anchor_value = anchor_ref[rows, :]
-            moment_value = moment_ref[rows, :]
-            mean = got_ref[d, c].astype(jnp.float32) * 0.5
-            new_anchor, new_moment = nesterov(anchor_value, moment_value, mean)
-            new_anchor = jnp.where(used_here, new_anchor, anchor_value)
-            new_anchor_ref[rows, :] = new_anchor
-            new_moment_ref[rows, :] = jnp.where(used_here, new_moment, moment_value)
-            out_ref[d, c] = new_anchor.astype(out_ref.dtype)
-
-    state = pl.BlockSpec((None, anchor.shape[1], width), lambda c, *_: (c, 0, start // width))
-    part = full(got.shape)
-    return call(
-        kernel,
-        (here, used),
-        (got, anchor, moment, *earlier),
-        [part, state, state] + [WHOLE] * len(earlier),
-        [like(anchor.shape, anchor.dtype)] * 2 + [like(got.shape)],
-        [state, state, part],
-        grid=(capacity,),
-        aliases={3: 0, 4: 1} if earlier else {},
-        after=after,
-        name="update_owned",
-    )
-
-
 def pack_for_planes(here, owner_pos, owner_used, backs, slots, after):
     capacity, _, row_count, width = backs[0].shape
     inside = len(backs)
@@ -287,27 +266,6 @@
         full(block),
         after=after,
         name="unpack",
-    )
-
-
-def unpack_owned(slab_owner, slot_index, got, after):
-    slab_count = slab_owner.shape[0]
-
-    def kernel(owner_ref, slot_ref, got_ref, out_ref):
-        @pl.loop(0, slab_count)
-        def _(s):
-            out_ref[s] = got_ref[owner_ref[s], slot_ref[s]]
-
-    block = (slab_count,) + got.shape[2:]
-    return call(
-        kernel,
-        (slab_owner, slot_index),
-        (got,),
-        [full(got.shape)],
-        like(block),
-        full(block),
-        after=after,
-        name="unpack_owned",
     )
 
 
@@ -409,22 +367,24 @@
 
 def moved(
     slots,
+    local_shape,
     tables,
-    local_rows,
+    first_columns,
+    later_columns,
     anchor,
     moment,
     embed_rows,
+    peer_embed,
     anchor_embed,
     momentum_embed,
     embed_basis,
 ):
-    (here, to_ids, from_ids, from_counts, owner_pos, owner_used, my_used, slab_of, slab_owner,
-        slot_index) = tables
+    here, to_ids, from_ids, from_counts, owner_pos, owner_used = tables
     devices = lax.axis_size("shard")
     inside = devices // PLANES
     capacity = anchor.shape[0]
-    eighth = local_rows.shape[2] // 16
     swap = [(0, 1), (1, 0)]
+
     def over_planes(parts):
         return [parts[0]] + [
             lax.ppermute(
@@ -433,9 +393,6 @@
             for k in range(1, PLANES)
         ]
 
-    def over_devices(value):
-        return lax.all_to_all(value, "shard", split_axis=0, concat_axis=0, tiled=True)
-
     def in_plane(parts):
         return [parts[0]] + [
             lax.ppermute(parts[m], "shard", [(i, i ^ m) for i in range(devices)])
@@ -444,10 +401,7 @@
 
     def embed_steps():
         after = yield None
-        rows = lax.optimization_barrier((embed_rows, *after))[0]
-        peer = lax.ppermute(rows, "group", swap)
-        after = yield after[0]
-        factor = project_embed(embed_basis, anchor_embed, embed_rows, peer, after)
+        factor = project_embed(embed_basis, anchor_embed, embed_rows, peer_embed, after)
         step = 1
         while step < devices:
             pairs = [(i, i ^ step) for i in range(devices)]
@@ -461,7 +415,10 @@
     embed = embed_steps()
     next(embed)
     new_embed = None
-    held = [None] * len(CHUNKS)
+    held = [
+        (mine, lax.ppermute(outgoing, "group", swap)) for outgoing, mine in later_columns
+    ]
+    held.insert(FIRST, first_columns)
     state, new_rows, after = (), (), ()
     for chunk, step, *waits in ORDER:
         for wait in waits:
@@ -471,48 +428,28 @@
             if isinstance(new_embed, jax.Array):
                 after = (new_embed,)
             continue
-        start, width, direct = CHUNKS[chunk]
-        start, width = start * eighth, width * eighth
+        start = CHUNKS[chunk][0] * (local_shape[2] // 16)
         value = held[chunk]
-        if step == 0:
-            if not after:
-                first = (1 - here[0]) * (local_rows.shape[2] // 2) + start
-                after = (lax.dynamic_slice_in_dim(local_rows, first, width, axis=2),)
-                value = lax.ppermute(after[0], "group", swap)
-                token, mine = take_columns(here, local_rows, start, width, after)
-                value = (mine, value)
-            else:
-                token, mine = take_columns(here, local_rows, start, width, after)
-                value = (mine, lax.ppermute(token, "group", swap))
-        elif step == 1 and direct:
-            token = sum_for_owners(slab_of, *value, after)
-            value = over_devices(token)
-        elif step == 1:
+        if step == 1:
             parts = sum_and_pack(to_ids, *value, slots, after)
             token, value = parts[0], over_planes(parts)
         elif step == 2:
             parts = pack_for_owners(here, owner_pos, value, inside, capacity, after)
             token = parts[0]
             value = in_plane(parts)
-        elif step == 3 and direct:
-            *state, token = update_owned(here, my_used, value, anchor, moment, start, state, after)
-            value = over_devices(token)
         elif step == 3:
             first, second, *parts = update_chunk(
-                here, my_used, value, anchor, moment, start, state, after
+                here, owner_used, value, anchor, moment, start, state, after
             )
             state, token, value = (first, second), parts[0], in_plane(parts)
         elif step == 4:
             parts = pack_for_planes(here, owner_pos, owner_used, value, slots, after)
             token, value = parts[0], over_planes(parts)
         elif step == 5:
-            if direct:
-                token = unpack_owned(slab_owner, slot_index, value, after)
-            else:
-                token = unpack(from_ids, from_counts, value, slab_owner.shape[0], after)
+            token = unpack(from_ids, from_counts, value, local_shape[0], after)
             value = (token, lax.ppermute(token, "group", swap))
         else:
-            new_rows = (place(here, *value, start, local_rows.shape, new_rows, after),)
+            new_rows = (place(here, *value, start, local_shape, new_rows, after),)
         held[chunk] = value
         after = (token,)
     while isinstance(new_embed, jax.Array):
@@ -530,64 +467,49 @@
     momentum_embed,
     embed_basis,
 ):
-    slab_count = slab_owner.shape[0]
     devices = lax.axis_size("shard")
     capacity = anchor_slabs.shape[1]
     inside = devices // PLANES
     device_here = lax.axis_index("shard")
-    plane, place_here = device_here // inside, device_here % inside
-    here = jnp.stack([lax.axis_index("group"), plane, place_here]).astype(jnp.int32)
-
-    order = jnp.arange(slab_count, dtype=jnp.int32)
-    earlier = order[None, :] < order[:, None]
-    same_owner = slab_owner[:, None] == slab_owner[None, :]
-    slab_plane = slab_owner // inside
-    same_plane = slab_plane[:, None] == slab_plane[None, :]
-    slot_index = jnp.sum((same_owner & earlier).astype(jnp.int32), axis=1)
-    position = jnp.sum((same_plane & earlier).astype(jnp.int32), axis=1)
-    offsets = jnp.arange(PLANES, dtype=jnp.int32)
-    places = jnp.arange(capacity * inside, dtype=jnp.int32)
-
-    def slots_of(planes):
-        held = slab_plane[None, :] == planes[:, None]
-        at_place = held[:, None, :] & (position[None, None, :] == places[None, :, None])
-        return (
-            jnp.sum(jnp.where(at_place, order, 0), axis=2),
-            jnp.sum(held.astype(jnp.int32), axis=1),
+    here = jnp.stack(
+        [lax.axis_index("group"), device_here // inside, device_here % inside]
+    ).astype(jnp.int32)
+
+    local_rows, embed_rows = replica_weights[0], replica_embed[0]
+    half = local_rows.shape[2] // 2
+    pairs = []
+    for start, width in CHUNKS:
+        pairs.append(
+            tuple(
+                lax.dynamic_slice_in_dim(
+                    local_rows, group * half + start * (half // 8), width * (half // 8), axis=2
+                )
+                for group in (1 - here[0], here[0])
+            )
         )
-
-    to_ids, _ = slots_of((plane + offsets) % PLANES)
-    from_ids, from_counts = slots_of((plane - offsets) % PLANES)
-    owners = plane * inside + (place_here ^ jnp.arange(inside, dtype=jnp.int32))
-    at_owner = (slab_owner[None, None, :] == owners[:, None, None]) & (
-        slot_index[None, None, :] == jnp.arange(capacity, dtype=jnp.int32)[None, :, None]
-    )
-    owner_pos = jnp.sum(jnp.where(at_owner, position, 0), axis=2)
-    owner_used = jnp.any(at_owner, axis=2).astype(jnp.int32)
-    matches = (slab_owner[None, None, :] == jnp.arange(devices, dtype=jnp.int32)[:, None, None]) & (
-        slot_index[None, None, :] == jnp.arange(capacity, dtype=jnp.int32)[None, :, None]
-    )
-    slab_of = jnp.sum(jnp.where(matches, order, 0), axis=2)
-    tables = (
-        here, to_ids, from_ids, from_counts, owner_pos, owner_used, owner_used[0], slab_of, slab_owner, slot_index
-    )
-
-    most = capacity * inside
-    fewer = most * 3 // 4
+    outgoing, mine = pairs.pop(FIRST)
+    swap = [(0, 1), (1, 0)]
+    peer = lax.ppermute(outgoing, "group", swap)
+    *tables, fullest = slot_tables(here, slab_owner, devices, capacity)
     operands = (
-        tables,
-        replica_weights[0],
+        (here, *tables),
+        (mine, peer),
+        pairs,
         anchor_slabs[0],
         momentum_slabs[0],
-        replica_embed[0],
+        embed_rows,
+        lax.ppermute(embed_rows, "group", swap),
         anchor_embed,
         momentum_embed,
         embed_basis,
     )
+    most = capacity * inside
+    fewer = most * 3 // 4
+    shape = local_rows.shape
     results = lax.cond(
-        jnp.max(from_counts) <= fewer,
-        lambda *values: moved(fewer, *values),
-        lambda *values: moved(most, *values),
+        fullest[0] <= fewer,
+        lambda *values: moved(fewer, shape, *values),
+        lambda *values: moved(most, shape, *values),
         *operands,
     )
     return tuple(

time: 142 us -> 138 us (0.972)
  other arithmetic: 7.27 us -> 0.08 us
  local copies, waits for them, and re-layouts: 1.42 us -> 5.79 us
  waiting for transfers between devices: 43.1 us -> 47.2 us
  starting transfers between devices: 60.7 us -> 58.2 us
  Pallas kernels: 27.4 us -> 25 us
    ppermute x18, waiting for transfers between devices: 20.9 us -> 29.5 us  [over_planes(): lax.ppermute(parts[k], 'shard', [(i, (i + k * inside) % devices) for i in...]
    ppermute x4, waiting for transfers between devices: 8.35 us -> 2.38 us  [embed_steps(): other = lax.ppermute(factor, 'shard', pairs)]
    ppermute x4, waiting for transfers between devices: 0.01 us -> 3.97 us  [the longest x1 3.96 us: on_device(): lax.ppermute(embed_rows, 'group', swap)]
    dynamic_slice x1 -> x3, local copies, waits for them, and re-layouts: 1.12 us -> 4.48 us  [on_device(): lax.dynamic_slice_in_dim(local_rows, group * half + start * (half // 8),...]
    reduce_sum x5 -> x0, other arithmetic: 2.95 us -> none  [the longest x1 0.91 us: on_device(): slot_index = jnp.sum((same_owner & earlier).astype(jnp.int32), axis=1)]
    ppermute x3, waiting for transfers between devices: 7.52 us -> 4.95 us  [moved(): value = (token, lax.ppermute(token, 'group', swap))]
    pallas_call x27 -> x25, Pallas kernels: 27.4 us -> 25 us  [call(): pl.pallas_call(body, grid_spec=pltpu.PrefetchScalarGridSpec(num_scalar_pr...]
    eq x5 -> x0, other arithmetic: 2.17 us -> none  [the longest x2 0.74 us: slots_of(): held = slab_plane[None, :] == planes[:, None]]
  transfers between devices with their start and end apart: 47 -> 47, of which waited for: 14 -> 19; matrix products, arithmetic and copies ran while one was open for 2% -> 1% of each run, Pallas kernels for 17% -> 16%
where the time goes in v3:
time: 138 us
  starting transfers between devices  58.2 us (42%)
  waiting for transfers between devices  47.2 us (34%)
  Pallas kernels  25 us (18%)
  local copies, waits for them, and re-layouts  5.79 us (4%)
    ppermute x18, starting transfers between devices, over_planes(): lax.ppermute(parts[k], 'shard', [(i, (i + k * inside) % devices) for i in...  35.3 us
    ppermute x18, waiting for transfers between devices, over_planes(): lax.ppermute(parts[k], 'shard', [(i, (i + k * inside) % devices) for i in...  29.5 us
    pallas_call x25, Pallas kernels, call(): pl.pallas_call(body, grid_spec=pltpu.PrefetchScalarGridSpec(num_scalar_pr...  25 us
    ppermute x18, starting transfers between devices, in_plane(): lax.ppermute(parts[m], 'shard', [(i, i ^ m) for i in range(devices)])  11.2 us
    ppermute x18, waiting for transfers between devices, in_plane(): lax.ppermute(parts[m], 'shard', [(i, i ^ m) for i in range(devices)])  6.34 us
    ppermute x3, waiting for transfers between devices, moved(): value = (token, lax.ppermute(token, 'group', swap))  4.95 us
    dynamic_slice x3, local copies, waits for them, and re-layouts, on_device(): lax.dynamic_slice_in_dim(local_rows, group * half + start * (half // 8),...  4.48 us
    ppermute x1, waiting for transfers between devices, on_device(): lax.ppermute(embed_rows, 'group', swap)  3.96 us
  transfers between devices with their start and end apart: 47, of which 19 were waited for; matrix products, arithmetic and copies ran while one was open for 1% of the time, Pallas kernels for 16%

profile of v3, /device:TPU:0, one launch (start us, length us, event | category | flops | bytes accessed | tf_op | source)
XLA Modules:
  0.0 138.0 jit_solution(11948960166058147279)
XLA Ops:
  1.6 3.0 %collective-permute-start.90 = (bf16[16,32,256]{2,1,0:T(8,128)(2,1)S(1)}, bf16[16,32,256]{2,1,0:T(8,128)(2,1)S(1)}, u32[]{:S(2)}, u32[]{:S(2)}) collective-permute-start(bf16[16,32,256]{2,1,0:T(8,128)(2,1)S(1)} %dynamic-slice_bitcast_fusion.10), channel_id=1, source_target_pairs={{0,16},{16,0},{1,17},{17,1},{2,18},{18,2},{3,19},{19,3},{4,20},{20... | collective-permute-start | bytes 786440 | tf_op jit(solution)/shard_map/ppermute | solution.py:492
  5.4 1.9 %slot_tables.1 = (s32[4,8]{1,0:T(4,128)S(1)}, s32[4,8]{1,0:T(4,128)S(1)}, s32[4]{0:T(128)S(1)}, s32[4,2]{1,0:T(4,128)S(1)}, s32[4,2]{1,0:T(4,128)S(1)}, /*index=5*/s32[1]{0:T(128)}) custom-call(s32[3]{0:T(128)S(1)} %pad_add_fusion.refs_0_, s32[16]{0:T(128)S(1)} %copy-done), custom_call_target="tpu_custom_call" | custom-call | flops 1 | bytes 1 | tf_op jit(solution)/shard_map/slot_tables/pallas_call | solution.py:38
  8.0 4.0 %collective-permute-done.91 = bf16[48,512]{1,0:T(8,128)(2,1)S(1)} collective-permute-done((bf16[48,512]{1,0:T(8,128)(2,1)}, bf16[48,512]{1,0:T(8,128)(2,1)S(1)}, u32[]{:S(2)}, u32[]{:S(2)}) %collective-permute-start.91) | collective-permute-done | bytes 49184 | tf_op jit(solution)/shard_map/ppermute | solution.py:501
  12.0 125.4 %conditional.1 = (f32[2,512,1024]{2,1,0:T(8,128)}, f32[2,512,1024]{2,1,0:T(8,128)}, f32[48,512]{1,0:T(8,128)S(1)}, f32[48,512]{1,0:T(8,128)}, bf16[48,512]{1,0:T...) conditional(s32[]{:T(128)} %bitcast.19, (s32[]{:T(128)}, s32[]{:T(128)}, bf16[1,16,32,2048]{3,2,1,0:T(8,128)(2,1)}, ...), branch_computations={%region_0.1_spmd, %region_1.2_spmd} | conditional | flops 39 | bytes 72861856 | solution.py:509
  12.0 1.8 %dynamic-slice_bitcast_fusion.5 = (bf16[16,32,512]{2,1,0:T(8,128)(2,1)S(1)}, bf16[16,32,512]{2,1,0:T(8,128)(2,1)S(1)}) fusion(bf16[1,16,32,2048]{3,2,1,0:T(8,128)(2,1)} %get-tuple-element.274, s32[]{:T(128)S(6)} %select_n.43, s32[]{:T(128)S(6)} %select_n.42), kind=kLoop, calls=%fused_computation.5 | loop fusion | bytes 2097160 | tf_op jit(solution)/shard_map/dynamic_slice | solution.py:484
  13.8 1.8 %collective-permute-start.48 = (bf16[16,32,512]{2,1,0:T(8,128)(2,1)S(1)}, bf16[16,32,512]{2,1,0:T(8,128)(2,1)S(1)}, u32[]{:S(2)}, u32[]{:S(2)}) collective-permute-start(bf16[16,32,512]{2,1,0:T(8,128)(2,1)S(1)} %get-tuple-element.385), channel_id=1, source_target_pairs={{0,16},{16,0},{1,17},{17,1},{2,18},{18,2},{3,19},{19,3},{4,20},{20... | collective-permute-start | bytes 1572872 | tf_op jit(solution)/shard_map/cond/branch_1_fun/ppermute | solution.py:419
  15.6 1.7 %dynamic-slice_bitcast_fusion.7 = (bf16[16,32,256]{2,1,0:T(8,128)(2,1)S(1)}, bf16[16,32,256]{2,1,0:T(8,128)(2,1)S(1)}, bf16[16,32,256]{2,1,0:T(8,128)(2,1)S(1)}) fusion(bf16[1,16,32,2048]{3,2,1,0:T(8,128)(2,1)} %get-tuple-element.274, s32[]{:T(128)S(6)} %select_n.45, s32[]{:T(128)S(6)} %select_n.44, s32[]{:T(128)S(6)} %select_n.41), kind=kLoop, calls=%fused_computation.7 | loop fusion | bytes 1572876 | tf_op jit(solution)/shard_map/dynamic_slice | solution.py:484
  18.1 1.6 %collective-permute-start.45 = (bf16[6,32,256]{2,1,0:T(8,128)(2,1)S(1)}, bf16[6,32,256]{2,1,0:T(8,128)(2,1)S(1)}, u32[]{:S(2)}, u32[]{:S(2)}) collective-permute-start(bf16[6,32,256]{2,1,0:T(8,128)(2,1)S(1)} %get-tuple-element.279), channel_id=1, source_target_pairs={{0,4},{1,5},{2,6},{3,7},{4,8},{5,9},{6,10},{7,11},{8,12},{9,13},{1... | collective-permute-start | bytes 294920 | tf_op jit(solution)/shard_map/cond/branch_1_fun/ppermute | solution.py:390
  19.8 2.6 %collective-permute-start.46 = (bf16[6,32,256]{2,1,0:T(8,128)(2,1)S(1)}, bf16[6,32,256]{2,1,0:T(8,128)(2,1)S(1)}, u32[]{:S(2)}, u32[]{:S(2)}) collective-permute-start(bf16[6,32,256]{2,1,0:T(8,128)(2,1)S(1)} %get-tuple-element.280), channel_id=1, source_target_pairs={{0,8},{1,9},{2,10},{3,11},{4,12},{5,13},{6,14},{7,15},{8,0},{9,1},... | collective-permute-start | bytes 294920 | tf_op jit(solution)/shard_map/cond/branch_1_fun/ppermute | solution.py:390
  22.3 1.3 collective-permute-start.47
  23.7 2.0 %collective-permute-done.45.refs_3_.refs_4_ = bf16[6,32,256]{2,1,0:T(8,128)(2,1)S(1)} collective-permute-done((bf16[6,32,256]{2,1,0:T(8,128)(2,1)S(1)}, bf16[6,32,256]{2,1,0:T(8,128)(2,1)S(1)}, u32[]{:S(2)}, u32[]{:S(2)}) %collective-permute-start.45) | collective-permute-done | bytes 98336 | tf_op jit(solution)/shard_map/cond/branch_1_fun/ppermute | solution.py:390
  25.7 2.5 %collective-permute-done.46.refs_4_.refs_5_ = bf16[6,32,256]{2,1,0:T(8,128)(2,1)S(1)} collective-permute-done((bf16[6,32,256]{2,1,0:T(8,128)(2,1)S(1)}, bf16[6,32,256]{2,1,0:T(8,128)(2,1)S(1)}, u32[]{:S(2)}, u32[]{:S(2)}) %collective-permute-start.46) | collective-permute-done | bytes 98336 | tf_op jit(solution)/shard_map/cond/branch_1_fun/ppermute | solution.py:390
  30.2 1.6 %collective-permute-start.50 = (bf16[2,4,32,256]{3,2,1,0:T(8,128)(2,1)S(1)}, bf16[2,4,32,256]{3,2,1,0:T(8,128)(2,1)S(1)}, u32[]{:S(2)}, u32[]{:S(2)}) collective-permute-start(bf16[2,4,32,256]{3,2,1,0:T(8,128)(2,1)S(1)} %get-tuple-element.290), channel_id=1, source_target_pairs={{0,2},{1,3},{2,0},{3,1},{4,6},{5,7},{6,4},{7,5},{8,10},{9,11},{10,... | collective-permute-start | bytes 393224 | tf_op jit(solution)/shard_map/cond/branch_1_fun/ppermute | solution.py:398
  31.8 2.2 %collective-permute-start.53 = (bf16[6,32,512]{2,1,0:T(8,128)(2,1)S(1)}, bf16[6,32,512]{2,1,0:T(8,128)(2,1)S(1)}, u32[]{:S(2)}, u32[]{:S(2)}) collective-permute-start(bf16[6,32,512]{2,1,0:T(8,128)(2,1)S(1)} %get-tuple-element.295), channel_id=1, source_target_pairs={{0,4},{1,5},{2,6},{3,7},{4,8},{5,9},{6,10},{7,11},{8,12},{9,13},{1... | collective-permute-start | bytes 589832 | tf_op jit(solution)/shard_map/cond/branch_1_fun/ppermute | solution.py:390
  34.0 1.8 %collective-permute-start.54 = (bf16[6,32,512]{2,1,0:T(8,128)(2,1)S(1)}, bf16[6,32,512]{2,1,0:T(8,128)(2,1)S(1)}, u32[]{:S(2)}, u32[]{:S(2)}) collective-permute-start(bf16[6,32,512]{2,1,0:T(8,128)(2,1)S(1)} %get-tuple-element.296), channel_id=1, source_target_pairs={{0,8},{1,9},{2,10},{3,11},{4,12},{5,13},{6,14},{7,15},{8,0},{9,1},... | collective-permute-start | bytes 589832 | tf_op jit(solution)/shard_map/cond/branch_1_fun/ppermute | solution.py:390
  36.5 1.3 collective-permute-done.51.refs_6_
  37.8 3.5 %collective-permute-start.55 = (bf16[6,32,512]{2,1,0:T(8,128)(2,1)S(1)}, bf16[6,32,512]{2,1,0:T(8,128)(2,1)S(1)}, u32[]{:S(2)}, u32[]{:S(2)}) collective-permute-start(bf16[6,32,512]{2,1,0:T(8,128)(2,1)S(1)} %get-tuple-element.297), channel_id=1, source_target_pairs={{0,12},{1,13},{2,14},{3,15},{4,0},{5,1},{6,2},{7,3},{8,4},{9,5},{1... | collective-permute-start | bytes 589832 | tf_op jit(solution)/shard_map/cond/branch_1_fun/ppermute | solution.py:390
  41.2 3.2 %update_chunk.9 = (f32[2,512,1024]{2,1,0:T(8,128)}, f32[2,512,1024]{2,1,0:T(8,128)}, bf16[2,4,32,256]{3,2,1,0:T(8,128)(2,1)S(1)}, bf16[2,4,32,256]{3,2,1,0:T(8,1...) custom-call(s32[3]{0:T(128)S(1)} %get-tuple-element.270.refs_0_, ...), custom_call_target="tpu_custom_call" | custom-call | flops 1 | bytes 1 | tf_op jit(solution)/shard_map/cond/branch_1_fun/update_chunk/pallas_call | solution.py:38
  45.2 1.5 %collective-permute-start.62 = (bf16[2,4,32,256]{3,2,1,0:T(8,128)(2,1)S(1)}, bf16[2,4,32,256]{3,2,1,0:T(8,128)(2,1)S(1)}, u32[]{:S(2)}, u32[]{:S(2)}) collective-permute-start(bf16[2,4,32,256]{3,2,1,0:T(8,128)(2,1)S(1)} %get-tuple-element.306), channel_id=1, source_target_pairs={{0,2},{1,3},{2,0},{3,1},{4,6},{5,7},{6,4},{7,5},{8,10},{9,11},{10,... | collective-permute-start | bytes 393224 | tf_op jit(solution)/shard_map/cond/branch_1_fun/ppermute | solution.py:398
  46.7 2.8 %collective-permute-done.54.refs_4_.refs_5_ = bf16[6,32,512]{2,1,0:T(8,128)(2,1)S(1)} collective-permute-done((bf16[6,32,512]{2,1,0:T(8,128)(2,1)S(1)}, bf16[6,32,512]{2,1,0:T(8,128)(2,1)S(1)}, u32[]{:S(2)}, u32[]{:S(2)}) %collective-permute-start.54) | collective-permute-done | bytes 196640 | tf_op jit(solution)/shard_map/cond/branch_1_fun/ppermute | solution.py:390
  49.5 1.6 %collective-permute-start.57 = (f32[64,512]{1,0:T(8,128)S(1)}, f32[64,512]{1,0:T(8,128)S(1)}, u32[]{:S(2)}, u32[]{:S(2)}) collective-permute-start(f32[64,512]{1,0:T(8,128)S(1)} %add.85.refs_1_), channel_id=1, source_target_pairs={{0,2},{1,3},{2,0},{3,1},{4,6},{5,7},{6,4},{7,5},{8,10},{9,11},{10,... | collective-permute-start | bytes 393224 | tf_op jit(solution)/shard_map/cond/branch_1_fun/ppermute | solution.py:408
  51.9 3.1 %collective-permute-start.58 = (bf16[6,32,256]{2,1,0:T(8,128)(2,1)S(1)}, bf16[6,32,256]{2,1,0:T(8,128)(2,1)S(1)}, u32[]{:S(2)}, u32[]{:S(2)}) collective-permute-start(bf16[6,32,256]{2,1,0:T(8,128)(2,1)S(1)} %get-tuple-element.302), channel_id=1, source_target_pairs={{0,4},{1,5},{2,6},{3,7},{4,8},{5,9},{6,10},{7,11},{8,12},{9,13},{1... | collective-permute-start | bytes 294920 | tf_op jit(solution)/shard_map/cond/branch_1_fun/ppermute | solution.py:390
  55.8 1.7 %collective-permute-start.65 = (bf16[2,4,32,512]{3,2,1,0:T(8,128)(2,1)S(1)}, bf16[2,4,32,512]{3,2,1,0:T(8,128)(2,1)S(1)}, u32[]{:S(2)}, u32[]{:S(2)}) collective-permute-start(bf16[2,4,32,512]{3,2,1,0:T(8,128)(2,1)S(1)} %get-tuple-element.311), channel_id=1, source_target_pairs={{0,2},{1,3},{2,0},{3,1},{4,6},{5,7},{6,4},{7,5},{8,10},{9,11},{10,... | collective-permute-start | bytes 786440 | tf_op jit(solution)/shard_map/cond/branch_1_fun/ppermute | solution.py:398
  57.6 3.0 %collective-permute-start.59 = (bf16[6,32,256]{2,1,0:T(8,128)(2,1)S(1)}, bf16[6,32,256]{2,1,0:T(8,128)(2,1)S(1)}, u32[]{:S(2)}, u32[]{:S(2)}) collective-permute-start(bf16[6,32,256]{2,1,0:T(8,128)(2,1)S(1)} %get-tuple-element.303), channel_id=1, source_target_pairs={{0,8},{1,9},{2,10},{3,11},{4,12},{5,13},{6,14},{7,15},{8,0},{9,1},... | collective-permute-start | bytes 294920 | tf_op jit(solution)/shard_map/cond/branch_1_fun/ppermute | solution.py:390
  60.7 1.4 %collective-permute-start.60 = (bf16[6,32,256]{2,1,0:T(8,128)(2,1)S(1)}, bf16[6,32,256]{2,1,0:T(8,128)(2,1)S(1)}, u32[]{:S(2)}, u32[]{:S(2)}) collective-permute-start(bf16[6,32,256]{2,1,0:T(8,128)(2,1)S(1)} %get-tuple-element.304), channel_id=1, source_target_pairs={{0,12},{1,13},{2,14},{3,15},{4,0},{5,1},{6,2},{7,3},{8,4},{9,5},{1... | collective-permute-start | bytes 294920 | tf_op jit(solution)/shard_map/cond/branch_1_fun/ppermute | solution.py:390
  62.1 3.5 %collective-permute-done.59.refs_6_.refs_5_ = bf16[6,32,256]{2,1,0:T(8,128)(2,1)S(1)} collective-permute-done((bf16[6,32,256]{2,1,0:T(8,128)(2,1)S(1)}, bf16[6,32,256]{2,1,0:T(8,128)(2,1)S(1)}, u32[]{:S(2)}, u32[]{:S(2)}) %collective-permute-start.59) | collective-permute-done | bytes 98336 | tf_op jit(solution)/shard_map/cond/branch_1_fun/ppermute | solution.py:390
  65.6 1.8 %collective-permute-done.60.refs_7_.refs_6_ = bf16[6,32,256]{2,1,0:T(8,128)(2,1)S(1)} collective-permute-done((bf16[6,32,256]{2,1,0:T(8,128)(2,1)S(1)}, bf16[6,32,256]{2,1,0:T(8,128)(2,1)S(1)}, u32[]{:S(2)}, u32[]{:S(2)}) %collective-permute-start.60) | collective-permute-done | bytes 98336 | tf_op jit(solution)/shard_map/cond/branch_1_fun/ppermute | solution.py:390
  69.9 1.2 collective-permute-start.68
  71.3 3.5 %update_chunk.10 = (f32[2,512,1024]{2,1,0:T(8,128)}, f32[2,512,1024]{2,1,0:T(8,128)}, bf16[2,4,32,512]{3,2,1,0:T(8,128)(2,1)S(1)}, bf16[2,4,32,512]{3,2,1,0:T(8,...) custom-call(s32[3]{0:T(128)S(1)} %get-tuple-element.270.refs_0_, ...), custom_call_target="tpu_custom_call", output_to_operand_aliasing={{0}: (9, {}), {1}: (10, {})} | custom-call | flops 1 | bytes 1 | tf_op jit(solution)/shard_map/cond/branch_1_fun/update_chunk/pallas_call | solution.py:38
  77.0 2.6 %collective-permute-start.71 = (bf16[6,32,256]{2,1,0:T(8,128)(2,1)S(1)}, bf16[6,32,256]{2,1,0:T(8,128)(2,1)S(1)}, u32[]{:S(2)}, u32[]{:S(2)}) collective-permute-start(bf16[6,32,256]{2,1,0:T(8,128)(2,1)S(1)} %get-tuple-element.327), channel_id=1, source_target_pairs={{0,8},{1,9},{2,10},{3,11},{4,12},{5,13},{6,14},{7,15},{8,0},{9,1},... | collective-permute-start | bytes 294920 | tf_op jit(solution)/shard_map/cond/branch_1_fun/ppermute | solution.py:390
  80.2 2.3 %update_chunk.11 = (f32[2,512,1024]{2,1,0:T(8,128)}, f32[2,512,1024]{2,1,0:T(8,128)}, bf16[2,4,32,256]{3,2,1,0:T(8,128)(2,1)S(1)}, bf16[2,4,32,256]{3,2,1,0:T(8,...) custom-call(s32[3]{0:T(128)S(1)} %get-tuple-element.270.refs_0_, ...), custom_call_target="tpu_custom_call", output_to_operand_aliasing={{0}: (9, {}), {1}: (10, {})} | custom-call | flops 1 | bytes 1 | tf_op jit(solution)/shard_map/cond/branch_1_fun/update_chunk/pallas_call | solution.py:38
  82.5 3.2 %collective-permute-done.71.refs_5_ = bf16[6,32,256]{2,1,0:T(8,128)(2,1)S(1)} collective-permute-done((bf16[6,32,256]{2,1,0:T(8,128)(2,1)S(1)}, bf16[6,32,256]{2,1,0:T(8,128)(2,1)S(1)}, u32[]{:S(2)}, u32[]{:S(2)}) %collective-permute-start.71) | collective-permute-done | bytes 98336 | tf_op jit(solution)/shard_map/cond/branch_1_fun/ppermute | solution.py:390
  90.5 2.6 %collective-permute-start.77 = (bf16[6,32,512]{2,1,0:T(8,128)(2,1)S(1)}, bf16[6,32,512]{2,1,0:T(8,128)(2,1)S(1)}, u32[]{:S(2)}, u32[]{:S(2)}) collective-permute-start(bf16[6,32,512]{2,1,0:T(8,128)(2,1)S(1)} %get-tuple-element.334), channel_id=1, source_target_pairs={{0,8},{1,9},{2,10},{3,11},{4,12},{5,13},{6,14},{7,15},{8,0},{9,1},... | collective-permute-start | bytes 589832 | tf_op jit(solution)/shard_map/cond/branch_1_fun/ppermute | solution.py:390
  93.1 1.9 %collective-permute-start.78 = (bf16[6,32,512]{2,1,0:T(8,128)(2,1)S(1)}, bf16[6,32,512]{2,1,0:T(8,128)(2,1)S(1)}, u32[]{:S(2)}, u32[]{:S(2)}) collective-permute-start(bf16[6,32,512]{2,1,0:T(8,128)(2,1)S(1)} %get-tuple-element.335), channel_id=1, source_target_pairs={{0,12},{1,13},{2,14},{3,15},{4,0},{5,1},{6,2},{7,3},{8,4},{9,5},{1... | collective-permute-start | bytes 589832 | tf_op jit(solution)/shard_map/cond/branch_1_fun/ppermute | solution.py:390
  95.0 1.1 collective-permute-start.81
  96.0 4.0 %collective-permute-done.81.refs_11_ = bf16[2,4,32,256]{3,2,1,0:T(8,128)(2,1)S(1)} collective-permute-done((bf16[2,4,32,256]{3,2,1,0:T(8,128)(2,1)S(1)}, bf16[2,4,32,256]{3,2,1,0:T(8,128)(2,1)S(1)}, u32[]{:S(2)}, u32[]{:S(2)}) %collective-permute-start.81) | collective-permute-done | bytes 131104 | tf_op jit(solution)/shard_map/cond/branch_1_fun/ppermute | solution.py:398
  100.0 7.6 %collective-permute-done.77.refs_6_.refs_5_ = bf16[6,32,512]{2,1,0:T(8,128)(2,1)S(1)} collective-permute-done((bf16[6,32,512]{2,1,0:T(8,128)(2,1)S(1)}, bf16[6,32,512]{2,1,0:T(8,128)(2,1)S(1)}, u32[]{:S(2)}, u32[]{:S(2)}) %collective-permute-start.77) | collective-permute-done | bytes 196640 | tf_op jit(solution)/shard_map/cond/branch_1_fun/ppermute | solution.py:390
  108.4 1.5 %collective-permute-done.82.refs_2_ = f32[64,512]{1,0:T(8,128)S(1)} collective-permute-done((f32[64,512]{1,0:T(8,128)S(1)}, f32[64,512]{1,0:T(8,128)S(1)}, u32[]{:S(2)}, u32[]{:S(2)}) %collective-permute-start.82) | collective-permute-done | bytes 131104 | tf_op jit(solution)/shard_map/cond/branch_1_fun/ppermute | solution.py:408
  110.6 1.1 collective-permute-start.88
  111.7 2.8 %collective-permute-start.83 = (bf16[6,32,256]{2,1,0:T(8,128)(2,1)S(1)}, bf16[6,32,256]{2,1,0:T(8,128)(2,1)S(1)}, u32[]{:S(2)}, u32[]{:S(2)}) collective-permute-start(bf16[6,32,256]{2,1,0:T(8,128)(2,1)S(1)} %get-tuple-element.340), channel_id=1, source_target_pairs={{0,4},{1,5},{2,6},{3,7},{4,8},{5,9},{6,10},{7,11},{8,12},{9,13},{1... | collective-permute-start | bytes 294920 | tf_op jit(solution)/shard_map/cond/branch_1_fun/ppermute | solution.py:390
  114.5 1.6 %collective-permute-start.84 = (bf16[6,32,256]{2,1,0:T(8,128)(2,1)S(1)}, bf16[6,32,256]{2,1,0:T(8,128)(2,1)S(1)}, u32[]{:S(2)}, u32[]{:S(2)}) collective-permute-start(bf16[6,32,256]{2,1,0:T(8,128)(2,1)S(1)} %get-tuple-element.341), channel_id=1, source_target_pairs={{0,8},{1,9},{2,10},{3,11},{4,12},{5,13},{6,14},{7,15},{8,0},{9,1},... | collective-permute-start | bytes 294920 | tf_op jit(solution)/shard_map/cond/branch_1_fun/ppermute | solution.py:390
  117.9 1.4 %collective-permute-done.83.refs_4_ = bf16[6,32,256]{2,1,0:T(8,128)(2,1)S(1)} collective-permute-done((bf16[6,32,256]{2,1,0:T(8,128)(2,1)S(1)}, bf16[6,32,256]{2,1,0:T(8,128)(2,1)S(1)}, u32[]{:S(2)}, u32[]{:S(2)}) %collective-permute-start.83) | collective-permute-done | bytes 98336 | tf_op jit(solution)/shard_map/cond/branch_1_fun/ppermute | solution.py:390
  119.3 3.5 %collective-permute-done.84.refs_5_ = bf16[6,32,256]{2,1,0:T(8,128)(2,1)S(1)} collective-permute-done((bf16[6,32,256]{2,1,0:T(8,128)(2,1)S(1)}, bf16[6,32,256]{2,1,0:T(8,128)(2,1)S(1)}, u32[]{:S(2)}, u32[]{:S(2)}) %collective-permute-start.84) | collective-permute-done | bytes 98336 | tf_op jit(solution)/shard_map/cond/branch_1_fun/ppermute | solution.py:390
  124.6 1.6 %collective-permute-start.86 = (f32[64,512]{1,0:T(8,128)S(1)}, f32[64,512]{1,0:T(8,128)S(1)}, u32[]{:S(2)}, u32[]{:S(2)}) collective-permute-start(f32[64,512]{1,0:T(8,128)S(1)} %add.87.refs_2_.refs_1_), channel_id=1, source_target_pairs={{0,8},{1,9},{2,10},{3,11},{4,12},{5,13},{6,14},{7,15},{8,0},{9,1},... | collective-permute-start | bytes 393224 | tf_op jit(solution)/shard_map/cond/branch_1_fun/ppermute | solution.py:408
  126.1 4.9 %collective-permute-done.89.refs_3_ = bf16[16,32,256]{2,1,0:T(8,128)(2,1)S(1)} collective-permute-done((bf16[16,32,256]{2,1,0:T(8,128)(2,1)S(1)}, bf16[16,32,256]{2,1,0:T(8,128)(2,1)S(1)}, u32[]{:S(2)}, u32[]{:S(2)}) %collective-permute-start.89) | collective-permute-done | bytes 262176 | tf_op jit(solution)/shard_map/cond/branch_1_fun/ppermute | solution.py:450
  131.1 1.3 place.9.refs_4_
  134.2 1.5 %place.10.refs_4_ = bf16[16,32,2048]{2,1,0:T(8,128)(2,1)} custom-call(s32[3]{0:T(128)S(1)} %get-tuple-element.270.refs_0_, f32[64,512]{1,0:T(8,128)S(1)} %add.88.refs_2_.refs_1_, bf16[16,32,512]{2,1,0:T(8,128)(2,1)S(1)} %unpack.10.refs_2_.refs_1_, bf16[16,32,512]{2,1,0:T(8,128)(2,1)S(1)} %collective-permute-done.88.refs_3_, ...), custom_call_target="tpu_custom_call", output_to_operand_aliasing={{}: (4, {})} | custom-call | flops 1 | bytes 1 | tf_op jit(solution)/shard_map/cond/branch_1_fun/place/pallas_call | solution.py:38
  135.8 1.4 place.11
  (92 shorter events, 25.3 us)
Async XLA Ops:
  1.6 10.4 %collective-permute-start.90 = (bf16[16,32,256]{2,1,0:T(8,128)(2,1)S(1)}, bf16[16,32,256]{2,1,0:T(8,128)(2,1)S(1)}, u32[]{:S(2)}, u32[]{:S(2)}) collective-permute-start(bf16[16,32,256]{2,1,0:T(8,128)(2,1)S(1)} %dynamic-slice_bitcast_fusion.10), channel_id=1, source_target_pairs={{0,16},{16,0},{1,17},{17,1},{2,18},{18,2},{3,19},{19,3},{4,20},{20... | collective-permute-start | bytes 786440 | tf_op jit(solution)/shard_map/ppermute | solution.py:492
  4.6 7.4 %collective-permute-start.91 = (bf16[48,512]{1,0:T(8,128)(2,1)}, bf16[48,512]{1,0:T(8,128)(2,1)S(1)}, u32[]{:S(2)}, u32[]{:S(2)}) collective-permute-start(bf16[48,512]{1,0:T(8,128)(2,1)} %bitcast.48), channel_id=1, source_target_pairs={{0,16},{16,0},{1,17},{17,1},{2,18},{18,2},{3,19},{19,3},{4,20},{20... | collective-permute-start | bytes 147464 | tf_op jit(solution)/shard_map/ppermute | solution.py:501
  13.8 14.3 %collective-permute-start.48 = (bf16[16,32,512]{2,1,0:T(8,128)(2,1)S(1)}, bf16[16,32,512]{2,1,0:T(8,128)(2,1)S(1)}, u32[]{:S(2)}, u32[]{:S(2)}) collective-permute-start(bf16[16,32,512]{2,1,0:T(8,128)(2,1)S(1)} %get-tuple-element.385), channel_id=1, source_target_pairs={{0,16},{16,0},{1,17},{17,1},{2,18},{18,2},{3,19},{19,3},{4,20},{20... | collective-permute-start | bytes 1572872 | tf_op jit(solution)/shard_map/cond/branch_1_fun/ppermute | solution.py:419
  18.1 7.5 %collective-permute-start.45 = (bf16[6,32,256]{2,1,0:T(8,128)(2,1)S(1)}, bf16[6,32,256]{2,1,0:T(8,128)(2,1)S(1)}, u32[]{:S(2)}, u32[]{:S(2)}) collective-permute-start(bf16[6,32,256]{2,1,0:T(8,128)(2,1)S(1)} %get-tuple-element.279), channel_id=1, source_target_pairs={{0,4},{1,5},{2,6},{3,7},{4,8},{5,9},{6,10},{7,11},{8,12},{9,13},{1... | collective-permute-start | bytes 294920 | tf_op jit(solution)/shard_map/cond/branch_1_fun/ppermute | solution.py:390
  19.8 8.4 %collective-permute-start.46 = (bf16[6,32,256]{2,1,0:T(8,128)(2,1)S(1)}, bf16[6,32,256]{2,1,0:T(8,128)(2,1)S(1)}, u32[]{:S(2)}, u32[]{:S(2)}) collective-permute-start(bf16[6,32,256]{2,1,0:T(8,128)(2,1)S(1)} %get-tuple-element.280), channel_id=1, source_target_pairs={{0,8},{1,9},{2,10},{3,11},{4,12},{5,13},{6,14},{7,15},{8,0},{9,1},... | collective-permute-start | bytes 294920 | tf_op jit(solution)/shard_map/cond/branch_1_fun/ppermute | solution.py:390
  22.3 5.8 %collective-permute-start.47 = (bf16[6,32,256]{2,1,0:T(8,128)(2,1)S(1)}, bf16[6,32,256]{2,1,0:T(8,128)(2,1)S(1)}, u32[]{:S(2)}, u32[]{:S(2)}) collective-permute-start(bf16[6,32,256]{2,1,0:T(8,128)(2,1)S(1)} %get-tuple-element.281), channel_id=1, source_target_pairs={{0,12},{1,13},{2,14},{3,15},{4,0},{5,1},{6,2},{7,3},{8,4},{9,5},{1... | collective-permute-start | bytes 294920 | tf_op jit(solution)/shard_map/cond/branch_1_fun/ppermute | solution.py:390
  29.6 4.4 %collective-permute-start.49 = (bf16[2,4,32,256]{3,2,1,0:T(8,128)(2,1)S(1)}, bf16[2,4,32,256]{3,2,1,0:T(8,128)(2,1)S(1)}, u32[]{:S(2)}, u32[]{:S(2)}) collective-permute-start(bf16[2,4,32,256]{3,2,1,0:T(8,128)(2,1)S(1)} %get-tuple-element.289), channel_id=1, source_target_pairs={{0,1},{1,0},{2,3},{3,2},{4,5},{5,4},{6,7},{7,6},{8,9},{9,8},{10,11... | collective-permute-start | bytes 393224 | tf_op jit(solution)/shard_map/cond/branch_1_fun/ppermute | solution.py:398
  29.7 14.8 %collective-permute-start.56 = (bf16[16,32,256]{2,1,0:T(8,128)(2,1)S(1)}, bf16[16,32,256]{2,1,0:T(8,128)(2,1)S(1)}, u32[]{:S(2)}, u32[]{:S(2)}) collective-permute-start(bf16[16,32,256]{2,1,0:T(8,128)(2,1)S(1)} %get-tuple-element.382), channel_id=1, source_target_pairs={{0,16},{16,0},{1,17},{17,1},{2,18},{18,2},{3,19},{19,3},{4,20},{20... | collective-permute-start | bytes 786440 | tf_op jit(solution)/shard_map/cond/branch_1_fun/ppermute | solution.py:419
  30.2 6.3 %collective-permute-start.50 = (bf16[2,4,32,256]{3,2,1,0:T(8,128)(2,1)S(1)}, bf16[2,4,32,256]{3,2,1,0:T(8,128)(2,1)S(1)}, u32[]{:S(2)}, u32[]{:S(2)}) collective-permute-start(bf16[2,4,32,256]{3,2,1,0:T(8,128)(2,1)S(1)} %get-tuple-element.290), channel_id=1, source_target_pairs={{0,2},{1,3},{2,0},{3,1},{4,6},{5,7},{6,4},{7,5},{8,10},{9,11},{10,... | collective-permute-start | bytes 393224 | tf_op jit(solution)/shard_map/cond/branch_1_fun/ppermute | solution.py:398
  31.8 6.0 %collective-permute-start.51 = (bf16[2,4,32,256]{3,2,1,0:T(8,128)(2,1)S(1)}, bf16[2,4,32,256]{3,2,1,0:T(8,128)(2,1)S(1)}, u32[]{:S(2)}, u32[]{:S(2)}) collective-permute-start(bf16[2,4,32,256]{3,2,1,0:T(8,128)(2,1)S(1)} %get-tuple-element.291), channel_id=1, source_target_pairs={{0,3},{1,2},{2,1},{3,0},{4,7},{5,6},{6,5},{7,4},{8,11},{9,10},{10,... | collective-permute-start | bytes 393224 | tf_op jit(solution)/shard_map/cond/branch_1_fun/ppermute | solution.py:398
  31.8 14.9 %collective-permute-start.53 = (bf16[6,32,512]{2,1,0:T(8,128)(2,1)S(1)}, bf16[6,32,512]{2,1,0:T(8,128)(2,1)S(1)}, u32[]{:S(2)}, u32[]{:S(2)}) collective-permute-start(bf16[6,32,512]{2,1,0:T(8,128)(2,1)S(1)} %get-tuple-element.295), channel_id=1, source_target_pairs={{0,4},{1,5},{2,6},{3,7},{4,8},{5,9},{6,10},{7,11},{8,12},{9,13},{1... | collective-permute-start | bytes 589832 | tf_op jit(solution)/shard_map/cond/branch_1_fun/ppermute | solution.py:390
  34.0 15.5 %collective-permute-start.54 = (bf16[6,32,512]{2,1,0:T(8,128)(2,1)S(1)}, bf16[6,32,512]{2,1,0:T(8,128)(2,1)S(1)}, u32[]{:S(2)}, u32[]{:S(2)}) collective-permute-start(bf16[6,32,512]{2,1,0:T(8,128)(2,1)S(1)} %get-tuple-element.296), channel_id=1, source_target_pairs={{0,8},{1,9},{2,10},{3,11},{4,12},{5,13},{6,14},{7,15},{8,0},{9,1},... | collective-permute-start | bytes 589832 | tf_op jit(solution)/shard_map/cond/branch_1_fun/ppermute | solution.py:390
  36.5 8.6 %collective-permute-start.52 = (f32[64,512]{1,0:T(8,128)S(1)}, f32[64,512]{1,0:T(8,128)S(1)}, u32[]{:S(2)}, u32[]{:S(2)}) collective-permute-start(f32[64,512]{1,0:T(8,128)S(1)} %project_embed.3.refs_2_.refs_1_), channel_id=1, source_target_pairs={{0,1},{1,0},{2,3},{3,2},{4,5},{5,4},{6,7},{7,6},{8,9},{9,8},{10,11... | collective-permute-start | bytes 393224 | tf_op jit(solution)/shard_map/cond/branch_1_fun/ppermute | solution.py:408
  37.8 13.3 %collective-permute-start.55 = (bf16[6,32,512]{2,1,0:T(8,128)(2,1)S(1)}, bf16[6,32,512]{2,1,0:T(8,128)(2,1)S(1)}, u32[]{:S(2)}, u32[]{:S(2)}) collective-permute-start(bf16[6,32,512]{2,1,0:T(8,128)(2,1)S(1)} %get-tuple-element.297), channel_id=1, source_target_pairs={{0,12},{1,13},{2,14},{3,15},{4,0},{5,1},{6,2},{7,3},{8,4},{9,5},{1... | collective-permute-start | bytes 589832 | tf_op jit(solution)/shard_map/cond/branch_1_fun/ppermute | solution.py:390
  44.5 26.8 %copy-start.4 = (f32[1,2,512,1024]{3,2,1,0:T(8,128)S(1)}, f32[1,2,512,1024]{3,2,1,0:T(8,128)}, u32[]{:S(2)}) copy-start(f32[1,2,512,1024]{3,2,1,0:T(8,128)} %get-tuple-element.293) | copy-start | bytes 12582916 | tf_op jit(solution)/shard_map/cond
  44.5 11.2 %collective-permute-start.61 = (bf16[2,4,32,256]{3,2,1,0:T(8,128)(2,1)S(1)}, bf16[2,4,32,256]{3,2,1,0:T(8,128)(2,1)S(1)}, u32[]{:S(2)}, u32[]{:S(2)}) collective-permute-start(bf16[2,4,32,256]{3,2,1,0:T(8,128)(2,1)S(1)} %get-tuple-element.305), channel_id=1, source_target_pairs={{0,1},{1,0},{2,3},{3,2},{4,5},{5,4},{6,7},{7,6},{8,9},{9,8},{10,11... | collective-permute-start | bytes 393224 | tf_op jit(solution)/shard_map/cond/branch_1_fun/ppermute | solution.py:398
  45.2 10.6 %collective-permute-start.62 = (bf16[2,4,32,256]{3,2,1,0:T(8,128)(2,1)S(1)}, bf16[2,4,32,256]{3,2,1,0:T(8,128)(2,1)S(1)}, u32[]{:S(2)}, u32[]{:S(2)}) collective-permute-start(bf16[2,4,32,256]{3,2,1,0:T(8,128)(2,1)S(1)} %get-tuple-element.306), channel_id=1, source_target_pairs={{0,2},{1,3},{2,0},{3,1},{4,6},{5,7},{6,4},{7,5},{8,10},{9,11},{10,... | collective-permute-start | bytes 393224 | tf_op jit(solution)/shard_map/cond/branch_1_fun/ppermute | solution.py:398
  46.7 10.8 %collective-permute-start.63 = (bf16[2,4,32,256]{3,2,1,0:T(8,128)(2,1)S(1)}, bf16[2,4,32,256]{3,2,1,0:T(8,128)(2,1)S(1)}, u32[]{:S(2)}, u32[]{:S(2)}) collective-permute-start(bf16[2,4,32,256]{3,2,1,0:T(8,128)(2,1)S(1)} %get-tuple-element.307), channel_id=1, source_target_pairs={{0,3},{1,2},{2,1},{3,0},{4,7},{5,6},{6,5},{7,4},{8,11},{9,10},{10,... | collective-permute-start | bytes 393224 | tf_op jit(solution)/shard_map/cond/branch_1_fun/ppermute | solution.py:398
  49.5 8.2 %collective-permute-start.57 = (f32[64,512]{1,0:T(8,128)S(1)}, f32[64,512]{1,0:T(8,128)S(1)}, u32[]{:S(2)}, u32[]{:S(2)}) collective-permute-start(f32[64,512]{1,0:T(8,128)S(1)} %add.85.refs_1_), channel_id=1, source_target_pairs={{0,2},{1,3},{2,0},{3,1},{4,6},{5,7},{6,4},{7,5},{8,10},{9,11},{10,... | collective-permute-start | bytes 393224 | tf_op jit(solution)/shard_map/cond/branch_1_fun/ppermute | solution.py:408
  51.9 8.8 %collective-permute-start.58 = (bf16[6,32,256]{2,1,0:T(8,128)(2,1)S(1)}, bf16[6,32,256]{2,1,0:T(8,128)(2,1)S(1)}, u32[]{:S(2)}, u32[]{:S(2)}) collective-permute-start(bf16[6,32,256]{2,1,0:T(8,128)(2,1)S(1)} %get-tuple-element.302), channel_id=1, source_target_pairs={{0,4},{1,5},{2,6},{3,7},{4,8},{5,9},{6,10},{7,11},{8,12},{9,13},{1... | collective-permute-start | bytes 294920 | tf_op jit(solution)/shard_map/cond/branch_1_fun/ppermute | solution.py:390
  55.7 14.3 %collective-permute-start.64 = (bf16[2,4,32,512]{3,2,1,0:T(8,128)(2,1)S(1)}, bf16[2,4,32,512]{3,2,1,0:T(8,128)(2,1)S(1)}, u32[]{:S(2)}, u32[]{:S(2)}) collective-permute-start(bf16[2,4,32,512]{3,2,1,0:T(8,128)(2,1)S(1)} %get-tuple-element.310), channel_id=1, source_target_pairs={{0,1},{1,0},{2,3},{3,2},{4,5},{5,4},{6,7},{7,6},{8,9},{9,8},{10,11... | collective-permute-start | bytes 786440 | tf_op jit(solution)/shard_map/cond/branch_1_fun/ppermute | solution.py:398
  55.8 15.4 %collective-permute-start.65 = (bf16[2,4,32,512]{3,2,1,0:T(8,128)(2,1)S(1)}, bf16[2,4,32,512]{3,2,1,0:T(8,128)(2,1)S(1)}, u32[]{:S(2)}, u32[]{:S(2)}) collective-permute-start(bf16[2,4,32,512]{3,2,1,0:T(8,128)(2,1)S(1)} %get-tuple-element.311), channel_id=1, source_target_pairs={{0,2},{1,3},{2,0},{3,1},{4,6},{5,7},{6,4},{7,5},{8,10},{9,11},{10,... | collective-permute-start | bytes 786440 | tf_op jit(solution)/shard_map/cond/branch_1_fun/ppermute | solution.py:398
  57.5 13.8 %collective-permute-start.66 = (bf16[2,4,32,512]{3,2,1,0:T(8,128)(2,1)S(1)}, bf16[2,4,32,512]{3,2,1,0:T(8,128)(2,1)S(1)}, u32[]{:S(2)}, u32[]{:S(2)}) collective-permute-start(bf16[2,4,32,512]{3,2,1,0:T(8,128)(2,1)S(1)} %get-tuple-element.312), channel_id=1, source_target_pairs={{0,3},{1,2},{2,1},{3,0},{4,7},{5,6},{6,5},{7,4},{8,11},{9,10},{10,... | collective-permute-start | bytes 786440 | tf_op jit(solution)/shard_map/cond/branch_1_fun/ppermute | solution.py:398
  57.6 8.0 %collective-permute-start.59 = (bf16[6,32,256]{2,1,0:T(8,128)(2,1)S(1)}, bf16[6,32,256]{2,1,0:T(8,128)(2,1)S(1)}, u32[]{:S(2)}, u32[]{:S(2)}) collective-permute-start(bf16[6,32,256]{2,1,0:T(8,128)(2,1)S(1)} %get-tuple-element.303), channel_id=1, source_target_pairs={{0,8},{1,9},{2,10},{3,11},{4,12},{5,13},{6,14},{7,15},{8,0},{9,1},... | collective-permute-start | bytes 294920 | tf_op jit(solution)/shard_map/cond/branch_1_fun/ppermute | solution.py:390
  60.7 6.8 %collective-permute-start.60 = (bf16[6,32,256]{2,1,0:T(8,128)(2,1)S(1)}, bf16[6,32,256]{2,1,0:T(8,128)(2,1)S(1)}, u32[]{:S(2)}, u32[]{:S(2)}) collective-permute-start(bf16[6,32,256]{2,1,0:T(8,128)(2,1)S(1)} %get-tuple-element.304), channel_id=1, source_target_pairs={{0,12},{1,13},{2,14},{3,15},{4,0},{5,1},{6,2},{7,3},{8,4},{9,5},{1... | collective-permute-start | bytes 294920 | tf_op jit(solution)/shard_map/cond/branch_1_fun/ppermute | solution.py:390
  68.8 8.0 %collective-permute-start.67 = (bf16[2,4,32,256]{3,2,1,0:T(8,128)(2,1)S(1)}, bf16[2,4,32,256]{3,2,1,0:T(8,128)(2,1)S(1)}, u32[]{:S(2)}, u32[]{:S(2)}) collective-permute-start(bf16[2,4,32,256]{3,2,1,0:T(8,128)(2,1)S(1)} %get-tuple-element.316), channel_id=1, source_target_pairs={{0,1},{1,0},{2,3},{3,2},{4,5},{5,4},{6,7},{7,6},{8,9},{9,8},{10,11... | collective-permute-start | bytes 393224 | tf_op jit(solution)/shard_map/cond/branch_1_fun/ppermute | solution.py:398
  68.9 7.0 %collective-permute-start.70 = (bf16[6,32,256]{2,1,0:T(8,128)(2,1)S(1)}, bf16[6,32,256]{2,1,0:T(8,128)(2,1)S(1)}, u32[]{:S(2)}, u32[]{:S(2)}) collective-permute-start(bf16[6,32,256]{2,1,0:T(8,128)(2,1)S(1)} %get-tuple-element.326), channel_id=1, source_target_pairs={{0,4},{1,5},{2,6},{3,7},{4,8},{5,9},{6,10},{7,11},{8,12},{9,13},{1... | collective-permute-start | bytes 294920 | tf_op jit(solution)/shard_map/cond/branch_1_fun/ppermute | solution.py:390
  69.9 7.0 %collective-permute-start.68 = (bf16[2,4,32,256]{3,2,1,0:T(8,128)(2,1)S(1)}, bf16[2,4,32,256]{3,2,1,0:T(8,128)(2,1)S(1)}, u32[]{:S(2)}, u32[]{:S(2)}) collective-permute-start(bf16[2,4,32,256]{3,2,1,0:T(8,128)(2,1)S(1)} %get-tuple-element.317), channel_id=1, source_target_pairs={{0,2},{1,3},{2,0},{3,1},{4,6},{5,7},{6,4},{7,5},{8,10},{9,11},{10,... | collective-permute-start | bytes 393224 | tf_op jit(solution)/shard_map/cond/branch_1_fun/ppermute | solution.py:398
  71.2 8.4 %collective-permute-start.69 = (bf16[2,4,32,256]{3,2,1,0:T(8,128)(2,1)S(1)}, bf16[2,4,32,256]{3,2,1,0:T(8,128)(2,1)S(1)}, u32[]{:S(2)}, u32[]{:S(2)}) collective-permute-start(bf16[2,4,32,256]{3,2,1,0:T(8,128)(2,1)S(1)} %get-tuple-element.318), channel_id=1, source_target_pairs={{0,3},{1,2},{2,1},{3,0},{4,7},{5,6},{6,5},{7,4},{8,11},{9,10},{10,... | collective-permute-start | bytes 393224 | tf_op jit(solution)/shard_map/cond/branch_1_fun/ppermute | solution.py:398
  74.7 13.5 %collective-permute-start.73 = (bf16[2,4,32,512]{3,2,1,0:T(8,128)(2,1)S(1)}, bf16[2,4,32,512]{3,2,1,0:T(8,128)(2,1)S(1)}, u32[]{:S(2)}, u32[]{:S(2)}) collective-permute-start(bf16[2,4,32,512]{3,2,1,0:T(8,128)(2,1)S(1)} %get-tuple-element.329), channel_id=1, source_target_pairs={{0,1},{1,0},{2,3},{3,2},{4,5},{5,4},{6,7},{7,6},{8,9},{9,8},{10,11... | collective-permute-start | bytes 786440 | tf_op jit(solution)/shard_map/cond/branch_1_fun/ppermute | solution.py:398
  75.9 12.4 %collective-permute-start.74 = (bf16[2,4,32,512]{3,2,1,0:T(8,128)(2,1)S(1)}, bf16[2,4,32,512]{3,2,1,0:T(8,128)(2,1)S(1)}, u32[]{:S(2)}, u32[]{:S(2)}) collective-permute-start(bf16[2,4,32,512]{3,2,1,0:T(8,128)(2,1)S(1)} %get-tuple-element.330), channel_id=1, source_target_pairs={{0,2},{1,3},{2,0},{3,1},{4,6},{5,7},{6,4},{7,5},{8,10},{9,11},{10,... | collective-permute-start | bytes 786440 | tf_op jit(solution)/shard_map/cond/branch_1_fun/ppermute | solution.py:398
  76.8 12.2 %collective-permute-start.75 = (bf16[2,4,32,512]{3,2,1,0:T(8,128)(2,1)S(1)}, bf16[2,4,32,512]{3,2,1,0:T(8,128)(2,1)S(1)}, u32[]{:S(2)}, u32[]{:S(2)}) collective-permute-start(bf16[2,4,32,512]{3,2,1,0:T(8,128)(2,1)S(1)} %get-tuple-element.331), channel_id=1, source_target_pairs={{0,3},{1,2},{2,1},{3,0},{4,7},{5,6},{6,5},{7,4},{8,11},{9,10},{10,... | collective-permute-start | bytes 786440 | tf_op jit(solution)/shard_map/cond/branch_1_fun/ppermute | solution.py:398
  77.0 8.7 %collective-permute-start.71 = (bf16[6,32,256]{2,1,0:T(8,128)(2,1)S(1)}, bf16[6,32,256]{2,1,0:T(8,128)(2,1)S(1)}, u32[]{:S(2)}, u32[]{:S(2)}) collective-permute-start(bf16[6,32,256]{2,1,0:T(8,128)(2,1)S(1)} %get-tuple-element.327), channel_id=1, source_target_pairs={{0,8},{1,9},{2,10},{3,11},{4,12},{5,13},{6,14},{7,15},{8,0},{9,1},... | collective-permute-start | bytes 294920 | tf_op jit(solution)/shard_map/cond/branch_1_fun/ppermute | solution.py:390
  79.5 7.1 %collective-permute-start.72 = (bf16[6,32,256]{2,1,0:T(8,128)(2,1)S(1)}, bf16[6,32,256]{2,1,0:T(8,128)(2,1)S(1)}, u32[]{:S(2)}, u32[]{:S(2)}) collective-permute-start(bf16[6,32,256]{2,1,0:T(8,128)(2,1)S(1)} %get-tuple-element.328), channel_id=1, source_target_pairs={{0,12},{1,13},{2,14},{3,15},{4,0},{5,1},{6,2},{7,3},{8,4},{9,5},{1... | collective-permute-start | bytes 294920 | tf_op jit(solution)/shard_map/cond/branch_1_fun/ppermute | solution.py:390
  85.7 9.3 %collective-permute-start.79 = (bf16[2,4,32,256]{3,2,1,0:T(8,128)(2,1)S(1)}, bf16[2,4,32,256]{3,2,1,0:T(8,128)(2,1)S(1)}, u32[]{:S(2)}, u32[]{:S(2)}) collective-permute-start(bf16[2,4,32,256]{3,2,1,0:T(8,128)(2,1)S(1)} %get-tuple-element.336), channel_id=1, source_target_pairs={{0,1},{1,0},{2,3},{3,2},{4,5},{5,4},{6,7},{7,6},{8,9},{9,8},{10,11... | collective-permute-start | bytes 393224 | tf_op jit(solution)/shard_map/cond/branch_1_fun/ppermute | solution.py:398
  86.6 9.4 %collective-permute-start.80 = (bf16[2,4,32,256]{3,2,1,0:T(8,128)(2,1)S(1)}, bf16[2,4,32,256]{3,2,1,0:T(8,128)(2,1)S(1)}, u32[]{:S(2)}, u32[]{:S(2)}) collective-permute-start(bf16[2,4,32,256]{3,2,1,0:T(8,128)(2,1)S(1)} %get-tuple-element.337), channel_id=1, source_target_pairs={{0,2},{1,3},{2,0},{3,1},{4,6},{5,7},{6,4},{7,5},{8,10},{9,11},{10,... | collective-permute-start | bytes 393224 | tf_op jit(solution)/shard_map/cond/branch_1_fun/ppermute | solution.py:398
  89.7 10.3 %collective-permute-start.76 = (bf16[6,32,512]{2,1,0:T(8,128)(2,1)S(1)}, bf16[6,32,512]{2,1,0:T(8,128)(2,1)S(1)}, u32[]{:S(2)}, u32[]{:S(2)}) collective-permute-start(bf16[6,32,512]{2,1,0:T(8,128)(2,1)S(1)} %get-tuple-element.333), channel_id=1, source_target_pairs={{0,4},{1,5},{2,6},{3,7},{4,8},{5,9},{6,10},{7,11},{8,12},{9,13},{1... | collective-permute-start | bytes 589832 | tf_op jit(solution)/shard_map/cond/branch_1_fun/ppermute | solution.py:390
  90.5 17.1 %collective-permute-start.77 = (bf16[6,32,512]{2,1,0:T(8,128)(2,1)S(1)}, bf16[6,32,512]{2,1,0:T(8,128)(2,1)S(1)}, u32[]{:S(2)}, u32[]{:S(2)}) collective-permute-start(bf16[6,32,512]{2,1,0:T(8,128)(2,1)S(1)} %get-tuple-element.334), channel_id=1, source_target_pairs={{0,8},{1,9},{2,10},{3,11},{4,12},{5,13},{6,14},{7,15},{8,0},{9,1},... | collective-permute-start | bytes 589832 | tf_op jit(solution)/shard_map/cond/branch_1_fun/ppermute | solution.py:390
  93.1 14.5 %collective-permute-start.78 = (bf16[6,32,512]{2,1,0:T(8,128)(2,1)S(1)}, bf16[6,32,512]{2,1,0:T(8,128)(2,1)S(1)}, u32[]{:S(2)}, u32[]{:S(2)}) collective-permute-start(bf16[6,32,512]{2,1,0:T(8,128)(2,1)S(1)} %get-tuple-element.335), channel_id=1, source_target_pairs={{0,12},{1,13},{2,14},{3,15},{4,0},{5,1},{6,2},{7,3},{8,4},{9,5},{1... | collective-permute-start | bytes 589832 | tf_op jit(solution)/shard_map/cond/branch_1_fun/ppermute | solution.py:390
  95.0 5.1 %collective-permute-start.81 = (bf16[2,4,32,256]{3,2,1,0:T(8,128)(2,1)S(1)}, bf16[2,4,32,256]{3,2,1,0:T(8,128)(2,1)S(1)}, u32[]{:S(2)}, u32[]{:S(2)}) collective-permute-start(bf16[2,4,32,256]{3,2,1,0:T(8,128)(2,1)S(1)} %get-tuple-element.338), channel_id=1, source_target_pairs={{0,3},{1,2},{2,1},{3,0},{4,7},{5,6},{6,5},{7,4},{8,11},{9,10},{10,... | collective-permute-start | bytes 393224 | tf_op jit(solution)/shard_map/cond/branch_1_fun/ppermute | solution.py:398
  96.0 13.8 %collective-permute-start.82 = (f32[64,512]{1,0:T(8,128)S(1)}, f32[64,512]{1,0:T(8,128)S(1)}, u32[]{:S(2)}, u32[]{:S(2)}) collective-permute-start(f32[64,512]{1,0:T(8,128)S(1)} %add.86.refs_3_.refs_1_), channel_id=1, source_target_pairs={{0,4},{1,5},{2,6},{3,7},{4,0},{5,1},{6,2},{7,3},{8,12},{9,13},{10,... | collective-permute-start | bytes 393224 | tf_op jit(solution)/shard_map/cond/branch_1_fun/ppermute | solution.py:408
  110.6 23.6 %collective-permute-start.88 = (bf16[16,32,512]{2,1,0:T(8,128)(2,1)S(1)}, bf16[16,32,512]{2,1,0:T(8,128)(2,1)S(1)}, u32[]{:S(2)}, u32[]{:S(2)}) collective-permute-start(bf16[16,32,512]{2,1,0:T(8,128)(2,1)S(1)} %unpack.10.refs_2_.refs_1_), channel_id=1, source_target_pairs={{0,16},{16,0},{1,17},{17,1},{2,18},{18,2},{3,19},{19,3},{4,20},{20... | collective-permute-start | bytes 1572872 | tf_op jit(solution)/shard_map/cond/branch_1_fun/ppermute | solution.py:450
  111.7 7.6 %collective-permute-start.83 = (bf16[6,32,256]{2,1,0:T(8,128)(2,1)S(1)}, bf16[6,32,256]{2,1,0:T(8,128)(2,1)S(1)}, u32[]{:S(2)}, u32[]{:S(2)}) collective-permute-start(bf16[6,32,256]{2,1,0:T(8,128)(2,1)S(1)} %get-tuple-element.340), channel_id=1, source_target_pairs={{0,4},{1,5},{2,6},{3,7},{4,8},{5,9},{6,10},{7,11},{8,12},{9,13},{1... | collective-permute-start | bytes 294920 | tf_op jit(solution)/shard_map/cond/branch_1_fun/ppermute | solution.py:390
  114.5 8.3 %collective-permute-start.84 = (bf16[6,32,256]{2,1,0:T(8,128)(2,1)S(1)}, bf16[6,32,256]{2,1,0:T(8,128)(2,1)S(1)}, u32[]{:S(2)}, u32[]{:S(2)}) collective-permute-start(bf16[6,32,256]{2,1,0:T(8,128)(2,1)S(1)} %get-tuple-element.341), channel_id=1, source_target_pairs={{0,8},{1,9},{2,10},{3,11},{4,12},{5,13},{6,14},{7,15},{8,0},{9,1},... | collective-permute-start | bytes 294920 | tf_op jit(solution)/shard_map/cond/branch_1_fun/ppermute | solution.py:390
  116.2 6.7 %collective-permute-start.85 = (bf16[6,32,256]{2,1,0:T(8,128)(2,1)S(1)}, bf16[6,32,256]{2,1,0:T(8,128)(2,1)S(1)}, u32[]{:S(2)}, u32[]{:S(2)}) collective-permute-start(bf16[6,32,256]{2,1,0:T(8,128)(2,1)S(1)} %get-tuple-element.342), channel_id=1, source_target_pairs={{0,12},{1,13},{2,14},{3,15},{4,0},{5,1},{6,2},{7,3},{8,4},{9,5},{1... | collective-permute-start | bytes 294920 | tf_op jit(solution)/shard_map/cond/branch_1_fun/ppermute | solution.py:390
  116.9 14.2 %collective-permute-start.89 = (bf16[16,32,256]{2,1,0:T(8,128)(2,1)S(1)}, bf16[16,32,256]{2,1,0:T(8,128)(2,1)S(1)}, u32[]{:S(2)}, u32[]{:S(2)}) collective-permute-start(bf16[16,32,256]{2,1,0:T(8,128)(2,1)S(1)} %unpack.9.refs_3_.refs_2_), channel_id=1, source_target_pairs={{0,16},{16,0},{1,17},{17,1},{2,18},{18,2},{3,19},{19,3},{4,20},{20... | collective-permute-start | bytes 786440 | tf_op jit(solution)/shard_map/cond/branch_1_fun/ppermute | solution.py:450
  123.5 12.2 %collective-permute-start.87 = (bf16[16,32,256]{2,1,0:T(8,128)(2,1)S(1)}, bf16[16,32,256]{2,1,0:T(8,128)(2,1)S(1)}, u32[]{:S(2)}, u32[]{:S(2)}) collective-permute-start(bf16[16,32,256]{2,1,0:T(8,128)(2,1)S(1)} %unpack.11.refs_0_.refs_1_.refs_2_), channel_id=1, source_target_pairs={{0,16},{16,0},{1,17},{17,1},{2,18},{18,2},{3,19},{19,3},{4,20},{20... | collective-permute-start | bytes 786440 | tf_op jit(solution)/shard_map/cond/branch_1_fun/ppermute | solution.py:450
  124.6 8.8 %collective-permute-start.86 = (f32[64,512]{1,0:T(8,128)S(1)}, f32[64,512]{1,0:T(8,128)S(1)}, u32[]{:S(2)}, u32[]{:S(2)}) collective-permute-start(f32[64,512]{1,0:T(8,128)S(1)} %add.87.refs_2_.refs_1_), channel_id=1, source_target_pairs={{0,8},{1,9},{2,10},{3,11},{4,12},{5,13},{6,14},{7,15},{8,0},{9,1},... | collective-permute-start | bytes 393224 | tf_op jit(solution)/shard_map/cond/branch_1_fun/ppermute | solution.py:408
  (7 other events, 124.0 us)

commit v4 on v3

--- a/solution.py
+++ b/solution.py
@@ -1,3 +1,5 @@
+import functools
+
 import jax
 import jax.numpy as jnp
 from jax import lax
@@ -11,10 +13,31 @@
 CHUNKS = ((4, 2), (0, 4), (6, 2))
 EMBED = None
 FIRST = 0
-ORDER = (
-    (0, 1), (1, 1, 0), (0, 2), (EMBED, 0), (0, 3), (EMBED, 0), (2, 1, 1), (1, 2), (EMBED, 0),
-    (0, 4, 2), (2, 2), (1, 3), (2, 3), (0, 5), (1, 4), (2, 4, 1), (EMBED, 0), (1, 5), (0, 6), (2, 5), (EMBED, 0),
-    (1, 6), (EMBED, 0), (2, 6),
+PLANS = (
+    (
+        5,
+        (
+            (0, 1), (0, 2), (EMBED, 0), (1, 1), (EMBED, 0), (0, 3), (2, 1, 1), (1, 2), (0, 4), (EMBED, 0), (2, 2),
+            (1, 3), (2, 3), (0, 5), (1, 4), (2, 4), (0, 6), (1, 5), (2, 5), (EMBED, 0), (2, 6), (1, 6), (EMBED, 0),
+            (EMBED, 0),
+        ),
+    ),
+    (
+        6,
+        (
+            (EMBED, 0), (0, 1), (1, 1), (EMBED, 0), (0, 2), (0, 3), (2, 1, 1), (1, 2), (EMBED, 0), (0, 4), (2, 2),
+            (1, 3), (2, 3), (0, 5), (1, 4), (2, 4, 1), (0, 6, 2), (EMBED, 0), (1, 5), (EMBED, 0), (1, 6, 2), (2, 5),
+            (2, 6), (EMBED, 0),
+        ),
+    ),
+    (
+        8,
+        (
+            (0, 1), (1, 1, 0), (0, 2), (EMBED, 0), (0, 3), (EMBED, 0), (2, 1, 1), (1, 2), (EMBED, 0), (0, 4, 2),
+            (2, 2), (1, 3), (2, 3), (0, 5), (1, 4), (2, 4, 1), (EMBED, 0), (1, 5), (0, 6), (2, 5), (EMBED, 0),
+            (1, 6), (EMBED, 0), (2, 6),
+        ),
+    ),
 )
 VMEM_LIMIT = 48 * 1024 * 1024
 
@@ -367,6 +390,7 @@
 
 def moved(
     slots,
+    order,
     local_shape,
     tables,
     first_columns,
@@ -420,7 +444,7 @@
     ]
     held.insert(FIRST, first_columns)
     state, new_rows, after = (), (), ()
-    for chunk, step, *waits in ORDER:
+    for chunk, step, *waits in order:
         for wait in waits:
             after += tuple(held[wait])
         if chunk == EMBED:
@@ -491,6 +515,7 @@
     swap = [(0, 1), (1, 0)]
     peer = lax.ppermute(outgoing, "group", swap)
     *tables, fullest = slot_tables(here, slab_owner, devices, capacity)
+    mine, pairs = lax.optimization_barrier((mine, pairs))
     operands = (
         (here, *tables),
         (mine, peer),
@@ -503,13 +528,11 @@
         momentum_embed,
         embed_basis,
     )
-    most = capacity * inside
-    fewer = most * 3 // 4
-    shape = local_rows.shape
-    results = lax.cond(
-        fullest[0] <= fewer,
-        lambda *values: moved(fewer, shape, *values),
-        lambda *values: moved(most, shape, *values),
+    most, shape = capacity * inside, local_rows.shape
+    counts = [most * eighths // 8 for eighths, _ in PLANS]
+    results = lax.switch(
+        sum((fullest[0] > count).astype(jnp.int32) for count in counts[:-1]),
+        [functools.partial(moved, n, order, shape) for n, (_, order) in zip(counts, PLANS)],
         *operands,
     )
     return tuple(

time: 138 us -> 128 us (0.928)
  starting transfers between devices: 58.2 us -> 53.1 us
  waiting for transfers between devices: 47.2 us -> 43 us
  local copies, waits for them, and re-layouts: 5.79 us -> 2.67 us
    ppermute x18, waiting for transfers between devices: 29.5 us -> 24.5 us  [over_planes(): lax.ppermute(parts[k], 'shard', [(i, (i + k * inside) % devices) for i in...]
    ppermute x18, starting transfers between devices: 35.3 us -> 32.7 us  [over_planes(): lax.ppermute(parts[k], 'shard', [(i, (i + k * inside) % devices) for i in...]
    dynamic_slice x3 -> x2, local copies, waits for them, and re-layouts: 4.48 us -> 2.64 us  [on_device(): lax.dynamic_slice_in_dim(local_rows, group * half + start * (half // 8),...]
    ppermute x18, waiting for transfers between devices: 6.34 us -> 7.75 us  [in_plane(): lax.ppermute(parts[m], 'shard', [(i, i ^ m) for i in range(devices)])]
  transfers between devices with their start and end apart: 47 -> 47, of which waited for: 19 -> 22; matrix products, arithmetic and copies ran while one was open for 1% -> 1% of each run, Pallas kernels for 16% -> 18%
where the time goes in v4:
time: 128 us; the launch traced here: 127 us
  starting transfers between devices  53.1 us (41%)
  waiting for transfers between devices  43 us (34%)
  Pallas kernels  25.2 us (20%)
  local copies, waits for them, and re-layouts  2.67 us (2%)
  between operations  2.22 us (2%)
    ppermute x18, starting transfers between devices, over_planes(): lax.ppermute(parts[k], 'shard', [(i, (i + k * inside) % devices) for i in...  32.7 us
    pallas_call x25, Pallas kernels, call(): pl.pallas_call(body, grid_spec=pltpu.PrefetchScalarGridSpec(num_scalar_pr...  25.2 us
    ppermute x18, waiting for transfers between devices, over_planes(): lax.ppermute(parts[k], 'shard', [(i, (i + k * inside) % devices) for i in...  24.5 us
    ppermute x18, starting transfers between devices, in_plane(): lax.ppermute(parts[m], 'shard', [(i, i ^ m) for i in range(devices)])  9.98 us
    ppermute x18, waiting for transfers between devices, in_plane(): lax.ppermute(parts[m], 'shard', [(i, i ^ m) for i in range(devices)])  7.75 us
    ppermute x3, waiting for transfers between devices, moved(): value = (token, lax.ppermute(token, 'group', swap))  5.9 us
    ppermute x1, starting transfers between devices, on_device(): peer = lax.ppermute(outgoing, 'group', swap)  3 us
    ppermute x3, starting transfers between devices, moved(): value = (token, lax.ppermute(token, 'group', swap))  2.69 us
  transfers between devices with their start and end apart: 47, of which 22 were waited for; matrix products, arithmetic and copies ran while one was open for 1% of the time, Pallas kernels for 18%

profile of v4, /device:TPU:0, one launch (start us, length us, event | category | flops | bytes accessed | tf_op | source)
XLA Modules:
  0.0 126.8 jit_solution(13769124149451335736)
XLA Ops:
  0.7 1.4 %dynamic-slice_bitcast_fusion.2 = (bf16[16,32,256]{2,1,0:T(8,128)(2,1)S(1)}, bf16[16,32,256]{2,1,0:T(8,128)(2,1)S(1)}, bf16[16,32,256]{2,1,0:T(8,128)(2,1)S(1)}, bf16[16,32,256]{2,1,0:T(8,128)(2,1)S(1)}) fusion(bf16[1,16,32,2048]{3,2,1,0:T(8,128)(2,1)} %param.11, s32[]{:T(128)S(6)} %select_n.36, s32[]{:T(128)S(6)} %select_n.34, s32[]{:T(128)S(6)} %select_n.31, ...), kind=kLoop, calls=%fused_computation.2 | loop fusion | bytes 2097168 | tf_op jit(solution)/shard_map/dynamic_slice | solution.py:508
  2.1 3.0 %collective-permute-start.135 = (bf16[16,32,256]{2,1,0:T(8,128)(2,1)S(1)}, bf16[16,32,256]{2,1,0:T(8,128)(2,1)S(1)}, u32[]{:S(2)}, u32[]{:S(2)}) collective-permute-start(bf16[16,32,256]{2,1,0:T(8,128)(2,1)S(1)} %get-tuple-element.383), channel_id=1, source_target_pairs={{0,16},{16,0},{1,17},{17,1},{2,18},{18,2},{3,19},{19,3},{4,20},{20... | collective-permute-start | bytes 786440 | tf_op jit(solution)/shard_map/ppermute | solution.py:516
  5.2 1.3 %dynamic-slice_bitcast_fusion = (bf16[16,32,512]{2,1,0:T(8,128)(2,1)S(1)}, bf16[16,32,512]{2,1,0:T(8,128)(2,1)S(1)}) fusion(bf16[1,16,32,2048]{3,2,1,0:T(8,128)(2,1)} %param.11, s32[]{:T(128)S(6)} %select_n.33, s32[]{:T(128)S(6)} %select_n.32), kind=kLoop, calls=%fused_computation | loop fusion | bytes 2097160 | tf_op jit(solution)/shard_map/dynamic_slice | solution.py:508
  6.5 1.9 %slot_tables.1 = (s32[4,8]{1,0:T(4,128)S(1)}, s32[4,8]{1,0:T(4,128)S(1)}, s32[4]{0:T(128)S(1)}, s32[4,2]{1,0:T(4,128)S(1)}, s32[4,2]{1,0:T(4,128)S(1)}, /*index=5*/s32[1]{0:T(128)}) custom-call(s32[3]{0:T(128)S(1)} %pad_add_fusion.refs_0_, s32[16]{0:T(128)S(1)} %copy-done), custom_call_target="tpu_custom_call" | custom-call | flops 1 | bytes 1 | tf_op jit(solution)/shard_map/slot_tables/pallas_call | solution.py:61
  9.8 2.7 %collective-permute-done.136 = bf16[48,512]{1,0:T(8,128)(2,1)S(1)} collective-permute-done((bf16[48,512]{1,0:T(8,128)(2,1)}, bf16[48,512]{1,0:T(8,128)(2,1)S(1)}, u32[]{:S(2)}, u32[]{:S(2)}) %collective-permute-start.136) | collective-permute-done | bytes 49184 | tf_op jit(solution)/shard_map/ppermute | solution.py:526
  12.5 114.2 %conditional.1 = (f32[2,512,1024]{2,1,0:T(8,128)}, f32[2,512,1024]{2,1,0:T(8,128)}, f32[48,512]{1,0:T(8,128)}, f32[48,512]{1,0:T(8,128)}, bf16[48,512]{1,0:T(8,128)(2,1)}, /*index=5*/bf16[1,16,32,2048]{3,2,1,0:T(8,128)(2,1)}) conditional(s32[]{:T(128)} %bitcast.6, (s32[4,8]{1,0:T(4,128)S(1)}, bf16[16,32,256]{2,1,0:T(8,128)(2,1)S(1)}, ...), branch_computations={%region_0.1_spmd, %region_1.2_spmd, %region_2.3_spmd} | conditional | flops 24 | bytes 68159352 | solution.py:533
  12.5 1.8 %collective-permute-start.3 = (bf16[16,32,512]{2,1,0:T(8,128)(2,1)S(1)}, bf16[16,32,512]{2,1,0:T(8,128)(2,1)S(1)}, u32[]{:S(2)}, u32[]{:S(2)}) collective-permute-start(bf16[16,32,512]{2,1,0:T(8,128)(2,1)S(1)} %get-tuple-element.131), channel_id=1, source_target_pairs={{0,16},{16,0},{1,17},{17,1},{2,18},{18,2},{3,19},{19,3},{4,20},{20... | collective-permute-start | bytes 1572872 | tf_op jit(solution)/shard_map/cond/branch_0_fun/ppermute | solution.py:443
  15.0 1.6 %collective-permute-start = (bf16[5,32,256]{2,1,0:T(8,128)(2,1)S(1)}, bf16[5,32,256]{2,1,0:T(8,128)(2,1)S(1)}, u32[]{:S(2)}, u32[]{:S(2)}) collective-permute-start(bf16[5,32,256]{2,1,0:T(8,128)(2,1)S(1)} %get-tuple-element.122), channel_id=1, source_target_pairs={{0,4},{1,5},{2,6},{3,7},{4,8},{5,9},{6,10},{7,11},{8,12},{9,13},{1... | collective-permute-start | bytes 245768 | tf_op jit(solution)/shard_map/cond/branch_0_fun/ppermute | solution.py:414
  16.7 2.6 %collective-permute-start.1 = (bf16[5,32,256]{2,1,0:T(8,128)(2,1)S(1)}, bf16[5,32,256]{2,1,0:T(8,128)(2,1)S(1)}, u32[]{:S(2)}, u32[]{:S(2)}) collective-permute-start(bf16[5,32,256]{2,1,0:T(8,128)(2,1)S(1)} %get-tuple-element.123), channel_id=1, source_target_pairs={{0,8},{1,9},{2,10},{3,11},{4,12},{5,13},{6,14},{7,15},{8,0},{9,1},... | collective-permute-start | bytes 245768 | tf_op jit(solution)/shard_map/cond/branch_0_fun/ppermute | solution.py:414
  19.3 1.3 %collective-permute-start.2 = (bf16[5,32,256]{2,1,0:T(8,128)(2,1)S(1)}, bf16[5,32,256]{2,1,0:T(8,128)(2,1)S(1)}, u32[]{:S(2)}, u32[]{:S(2)}) collective-permute-start(bf16[5,32,256]{2,1,0:T(8,128)(2,1)S(1)} %get-tuple-element.124), channel_id=1, source_target_pairs={{0,12},{1,13},{2,14},{3,15},{4,0},{5,1},{6,2},{7,3},{8,4},{9,5},{1... | collective-permute-start | bytes 245768 | tf_op jit(solution)/shard_map/cond/branch_0_fun/ppermute | solution.py:414
  20.6 1.6 %collective-permute-done.refs_4_ = bf16[5,32,256]{2,1,0:T(8,128)(2,1)S(1)} collective-permute-done((bf16[5,32,256]{2,1,0:T(8,128)(2,1)S(1)}, bf16[5,32,256]{2,1,0:T(8,128)(2,1)S(1)}, u32[]{:S(2)}, u32[]{:S(2)}) %collective-permute-start) | collective-permute-done | bytes 81952 | tf_op jit(solution)/shard_map/cond/branch_0_fun/ppermute | solution.py:414
  22.2 2.2 %collective-permute-done.1.refs_5_ = bf16[5,32,256]{2,1,0:T(8,128)(2,1)S(1)} collective-permute-done((bf16[5,32,256]{2,1,0:T(8,128)(2,1)S(1)}, bf16[5,32,256]{2,1,0:T(8,128)(2,1)S(1)}, u32[]{:S(2)}, u32[]{:S(2)}) %collective-permute-start.1) | collective-permute-done | bytes 81952 | tf_op jit(solution)/shard_map/cond/branch_0_fun/ppermute | solution.py:414
  26.1 1.6 %collective-permute-start.6 = (bf16[2,4,32,256]{3,2,1,0:T(8,128)(2,1)S(1)}, bf16[2,4,32,256]{3,2,1,0:T(8,128)(2,1)S(1)}, u32[]{:S(2)}, u32[]{:S(2)}) collective-permute-start(bf16[2,4,32,256]{3,2,1,0:T(8,128)(2,1)S(1)} %get-tuple-element.134), channel_id=1, source_target_pairs={{0,2},{1,3},{2,0},{3,1},{4,6},{5,7},{6,4},{7,5},{8,10},{9,11},{10,... | collective-permute-start | bytes 393224 | tf_op jit(solution)/shard_map/cond/branch_0_fun/ppermute | solution.py:422
  28.5 1.5 %collective-permute-start.8 = (bf16[5,32,512]{2,1,0:T(8,128)(2,1)S(1)}, bf16[5,32,512]{2,1,0:T(8,128)(2,1)S(1)}, u32[]{:S(2)}, u32[]{:S(2)}) collective-permute-start(bf16[5,32,512]{2,1,0:T(8,128)(2,1)S(1)} %get-tuple-element.139), channel_id=1, source_target_pairs={{0,4},{1,5},{2,6},{3,7},{4,8},{5,9},{6,10},{7,11},{8,12},{9,13},{1... | collective-permute-start | bytes 491528 | tf_op jit(solution)/shard_map/cond/branch_0_fun/ppermute | solution.py:414
  30.0 2.2 %collective-permute-start.9 = (bf16[5,32,512]{2,1,0:T(8,128)(2,1)S(1)}, bf16[5,32,512]{2,1,0:T(8,128)(2,1)S(1)}, u32[]{:S(2)}, u32[]{:S(2)}) collective-permute-start(bf16[5,32,512]{2,1,0:T(8,128)(2,1)S(1)} %get-tuple-element.140), channel_id=1, source_target_pairs={{0,8},{1,9},{2,10},{3,11},{4,12},{5,13},{6,14},{7,15},{8,0},{9,1},... | collective-permute-start | bytes 491528 | tf_op jit(solution)/shard_map/cond/branch_0_fun/ppermute | solution.py:414
  32.2 2.7 %collective-permute-start.10 = (bf16[5,32,512]{2,1,0:T(8,128)(2,1)S(1)}, bf16[5,32,512]{2,1,0:T(8,128)(2,1)S(1)}, u32[]{:S(2)}, u32[]{:S(2)}) collective-permute-start(bf16[5,32,512]{2,1,0:T(8,128)(2,1)S(1)} %get-tuple-element.141), channel_id=1, source_target_pairs={{0,12},{1,13},{2,14},{3,15},{4,0},{5,1},{6,2},{7,3},{8,4},{9,5},{1... | collective-permute-start | bytes 491528 | tf_op jit(solution)/shard_map/cond/branch_0_fun/ppermute | solution.py:414
  35.7 1.4 %collective-permute-start.15 = (f32[64,512]{1,0:T(8,128)S(1)}, f32[64,512]{1,0:T(8,128)S(1)}, u32[]{:S(2)}, u32[]{:S(2)}) collective-permute-start(f32[64,512]{1,0:T(8,128)S(1)} %add.75.refs_2_.refs_1_), channel_id=1, source_target_pairs={{0,2},{1,3},{2,0},{3,1},{4,6},{5,7},{6,4},{7,5},{8,10},{9,11},{10,... | collective-permute-start | bytes 393224 | tf_op jit(solution)/shard_map/cond/branch_0_fun/ppermute | solution.py:432
  37.1 3.6 %update_chunk.9 = (f32[2,512,1024]{2,1,0:T(8,128)}, f32[2,512,1024]{2,1,0:T(8,128)}, bf16[2,4,32,256]{3,2,1,0:T(8,128)(2,1)S(1)}, bf16[2,4,32,256]{3,2,1,0:T(8,1...) custom-call(s32[3]{0:T(128)S(1)} %get-tuple-element.115.refs_0_, ...), custom_call_target="tpu_custom_call" | custom-call | flops 1 | bytes 1 | tf_op jit(solution)/shard_map/cond/branch_0_fun/update_chunk/pallas_call | solution.py:61
  41.5 2.0 %collective-permute-done.9.refs_4_.refs_5_ = bf16[5,32,512]{2,1,0:T(8,128)(2,1)S(1)} collective-permute-done((bf16[5,32,512]{2,1,0:T(8,128)(2,1)S(1)}, bf16[5,32,512]{2,1,0:T(8,128)(2,1)S(1)}, u32[]{:S(2)}, u32[]{:S(2)}) %collective-permute-start.9) | collective-permute-done | bytes 163872 | tf_op jit(solution)/shard_map/cond/branch_0_fun/ppermute | solution.py:414
  45.6 3.5 %collective-permute-start.16 = (bf16[5,32,256]{2,1,0:T(8,128)(2,1)S(1)}, bf16[5,32,256]{2,1,0:T(8,128)(2,1)S(1)}, u32[]{:S(2)}, u32[]{:S(2)}) collective-permute-start(bf16[5,32,256]{2,1,0:T(8,128)(2,1)S(1)} %get-tuple-element.150), channel_id=1, source_target_pairs={{0,4},{1,5},{2,6},{3,7},{4,8},{5,9},{6,10},{7,11},{8,12},{9,13},{1... | collective-permute-start | bytes 245768 | tf_op jit(solution)/shard_map/cond/branch_0_fun/ppermute | solution.py:414
  49.6 1.0 collective-permute-start.21
  50.7 1.2 collective-permute-start.17
  52.8 1.8 %collective-permute-start.18 = (bf16[5,32,256]{2,1,0:T(8,128)(2,1)S(1)}, bf16[5,32,256]{2,1,0:T(8,128)(2,1)S(1)}, u32[]{:S(2)}, u32[]{:S(2)}) collective-permute-start(bf16[5,32,256]{2,1,0:T(8,128)(2,1)S(1)} %get-tuple-element.152), channel_id=1, source_target_pairs={{0,12},{1,13},{2,14},{3,15},{4,0},{5,1},{6,2},{7,3},{8,4},{9,5},{1... | collective-permute-start | bytes 245768 | tf_op jit(solution)/shard_map/cond/branch_0_fun/ppermute | solution.py:414
  55.3 2.6 %collective-permute-done.17.refs_5_ = bf16[5,32,256]{2,1,0:T(8,128)(2,1)S(1)} collective-permute-done((bf16[5,32,256]{2,1,0:T(8,128)(2,1)S(1)}, bf16[5,32,256]{2,1,0:T(8,128)(2,1)S(1)}, u32[]{:S(2)}, u32[]{:S(2)}) %collective-permute-start.17) | collective-permute-done | bytes 81952 | tf_op jit(solution)/shard_map/cond/branch_0_fun/ppermute | solution.py:414
  60.2 1.0 collective-permute-start.24
  61.3 1.1 collective-permute-done.21.refs_6_
  62.4 3.5 %update_chunk.10 = (f32[2,512,1024]{2,1,0:T(8,128)}, f32[2,512,1024]{2,1,0:T(8,128)}, bf16[2,4,32,512]{3,2,1,0:T(8,128)(2,1)S(1)}, bf16[2,4,32,512]{3,2,1,0:T(8,...) custom-call(s32[3]{0:T(128)S(1)} %get-tuple-element.115.refs_0_, ...), custom_call_target="tpu_custom_call", output_to_operand_aliasing={{0}: (9, {}), {1}: (10, {})} | custom-call | flops 1 | bytes 1 | tf_op jit(solution)/shard_map/cond/branch_0_fun/update_chunk/pallas_call | solution.py:61
  65.8 1.2 collective-permute-start.28
  67.1 1.2 collective-permute-start.30
  68.4 2.0 %collective-permute-start.26 = (bf16[5,32,256]{2,1,0:T(8,128)(2,1)S(1)}, bf16[5,32,256]{2,1,0:T(8,128)(2,1)S(1)}, u32[]{:S(2)}, u32[]{:S(2)}) collective-permute-start(bf16[5,32,256]{2,1,0:T(8,128)(2,1)S(1)} %get-tuple-element.171), channel_id=1, source_target_pairs={{0,8},{1,9},{2,10},{3,11},{4,12},{5,13},{6,14},{7,15},{8,0},{9,1},... | collective-permute-start | bytes 245768 | tf_op jit(solution)/shard_map/cond/branch_0_fun/ppermute | solution.py:414
  70.4 2.3 %update_chunk.11 = (f32[2,512,1024]{2,1,0:T(8,128)}, f32[2,512,1024]{2,1,0:T(8,128)}, bf16[2,4,32,256]{3,2,1,0:T(8,128)(2,1)S(1)}, bf16[2,4,32,256]{3,2,1,0:T(8,...) custom-call(s32[3]{0:T(128)S(1)} %get-tuple-element.115.refs_0_, ...), custom_call_target="tpu_custom_call", output_to_operand_aliasing={{0}: (9, {}), {1}: (10, {})} | custom-call | flops 1 | bytes 1 | tf_op jit(solution)/shard_map/cond/branch_0_fun/update_chunk/pallas_call | solution.py:61
  72.7 2.9 %collective-permute-done.25.refs_4_ = bf16[5,32,256]{2,1,0:T(8,128)(2,1)S(1)} collective-permute-done((bf16[5,32,256]{2,1,0:T(8,128)(2,1)S(1)}, bf16[5,32,256]{2,1,0:T(8,128)(2,1)S(1)}, u32[]{:S(2)}, u32[]{:S(2)}) %collective-permute-start.25) | collective-permute-done | bytes 81952 | tf_op jit(solution)/shard_map/cond/branch_0_fun/ppermute | solution.py:414
  75.6 2.4 %collective-permute-done.26.refs_5_ = bf16[5,32,256]{2,1,0:T(8,128)(2,1)S(1)} collective-permute-done((bf16[5,32,256]{2,1,0:T(8,128)(2,1)S(1)}, bf16[5,32,256]{2,1,0:T(8,128)(2,1)S(1)}, u32[]{:S(2)}, u32[]{:S(2)}) %collective-permute-start.26) | collective-permute-done | bytes 81952 | tf_op jit(solution)/shard_map/cond/branch_0_fun/ppermute | solution.py:414
  78.0 1.7 %collective-permute-start.27 = (bf16[5,32,256]{2,1,0:T(8,128)(2,1)S(1)}, bf16[5,32,256]{2,1,0:T(8,128)(2,1)S(1)}, u32[]{:S(2)}, u32[]{:S(2)}) collective-permute-start(bf16[5,32,256]{2,1,0:T(8,128)(2,1)S(1)} %get-tuple-element.172), channel_id=1, source_target_pairs={{0,12},{1,13},{2,14},{3,15},{4,0},{5,1},{6,2},{7,3},{8,4},{9,5},{1... | collective-permute-start | bytes 245768 | tf_op jit(solution)/shard_map/cond/branch_0_fun/ppermute | solution.py:414
  79.7 2.7 %collective-permute-done.27.refs_6_ = bf16[5,32,256]{2,1,0:T(8,128)(2,1)S(1)} collective-permute-done((bf16[5,32,256]{2,1,0:T(8,128)(2,1)S(1)}, bf16[5,32,256]{2,1,0:T(8,128)(2,1)S(1)}, u32[]{:S(2)}, u32[]{:S(2)}) %collective-permute-start.27) | collective-permute-done | bytes 81952 | tf_op jit(solution)/shard_map/cond/branch_0_fun/ppermute | solution.py:414
  83.9 4.1 %collective-permute-start.35 = (bf16[5,32,512]{2,1,0:T(8,128)(2,1)S(1)}, bf16[5,32,512]{2,1,0:T(8,128)(2,1)S(1)}, u32[]{:S(2)}, u32[]{:S(2)}) collective-permute-start(bf16[5,32,512]{2,1,0:T(8,128)(2,1)S(1)} %get-tuple-element.182), channel_id=1, source_target_pairs={{0,8},{1,9},{2,10},{3,11},{4,12},{5,13},{6,14},{7,15},{8,0},{9,1},... | collective-permute-start | bytes 491528 | tf_op jit(solution)/shard_map/cond/branch_0_fun/ppermute | solution.py:414
  88.8 5.3 %collective-permute-done.32.refs_6_ = bf16[2,4,32,256]{3,2,1,0:T(8,128)(2,1)S(1)} collective-permute-done((bf16[2,4,32,256]{3,2,1,0:T(8,128)(2,1)S(1)}, bf16[2,4,32,256]{3,2,1,0:T(8,128)(2,1)S(1)}, u32[]{:S(2)}, u32[]{:S(2)}) %collective-permute-start.32) | collective-permute-done | bytes 131104 | tf_op jit(solution)/shard_map/cond/branch_0_fun/ppermute | solution.py:422
  95.3 2.4 %collective-permute-done.35.refs_5_ = bf16[5,32,512]{2,1,0:T(8,128)(2,1)S(1)} collective-permute-done((bf16[5,32,512]{2,1,0:T(8,128)(2,1)S(1)}, bf16[5,32,512]{2,1,0:T(8,128)(2,1)S(1)}, u32[]{:S(2)}, u32[]{:S(2)}) %collective-permute-start.35) | collective-permute-done | bytes 163872 | tf_op jit(solution)/shard_map/cond/branch_0_fun/ppermute | solution.py:414
  98.5 1.6 %collective-permute-start.42 = (bf16[16,32,512]{2,1,0:T(8,128)(2,1)S(1)}, bf16[16,32,512]{2,1,0:T(8,128)(2,1)S(1)}, u32[]{:S(2)}, u32[]{:S(2)}) collective-permute-start(bf16[16,32,512]{2,1,0:T(8,128)(2,1)S(1)} %unpack.10.refs_2_), channel_id=1, source_target_pairs={{0,16},{16,0},{1,17},{17,1},{2,18},{18,2},{3,19},{19,3},{4,20},{20... | collective-permute-start | bytes 1572872 | tf_op jit(solution)/shard_map/cond/branch_0_fun/ppermute | solution.py:474
  100.0 4.0 %collective-permute-start.37 = (bf16[5,32,256]{2,1,0:T(8,128)(2,1)S(1)}, bf16[5,32,256]{2,1,0:T(8,128)(2,1)S(1)}, u32[]{:S(2)}, u32[]{:S(2)}) collective-permute-start(bf16[5,32,256]{2,1,0:T(8,128)(2,1)S(1)} %get-tuple-element.184), channel_id=1, source_target_pairs={{0,4},{1,5},{2,6},{3,7},{4,8},{5,9},{6,10},{7,11},{8,12},{9,13},{1... | collective-permute-start | bytes 245768 | tf_op jit(solution)/shard_map/cond/branch_0_fun/ppermute | solution.py:414
  104.1 2.2 %collective-permute-start.39 = (bf16[5,32,256]{2,1,0:T(8,128)(2,1)S(1)}, bf16[5,32,256]{2,1,0:T(8,128)(2,1)S(1)}, u32[]{:S(2)}, u32[]{:S(2)}) collective-permute-start(bf16[5,32,256]{2,1,0:T(8,128)(2,1)S(1)} %get-tuple-element.186), channel_id=1, source_target_pairs={{0,12},{1,13},{2,14},{3,15},{4,0},{5,1},{6,2},{7,3},{8,4},{9,5},{1... | collective-permute-start | bytes 245768 | tf_op jit(solution)/shard_map/cond/branch_0_fun/ppermute | solution.py:414
  107.4 3.4 %collective-permute-done.38.refs_5_ = bf16[5,32,256]{2,1,0:T(8,128)(2,1)S(1)} collective-permute-done((bf16[5,32,256]{2,1,0:T(8,128)(2,1)S(1)}, bf16[5,32,256]{2,1,0:T(8,128)(2,1)S(1)}, u32[]{:S(2)}, u32[]{:S(2)}) %collective-permute-start.38) | collective-permute-done | bytes 81952 | tf_op jit(solution)/shard_map/cond/branch_0_fun/ppermute | solution.py:414
  113.0 1.0 collective-permute-start.41
  114.0 5.0 %collective-permute-done.44.refs_3_ = bf16[16,32,256]{2,1,0:T(8,128)(2,1)S(1)} collective-permute-done((bf16[16,32,256]{2,1,0:T(8,128)(2,1)S(1)}, bf16[16,32,256]{2,1,0:T(8,128)(2,1)S(1)}, u32[]{:S(2)}, u32[]{:S(2)}) %collective-permute-start.44) | collective-permute-done | bytes 262176 | tf_op jit(solution)/shard_map/cond/branch_0_fun/ppermute | solution.py:474
  118.9 1.3 %place.9.refs_4_ = bf16[16,32,2048]{2,1,0:T(8,128)(2,1)} custom-call(s32[3]{0:T(128)S(1)} %get-tuple-element.115.refs_0_, bf16[5,32,256]{2,1,0:T(8,128)(2,1)S(1)} %get-tuple-element.180.refs_2_.refs_3_.refs_1_, bf16[16,32,256]{2,1,0:T(8,128)(2,1)S(1)} %unpack.9.refs_3_.refs_2_, bf16[16,32,256]{2,1,0:T(8,128)(2,1)S(1)} %collective-permute-done.44.refs_3_), custom_call_target="tpu_custom_call" | custom-call | flops 1 | bytes 1 | tf_op jit(solution)/shard_map/cond/branch_0_fun/place/pallas_call | solution.py:61
  120.3 1.3 %collective-permute-done.41.refs_2_ = f32[64,512]{1,0:T(8,128)S(1)} collective-permute-done((f32[64,512]{1,0:T(8,128)S(1)}, f32[64,512]{1,0:T(8,128)S(1)}, u32[]{:S(2)}, u32[]{:S(2)}) %collective-permute-start.41) | collective-permute-done | bytes 131104 | tf_op jit(solution)/shard_map/cond/branch_0_fun/ppermute | solution.py:432
  123.5 1.3 %place.10.refs_4_ = bf16[16,32,2048]{2,1,0:T(8,128)(2,1)} custom-call(s32[3]{0:T(128)S(1)} %get-tuple-element.115.refs_0_, f32[64,512]{1,0:T(8,128)S(1)} %add.77.refs_1_, bf16[16,32,256]{2,1,0:T(8,128)(2,1)S(1)} %unpack.11.refs_0_.refs_2_.refs_1_, bf16[16,32,256]{2,1,0:T(8,128)(2,1)S(1)} %collective-permute-done.43.refs_3_, ...), custom_call_target="tpu_custom_call", output_to_operand_aliasing={{}: (4, {})} | custom-call | flops 1 | bytes 1 | tf_op jit(solution)/shard_map/cond/branch_0_fun/place/pallas_call | solution.py:61
  124.9 1.5 %place.11 = bf16[16,32,2048]{2,1,0:T(8,128)(2,1)} custom-call(s32[3]{0:T(128)S(1)} %get-tuple-element.115.refs_0_, bf16[16,32,256]{2,1,0:T(8,128)(2,1)S(1)} %unpack.11.refs_0_.refs_2_.refs_1_, bf16[16,32,512]{2,1,0:T(8,128)(2,1)S(1)} %unpack.10.refs_2_, bf16[16,32,512]{2,1,0:T(8,128)(2,1)S(1)} %collective-permute-done.42.refs_3_, ...), custom_call_target="tpu_custom_call", output_to_operand_aliasing={{}: (4, {})} | custom-call | flops 1 | bytes 1 | tf_op jit(solution)/shard_map/cond/branch_0_fun/place/pallas_call | solution.py:61
  (89 shorter events, 21.0 us)
Async XLA Ops:
  2.1 10.4 %collective-permute-start.135 = (bf16[16,32,256]{2,1,0:T(8,128)(2,1)S(1)}, bf16[16,32,256]{2,1,0:T(8,128)(2,1)S(1)}, u32[]{:S(2)}, u32[]{:S(2)}) collective-permute-start(bf16[16,32,256]{2,1,0:T(8,128)(2,1)S(1)} %get-tuple-element.383), channel_id=1, source_target_pairs={{0,16},{16,0},{1,17},{17,1},{2,18},{18,2},{3,19},{19,3},{4,20},{20... | collective-permute-start | bytes 786440 | tf_op jit(solution)/shard_map/ppermute | solution.py:516
  5.1 7.4 %collective-permute-start.136 = (bf16[48,512]{1,0:T(8,128)(2,1)}, bf16[48,512]{1,0:T(8,128)(2,1)S(1)}, u32[]{:S(2)}, u32[]{:S(2)}) collective-permute-start(bf16[48,512]{1,0:T(8,128)(2,1)} %bitcast.31), channel_id=1, source_target_pairs={{0,16},{16,0},{1,17},{17,1},{2,18},{18,2},{3,19},{19,3},{4,20},{20... | collective-permute-start | bytes 147464 | tf_op jit(solution)/shard_map/ppermute | solution.py:526
  12.5 15.2 %collective-permute-start.3 = (bf16[16,32,512]{2,1,0:T(8,128)(2,1)S(1)}, bf16[16,32,512]{2,1,0:T(8,128)(2,1)S(1)}, u32[]{:S(2)}, u32[]{:S(2)}) collective-permute-start(bf16[16,32,512]{2,1,0:T(8,128)(2,1)S(1)} %get-tuple-element.131), channel_id=1, source_target_pairs={{0,16},{16,0},{1,17},{17,1},{2,18},{18,2},{3,19},{19,3},{4,20},{20... | collective-permute-start | bytes 1572872 | tf_op jit(solution)/shard_map/cond/branch_0_fun/ppermute | solution.py:443
  15.0 7.1 %collective-permute-start = (bf16[5,32,256]{2,1,0:T(8,128)(2,1)S(1)}, bf16[5,32,256]{2,1,0:T(8,128)(2,1)S(1)}, u32[]{:S(2)}, u32[]{:S(2)}) collective-permute-start(bf16[5,32,256]{2,1,0:T(8,128)(2,1)S(1)} %get-tuple-element.122), channel_id=1, source_target_pairs={{0,4},{1,5},{2,6},{3,7},{4,8},{5,9},{6,10},{7,11},{8,12},{9,13},{1... | collective-permute-start | bytes 245768 | tf_op jit(solution)/shard_map/cond/branch_0_fun/ppermute | solution.py:414
  16.7 7.7 %collective-permute-start.1 = (bf16[5,32,256]{2,1,0:T(8,128)(2,1)S(1)}, bf16[5,32,256]{2,1,0:T(8,128)(2,1)S(1)}, u32[]{:S(2)}, u32[]{:S(2)}) collective-permute-start(bf16[5,32,256]{2,1,0:T(8,128)(2,1)S(1)} %get-tuple-element.123), channel_id=1, source_target_pairs={{0,8},{1,9},{2,10},{3,11},{4,12},{5,13},{6,14},{7,15},{8,0},{9,1},... | collective-permute-start | bytes 245768 | tf_op jit(solution)/shard_map/cond/branch_0_fun/ppermute | solution.py:414
  19.3 5.1 %collective-permute-start.2 = (bf16[5,32,256]{2,1,0:T(8,128)(2,1)S(1)}, bf16[5,32,256]{2,1,0:T(8,128)(2,1)S(1)}, u32[]{:S(2)}, u32[]{:S(2)}) collective-permute-start(bf16[5,32,256]{2,1,0:T(8,128)(2,1)S(1)} %get-tuple-element.124), channel_id=1, source_target_pairs={{0,12},{1,13},{2,14},{3,15},{4,0},{5,1},{6,2},{7,3},{8,4},{9,5},{1... | collective-permute-start | bytes 245768 | tf_op jit(solution)/shard_map/cond/branch_0_fun/ppermute | solution.py:414
  25.3 4.7 %collective-permute-start.4 = (f32[64,512]{1,0:T(8,128)S(1)}, f32[64,512]{1,0:T(8,128)S(1)}, u32[]{:S(2)}, u32[]{:S(2)}) collective-permute-start(f32[64,512]{1,0:T(8,128)S(1)} %project_embed.3.refs_1_), channel_id=1, source_target_pairs={{0,1},{1,0},{2,3},{3,2},{4,5},{5,4},{6,7},{7,6},{8,9},{9,8},{10,11... | collective-permute-start | bytes 393224 | tf_op jit(solution)/shard_map/cond/branch_0_fun/ppermute | solution.py:432
  25.4 15.3 %collective-permute-start.11 = (bf16[16,32,256]{2,1,0:T(8,128)(2,1)S(1)}, bf16[16,32,256]{2,1,0:T(8,128)(2,1)S(1)}, u32[]{:S(2)}, u32[]{:S(2)}) collective-permute-start(bf16[16,32,256]{2,1,0:T(8,128)(2,1)S(1)} %get-tuple-element.143), channel_id=1, source_target_pairs={{0,16},{16,0},{1,17},{17,1},{2,18},{18,2},{3,19},{19,3},{4,20},{20... | collective-permute-start | bytes 786440 | tf_op jit(solution)/shard_map/cond/branch_0_fun/ppermute | solution.py:443
  25.9 4.1 %collective-permute-start.5 = (bf16[2,4,32,256]{3,2,1,0:T(8,128)(2,1)S(1)}, bf16[2,4,32,256]{3,2,1,0:T(8,128)(2,1)S(1)}, u32[]{:S(2)}, u32[]{:S(2)}) collective-permute-start(bf16[2,4,32,256]{3,2,1,0:T(8,128)(2,1)S(1)} %get-tuple-element.133), channel_id=1, source_target_pairs={{0,1},{1,0},{2,3},{3,2},{4,5},{5,4},{6,7},{7,6},{8,9},{9,8},{10,11... | collective-permute-start | bytes 393224 | tf_op jit(solution)/shard_map/cond/branch_0_fun/ppermute | solution.py:422
  26.1 6.1 %collective-permute-start.6 = (bf16[2,4,32,256]{3,2,1,0:T(8,128)(2,1)S(1)}, bf16[2,4,32,256]{3,2,1,0:T(8,128)(2,1)S(1)}, u32[]{:S(2)}, u32[]{:S(2)}) collective-permute-start(bf16[2,4,32,256]{3,2,1,0:T(8,128)(2,1)S(1)} %get-tuple-element.134), channel_id=1, source_target_pairs={{0,2},{1,3},{2,0},{3,1},{4,6},{5,7},{6,4},{7,5},{8,10},{9,11},{10,... | collective-permute-start | bytes 393224 | tf_op jit(solution)/shard_map/cond/branch_0_fun/ppermute | solution.py:422
  28.5 12.3 %collective-permute-start.8 = (bf16[5,32,512]{2,1,0:T(8,128)(2,1)S(1)}, bf16[5,32,512]{2,1,0:T(8,128)(2,1)S(1)}, u32[]{:S(2)}, u32[]{:S(2)}) collective-permute-start(bf16[5,32,512]{2,1,0:T(8,128)(2,1)S(1)} %get-tuple-element.139), channel_id=1, source_target_pairs={{0,4},{1,5},{2,6},{3,7},{4,8},{5,9},{6,10},{7,11},{8,12},{9,13},{1... | collective-permute-start | bytes 491528 | tf_op jit(solution)/shard_map/cond/branch_0_fun/ppermute | solution.py:414
  30.0 5.8 %collective-permute-start.7 = (bf16[2,4,32,256]{3,2,1,0:T(8,128)(2,1)S(1)}, bf16[2,4,32,256]{3,2,1,0:T(8,128)(2,1)S(1)}, u32[]{:S(2)}, u32[]{:S(2)}) collective-permute-start(bf16[2,4,32,256]{3,2,1,0:T(8,128)(2,1)S(1)} %get-tuple-element.135), channel_id=1, source_target_pairs={{0,3},{1,2},{2,1},{3,0},{4,7},{5,6},{6,5},{7,4},{8,11},{9,10},{10,... | collective-permute-start | bytes 393224 | tf_op jit(solution)/shard_map/cond/branch_0_fun/ppermute | solution.py:422
  30.0 13.6 %collective-permute-start.9 = (bf16[5,32,512]{2,1,0:T(8,128)(2,1)S(1)}, bf16[5,32,512]{2,1,0:T(8,128)(2,1)S(1)}, u32[]{:S(2)}, u32[]{:S(2)}) collective-permute-start(bf16[5,32,512]{2,1,0:T(8,128)(2,1)S(1)} %get-tuple-element.140), channel_id=1, source_target_pairs={{0,8},{1,9},{2,10},{3,11},{4,12},{5,13},{6,14},{7,15},{8,0},{9,1},... | collective-permute-start | bytes 491528 | tf_op jit(solution)/shard_map/cond/branch_0_fun/ppermute | solution.py:414
  32.2 11.5 %collective-permute-start.10 = (bf16[5,32,512]{2,1,0:T(8,128)(2,1)S(1)}, bf16[5,32,512]{2,1,0:T(8,128)(2,1)S(1)}, u32[]{:S(2)}, u32[]{:S(2)}) collective-permute-start(bf16[5,32,512]{2,1,0:T(8,128)(2,1)S(1)} %get-tuple-element.141), channel_id=1, source_target_pairs={{0,12},{1,13},{2,14},{3,15},{4,0},{5,1},{6,2},{7,3},{8,4},{9,5},{1... | collective-permute-start | bytes 491528 | tf_op jit(solution)/shard_map/cond/branch_0_fun/ppermute | solution.py:414
  35.7 9.9 %collective-permute-start.15 = (f32[64,512]{1,0:T(8,128)S(1)}, f32[64,512]{1,0:T(8,128)S(1)}, u32[]{:S(2)}, u32[]{:S(2)}) collective-permute-start(f32[64,512]{1,0:T(8,128)S(1)} %add.75.refs_2_.refs_1_), channel_id=1, source_target_pairs={{0,2},{1,3},{2,0},{3,1},{4,6},{5,7},{6,4},{7,5},{8,10},{9,11},{10,... | collective-permute-start | bytes 393224 | tf_op jit(solution)/shard_map/cond/branch_0_fun/ppermute | solution.py:432
  37.1 25.3 %copy-start.4 = (f32[2,512,1024]{2,1,0:T(8,128)S(1)}, f32[2,512,1024]{2,1,0:T(8,128)}, u32[]{:S(2)}) copy-start(f32[2,512,1024]{2,1,0:T(8,128)} %get-tuple-element.137.refs_8_) | copy-start | bytes 12582916 | tf_op jit(solution)/shard_map/cond
  40.7 8.4 %collective-permute-start.12 = (bf16[2,4,32,256]{3,2,1,0:T(8,128)(2,1)S(1)}, bf16[2,4,32,256]{3,2,1,0:T(8,128)(2,1)S(1)}, u32[]{:S(2)}, u32[]{:S(2)}) collective-permute-start(bf16[2,4,32,256]{3,2,1,0:T(8,128)(2,1)S(1)} %get-tuple-element.146), channel_id=1, source_target_pairs={{0,1},{1,0},{2,3},{3,2},{4,5},{5,4},{6,7},{7,6},{8,9},{9,8},{10,11... | collective-permute-start | bytes 393224 | tf_op jit(solution)/shard_map/cond/branch_0_fun/ppermute | solution.py:422
  40.7 8.9 %collective-permute-start.13 = (bf16[2,4,32,256]{3,2,1,0:T(8,128)(2,1)S(1)}, bf16[2,4,32,256]{3,2,1,0:T(8,128)(2,1)S(1)}, u32[]{:S(2)}, u32[]{:S(2)}) collective-permute-start(bf16[2,4,32,256]{3,2,1,0:T(8,128)(2,1)S(1)} %get-tuple-element.147), channel_id=1, source_target_pairs={{0,2},{1,3},{2,0},{3,1},{4,6},{5,7},{6,4},{7,5},{8,10},{9,11},{10,... | collective-permute-start | bytes 393224 | tf_op jit(solution)/shard_map/cond/branch_0_fun/ppermute | solution.py:422
  43.5 7.1 %collective-permute-start.14 = (bf16[2,4,32,256]{3,2,1,0:T(8,128)(2,1)S(1)}, bf16[2,4,32,256]{3,2,1,0:T(8,128)(2,1)S(1)}, u32[]{:S(2)}, u32[]{:S(2)}) collective-permute-start(bf16[2,4,32,256]{3,2,1,0:T(8,128)(2,1)S(1)} %get-tuple-element.148), channel_id=1, source_target_pairs={{0,3},{1,2},{2,1},{3,0},{4,7},{5,6},{6,5},{7,4},{8,11},{9,10},{10,... | collective-permute-start | bytes 393224 | tf_op jit(solution)/shard_map/cond/branch_0_fun/ppermute | solution.py:422
  45.1 15.1 %collective-permute-start.19 = (bf16[2,4,32,512]{3,2,1,0:T(8,128)(2,1)S(1)}, bf16[2,4,32,512]{3,2,1,0:T(8,128)(2,1)S(1)}, u32[]{:S(2)}, u32[]{:S(2)}) collective-permute-start(bf16[2,4,32,512]{3,2,1,0:T(8,128)(2,1)S(1)} %get-tuple-element.154), channel_id=1, source_target_pairs={{0,1},{1,0},{2,3},{3,2},{4,5},{5,4},{6,7},{7,6},{8,9},{9,8},{10,11... | collective-permute-start | bytes 786440 | tf_op jit(solution)/shard_map/cond/branch_0_fun/ppermute | solution.py:422
  45.6 7.2 %collective-permute-start.16 = (bf16[5,32,256]{2,1,0:T(8,128)(2,1)S(1)}, bf16[5,32,256]{2,1,0:T(8,128)(2,1)S(1)}, u32[]{:S(2)}, u32[]{:S(2)}) collective-permute-start(bf16[5,32,256]{2,1,0:T(8,128)(2,1)S(1)} %get-tuple-element.150), channel_id=1, source_target_pairs={{0,4},{1,5},{2,6},{3,7},{4,8},{5,9},{6,10},{7,11},{8,12},{9,13},{1... | collective-permute-start | bytes 245768 | tf_op jit(solution)/shard_map/cond/branch_0_fun/ppermute | solution.py:414
  49.1 12.1 %collective-permute-start.20 = (bf16[2,4,32,512]{3,2,1,0:T(8,128)(2,1)S(1)}, bf16[2,4,32,512]{3,2,1,0:T(8,128)(2,1)S(1)}, u32[]{:S(2)}, u32[]{:S(2)}) collective-permute-start(bf16[2,4,32,512]{3,2,1,0:T(8,128)(2,1)S(1)} %get-tuple-element.155), channel_id=1, source_target_pairs={{0,2},{1,3},{2,0},{3,1},{4,6},{5,7},{6,4},{7,5},{8,10},{9,11},{10,... | collective-permute-start | bytes 786440 | tf_op jit(solution)/shard_map/cond/branch_0_fun/ppermute | solution.py:422
  49.6 12.7 %collective-permute-start.21 = (bf16[2,4,32,512]{3,2,1,0:T(8,128)(2,1)S(1)}, bf16[2,4,32,512]{3,2,1,0:T(8,128)(2,1)S(1)}, u32[]{:S(2)}, u32[]{:S(2)}) collective-permute-start(bf16[2,4,32,512]{3,2,1,0:T(8,128)(2,1)S(1)} %get-tuple-element.156), channel_id=1, source_target_pairs={{0,3},{1,2},{2,1},{3,0},{4,7},{5,6},{6,5},{7,4},{8,11},{9,10},{10,... | collective-permute-start | bytes 786440 | tf_op jit(solution)/shard_map/cond/branch_0_fun/ppermute | solution.py:422
  50.7 7.2 %collective-permute-start.17 = (bf16[5,32,256]{2,1,0:T(8,128)(2,1)S(1)}, bf16[5,32,256]{2,1,0:T(8,128)(2,1)S(1)}, u32[]{:S(2)}, u32[]{:S(2)}) collective-permute-start(bf16[5,32,256]{2,1,0:T(8,128)(2,1)S(1)} %get-tuple-element.151), channel_id=1, source_target_pairs={{0,8},{1,9},{2,10},{3,11},{4,12},{5,13},{6,14},{7,15},{8,0},{9,1},... | collective-permute-start | bytes 245768 | tf_op jit(solution)/shard_map/cond/branch_0_fun/ppermute | solution.py:414
  52.8 5.9 %collective-permute-start.18 = (bf16[5,32,256]{2,1,0:T(8,128)(2,1)S(1)}, bf16[5,32,256]{2,1,0:T(8,128)(2,1)S(1)}, u32[]{:S(2)}, u32[]{:S(2)}) collective-permute-start(bf16[5,32,256]{2,1,0:T(8,128)(2,1)S(1)} %get-tuple-element.152), channel_id=1, source_target_pairs={{0,12},{1,13},{2,14},{3,15},{4,0},{5,1},{6,2},{7,3},{8,4},{9,5},{1... | collective-permute-start | bytes 245768 | tf_op jit(solution)/shard_map/cond/branch_0_fun/ppermute | solution.py:414
  59.3 7.8 %collective-permute-start.22 = (bf16[2,4,32,256]{3,2,1,0:T(8,128)(2,1)S(1)}, bf16[2,4,32,256]{3,2,1,0:T(8,128)(2,1)S(1)}, u32[]{:S(2)}, u32[]{:S(2)}) collective-permute-start(bf16[2,4,32,256]{3,2,1,0:T(8,128)(2,1)S(1)} %get-tuple-element.160), channel_id=1, source_target_pairs={{0,1},{1,0},{2,3},{3,2},{4,5},{5,4},{6,7},{7,6},{8,9},{9,8},{10,11... | collective-permute-start | bytes 393224 | tf_op jit(solution)/shard_map/cond/branch_0_fun/ppermute | solution.py:422
  59.4 9.0 %collective-permute-start.23 = (bf16[2,4,32,256]{3,2,1,0:T(8,128)(2,1)S(1)}, bf16[2,4,32,256]{3,2,1,0:T(8,128)(2,1)S(1)}, u32[]{:S(2)}, u32[]{:S(2)}) collective-permute-start(bf16[2,4,32,256]{3,2,1,0:T(8,128)(2,1)S(1)} %get-tuple-element.161), channel_id=1, source_target_pairs={{0,2},{1,3},{2,0},{3,1},{4,6},{5,7},{6,4},{7,5},{8,10},{9,11},{10,... | collective-permute-start | bytes 393224 | tf_op jit(solution)/shard_map/cond/branch_0_fun/ppermute | solution.py:422
  60.2 8.1 %collective-permute-start.24 = (bf16[2,4,32,256]{3,2,1,0:T(8,128)(2,1)S(1)}, bf16[2,4,32,256]{3,2,1,0:T(8,128)(2,1)S(1)}, u32[]{:S(2)}, u32[]{:S(2)}) collective-permute-start(bf16[2,4,32,256]{3,2,1,0:T(8,128)(2,1)S(1)} %get-tuple-element.162), channel_id=1, source_target_pairs={{0,3},{1,2},{2,1},{3,0},{4,7},{5,6},{6,5},{7,4},{8,11},{9,10},{10,... | collective-permute-start | bytes 393224 | tf_op jit(solution)/shard_map/cond/branch_0_fun/ppermute | solution.py:422
  65.8 17.3 %collective-permute-start.28 = (bf16[2,4,32,512]{3,2,1,0:T(8,128)(2,1)S(1)}, bf16[2,4,32,512]{3,2,1,0:T(8,128)(2,1)S(1)}, u32[]{:S(2)}, u32[]{:S(2)}) collective-permute-start(bf16[2,4,32,512]{3,2,1,0:T(8,128)(2,1)S(1)} %get-tuple-element.173), channel_id=1, source_target_pairs={{0,1},{1,0},{2,3},{3,2},{4,5},{5,4},{6,7},{7,6},{8,9},{9,8},{10,11... | collective-permute-start | bytes 786440 | tf_op jit(solution)/shard_map/cond/branch_0_fun/ppermute | solution.py:422
  67.0 16.2 %collective-permute-start.29 = (bf16[2,4,32,512]{3,2,1,0:T(8,128)(2,1)S(1)}, bf16[2,4,32,512]{3,2,1,0:T(8,128)(2,1)S(1)}, u32[]{:S(2)}, u32[]{:S(2)}) collective-permute-start(bf16[2,4,32,512]{3,2,1,0:T(8,128)(2,1)S(1)} %get-tuple-element.174), channel_id=1, source_target_pairs={{0,2},{1,3},{2,0},{3,1},{4,6},{5,7},{6,4},{7,5},{8,10},{9,11},{10,... | collective-permute-start | bytes 786440 | tf_op jit(solution)/shard_map/cond/branch_0_fun/ppermute | solution.py:422
  67.1 16.0 %collective-permute-start.30 = (bf16[2,4,32,512]{3,2,1,0:T(8,128)(2,1)S(1)}, bf16[2,4,32,512]{3,2,1,0:T(8,128)(2,1)S(1)}, u32[]{:S(2)}, u32[]{:S(2)}) collective-permute-start(bf16[2,4,32,512]{3,2,1,0:T(8,128)(2,1)S(1)} %get-tuple-element.175), channel_id=1, source_target_pairs={{0,3},{1,2},{2,1},{3,0},{4,7},{5,6},{6,5},{7,4},{8,11},{9,10},{10,... | collective-permute-start | bytes 786440 | tf_op jit(solution)/shard_map/cond/branch_0_fun/ppermute | solution.py:422
  68.4 7.2 %collective-permute-start.25 = (bf16[5,32,256]{2,1,0:T(8,128)(2,1)S(1)}, bf16[5,32,256]{2,1,0:T(8,128)(2,1)S(1)}, u32[]{:S(2)}, u32[]{:S(2)}) collective-permute-start(bf16[5,32,256]{2,1,0:T(8,128)(2,1)S(1)} %get-tuple-element.170), channel_id=1, source_target_pairs={{0,4},{1,5},{2,6},{3,7},{4,8},{5,9},{6,10},{7,11},{8,12},{9,13},{1... | collective-permute-start | bytes 245768 | tf_op jit(solution)/shard_map/cond/branch_0_fun/ppermute | solution.py:414
  68.4 9.6 %collective-permute-start.26 = (bf16[5,32,256]{2,1,0:T(8,128)(2,1)S(1)}, bf16[5,32,256]{2,1,0:T(8,128)(2,1)S(1)}, u32[]{:S(2)}, u32[]{:S(2)}) collective-permute-start(bf16[5,32,256]{2,1,0:T(8,128)(2,1)S(1)} %get-tuple-element.171), channel_id=1, source_target_pairs={{0,8},{1,9},{2,10},{3,11},{4,12},{5,13},{6,14},{7,15},{8,0},{9,1},... | collective-permute-start | bytes 245768 | tf_op jit(solution)/shard_map/cond/branch_0_fun/ppermute | solution.py:414
  75.6 13.3 %collective-permute-start.31 = (bf16[2,4,32,256]{3,2,1,0:T(8,128)(2,1)S(1)}, bf16[2,4,32,256]{3,2,1,0:T(8,128)(2,1)S(1)}, u32[]{:S(2)}, u32[]{:S(2)}) collective-permute-start(bf16[2,4,32,256]{3,2,1,0:T(8,128)(2,1)S(1)} %get-tuple-element.177), channel_id=1, source_target_pairs={{0,1},{1,0},{2,3},{3,2},{4,5},{5,4},{6,7},{7,6},{8,9},{9,8},{10,11... | collective-permute-start | bytes 393224 | tf_op jit(solution)/shard_map/cond/branch_0_fun/ppermute | solution.py:422
  78.0 4.4 %collective-permute-start.27 = (bf16[5,32,256]{2,1,0:T(8,128)(2,1)S(1)}, bf16[5,32,256]{2,1,0:T(8,128)(2,1)S(1)}, u32[]{:S(2)}, u32[]{:S(2)}) collective-permute-start(bf16[5,32,256]{2,1,0:T(8,128)(2,1)S(1)} %get-tuple-element.172), channel_id=1, source_target_pairs={{0,12},{1,13},{2,14},{3,15},{4,0},{5,1},{6,2},{7,3},{8,4},{9,5},{1... | collective-permute-start | bytes 245768 | tf_op jit(solution)/shard_map/cond/branch_0_fun/ppermute | solution.py:414
  83.9 11.5 %collective-permute-start.34 = (bf16[5,32,512]{2,1,0:T(8,128)(2,1)S(1)}, bf16[5,32,512]{2,1,0:T(8,128)(2,1)S(1)}, u32[]{:S(2)}, u32[]{:S(2)}) collective-permute-start(bf16[5,32,512]{2,1,0:T(8,128)(2,1)S(1)} %get-tuple-element.181), channel_id=1, source_target_pairs={{0,4},{1,5},{2,6},{3,7},{4,8},{5,9},{6,10},{7,11},{8,12},{9,13},{1... | collective-permute-start | bytes 491528 | tf_op jit(solution)/shard_map/cond/branch_0_fun/ppermute | solution.py:414
  83.9 13.8 %collective-permute-start.35 = (bf16[5,32,512]{2,1,0:T(8,128)(2,1)S(1)}, bf16[5,32,512]{2,1,0:T(8,128)(2,1)S(1)}, u32[]{:S(2)}, u32[]{:S(2)}) collective-permute-start(bf16[5,32,512]{2,1,0:T(8,128)(2,1)S(1)} %get-tuple-element.182), channel_id=1, source_target_pairs={{0,8},{1,9},{2,10},{3,11},{4,12},{5,13},{6,14},{7,15},{8,0},{9,1},... | collective-permute-start | bytes 491528 | tf_op jit(solution)/shard_map/cond/branch_0_fun/ppermute | solution.py:414
  88.0 9.7 %collective-permute-start.36 = (bf16[5,32,512]{2,1,0:T(8,128)(2,1)S(1)}, bf16[5,32,512]{2,1,0:T(8,128)(2,1)S(1)}, u32[]{:S(2)}, u32[]{:S(2)}) collective-permute-start(bf16[5,32,512]{2,1,0:T(8,128)(2,1)S(1)} %get-tuple-element.183), channel_id=1, source_target_pairs={{0,12},{1,13},{2,14},{3,15},{4,0},{5,1},{6,2},{7,3},{8,4},{9,5},{1... | collective-permute-start | bytes 491528 | tf_op jit(solution)/shard_map/cond/branch_0_fun/ppermute | solution.py:414
  88.0 6.1 %collective-permute-start.32 = (bf16[2,4,32,256]{3,2,1,0:T(8,128)(2,1)S(1)}, bf16[2,4,32,256]{3,2,1,0:T(8,128)(2,1)S(1)}, u32[]{:S(2)}, u32[]{:S(2)}) collective-permute-start(bf16[2,4,32,256]{3,2,1,0:T(8,128)(2,1)S(1)} %get-tuple-element.178), channel_id=1, source_target_pairs={{0,2},{1,3},{2,0},{3,1},{4,6},{5,7},{6,4},{7,5},{8,10},{9,11},{10,... | collective-permute-start | bytes 393224 | tf_op jit(solution)/shard_map/cond/branch_0_fun/ppermute | solution.py:422
  88.8 5.8 %collective-permute-start.33 = (bf16[2,4,32,256]{3,2,1,0:T(8,128)(2,1)S(1)}, bf16[2,4,32,256]{3,2,1,0:T(8,128)(2,1)S(1)}, u32[]{:S(2)}, u32[]{:S(2)}) collective-permute-start(bf16[2,4,32,256]{3,2,1,0:T(8,128)(2,1)S(1)} %get-tuple-element.179), channel_id=1, source_target_pairs={{0,3},{1,2},{2,1},{3,0},{4,7},{5,6},{6,5},{7,4},{8,11},{9,10},{10,... | collective-permute-start | bytes 393224 | tf_op jit(solution)/shard_map/cond/branch_0_fun/ppermute | solution.py:422
  98.5 26.4 %collective-permute-start.42 = (bf16[16,32,512]{2,1,0:T(8,128)(2,1)S(1)}, bf16[16,32,512]{2,1,0:T(8,128)(2,1)S(1)}, u32[]{:S(2)}, u32[]{:S(2)}) collective-permute-start(bf16[16,32,512]{2,1,0:T(8,128)(2,1)S(1)} %unpack.10.refs_2_), channel_id=1, source_target_pairs={{0,16},{16,0},{1,17},{17,1},{2,18},{18,2},{3,19},{19,3},{4,20},{20... | collective-permute-start | bytes 1572872 | tf_op jit(solution)/shard_map/cond/branch_0_fun/ppermute | solution.py:474
  100.0 6.8 %collective-permute-start.37 = (bf16[5,32,256]{2,1,0:T(8,128)(2,1)S(1)}, bf16[5,32,256]{2,1,0:T(8,128)(2,1)S(1)}, u32[]{:S(2)}, u32[]{:S(2)}) collective-permute-start(bf16[5,32,256]{2,1,0:T(8,128)(2,1)S(1)} %get-tuple-element.184), channel_id=1, source_target_pairs={{0,4},{1,5},{2,6},{3,7},{4,8},{5,9},{6,10},{7,11},{8,12},{9,13},{1... | collective-permute-start | bytes 245768 | tf_op jit(solution)/shard_map/cond/branch_0_fun/ppermute | solution.py:414
  104.0 6.8 %collective-permute-start.38 = (bf16[5,32,256]{2,1,0:T(8,128)(2,1)S(1)}, bf16[5,32,256]{2,1,0:T(8,128)(2,1)S(1)}, u32[]{:S(2)}, u32[]{:S(2)}) collective-permute-start(bf16[5,32,256]{2,1,0:T(8,128)(2,1)S(1)} %get-tuple-element.185), channel_id=1, source_target_pairs={{0,8},{1,9},{2,10},{3,11},{4,12},{5,13},{6,14},{7,15},{8,0},{9,1},... | collective-permute-start | bytes 245768 | tf_op jit(solution)/shard_map/cond/branch_0_fun/ppermute | solution.py:414
  104.1 6.7 %collective-permute-start.39 = (bf16[5,32,256]{2,1,0:T(8,128)(2,1)S(1)}, bf16[5,32,256]{2,1,0:T(8,128)(2,1)S(1)}, u32[]{:S(2)}, u32[]{:S(2)}) collective-permute-start(bf16[5,32,256]{2,1,0:T(8,128)(2,1)S(1)} %get-tuple-element.186), channel_id=1, source_target_pairs={{0,12},{1,13},{2,14},{3,15},{4,0},{5,1},{6,2},{7,3},{8,4},{9,5},{1... | collective-permute-start | bytes 245768 | tf_op jit(solution)/shard_map/cond/branch_0_fun/ppermute | solution.py:414
  106.3 6.6 %collective-permute-start.40 = (f32[64,512]{1,0:T(8,128)S(1)}, f32[64,512]{1,0:T(8,128)S(1)}, u32[]{:S(2)}, u32[]{:S(2)}) collective-permute-start(f32[64,512]{1,0:T(8,128)S(1)} %add.76.refs_2_.refs_1_), channel_id=1, source_target_pairs={{0,4},{1,5},{2,6},{3,7},{4,0},{5,1},{6,2},{7,3},{8,12},{9,13},{10,... | collective-permute-start | bytes 393224 | tf_op jit(solution)/shard_map/cond/branch_0_fun/ppermute | solution.py:432
  106.9 12.1 %collective-permute-start.44 = (bf16[16,32,256]{2,1,0:T(8,128)(2,1)S(1)}, bf16[16,32,256]{2,1,0:T(8,128)(2,1)S(1)}, u32[]{:S(2)}, u32[]{:S(2)}) collective-permute-start(bf16[16,32,256]{2,1,0:T(8,128)(2,1)S(1)} %unpack.9.refs_3_.refs_2_), channel_id=1, source_target_pairs={{0,16},{16,0},{1,17},{17,1},{2,18},{18,2},{3,19},{19,3},{4,20},{20... | collective-permute-start | bytes 786440 | tf_op jit(solution)/shard_map/cond/branch_0_fun/ppermute | solution.py:474
  111.5 12.0 %collective-permute-start.43 = (bf16[16,32,256]{2,1,0:T(8,128)(2,1)S(1)}, bf16[16,32,256]{2,1,0:T(8,128)(2,1)S(1)}, u32[]{:S(2)}, u32[]{:S(2)}) collective-permute-start(bf16[16,32,256]{2,1,0:T(8,128)(2,1)S(1)} %unpack.11.refs_0_.refs_2_.refs_1_), channel_id=1, source_target_pairs={{0,16},{16,0},{1,17},{17,1},{2,18},{18,2},{3,19},{19,3},{4,20},{20... | collective-permute-start | bytes 786440 | tf_op jit(solution)/shard_map/cond/branch_0_fun/ppermute | solution.py:474
  113.0 8.6 %collective-permute-start.41 = (f32[64,512]{1,0:T(8,128)S(1)}, f32[64,512]{1,0:T(8,128)S(1)}, u32[]{:S(2)}, u32[]{:S(2)}) collective-permute-start(f32[64,512]{1,0:T(8,128)S(1)} %add.77.refs_1_), channel_id=1, source_target_pairs={{0,8},{1,9},{2,10},{3,11},{4,12},{5,13},{6,14},{7,15},{8,0},{9,1},... | collective-permute-start | bytes 393224 | tf_op jit(solution)/shard_map/cond/branch_0_fun/ppermute | solution.py:432
  (6 other events, 78.3 us)
